TPU v7x, 32 devices: a whole 2x2x4 slice. The times are simulated.
32 devices in a mesh: gx: 4 (over z), gy: 4 (over y, x), gz: 2 (over core).
Axes of the slice: x: 2, y: 2, z: 4, core: 2. Of those that a mesh axis runs over, the one named last changes fastest.
Arguments:
- density: float32 [128, 64, 256], P('gx', 'gy', 'gz'), may hold values from 0.5 to 2
- momentum: float32 [2, 128, 64, 256], P(None, 'gx', 'gy', 'gz'), may hold values from -3 to 3
- lower_face: float32 [128], P('gx'), may hold values from 2048 to 8192
Outputs:
- updated: float32 [3, 128, 64, 256], P(None, 'gx', 'gy', 'gz')
All inputs are finite; a program needn't handle non-finite values.
Results may differ from a plain program's by a relative error of at most 0.0003.
Values sent between devices are 32-bit elements; how exact they have to be, the bound alone decides.
No kernel may reach another device: no remote copies, remote signals or barrier semaphores. Data moves between devices by JAX's collectives and lax.ppermute only.
A program may use at most 64 MiB of HBM per device.

v0:
```python
import jax
import jax.numpy as jnp
from jax import lax
from jax.sharding import PartitionSpec as P

time_step = 0.2


def with_halo(block, sides, width):
    for axis, dim in sides:
        count = lax.axis_size(axis)
        forward = [(i, i + 1) for i in range(count - 1)]
        forward.append((count - 1, 0))
        backward = [(target, source) for source, target in forward]
        low = lax.ppermute(
            lax.slice_in_dim(block, block.shape[dim] - width, None, axis=dim), axis, forward
        )
        high = lax.ppermute(lax.slice_in_dim(block, 0, width, axis=dim), axis, backward)
        block = jnp.concatenate([low, block, high], axis=dim)
    return block


def passed_along(value, axis, steps):
    count = lax.axis_size(axis)
    first, last = (max(0, -steps), min(count, count - steps))
    return lax.ppermute(value, axis, [(source, source + steps) for source in range(first, last)])


def central_sixth(padded, axis, count):

    def take(offset):
        return lax.slice_in_dim(padded, 3 + offset, 3 + offset + count, axis=axis)

    return (45.0 * (take(1) - take(-1)) - 9.0 * (take(2) - take(-2)) + (take(3) - take(-3))) / 60.0


def mat_mat(left, right):
    return jnp.einsum("nij,njk->nik", left, right, precision=lax.Precision.HIGHEST)


def mat_vec(left, vec):
    return jnp.einsum("nij,njab->niab", left, vec, precision=lax.Precision.HIGHEST)


def invert_pair(mat):
    det = mat[:, 0, 0] * mat[:, 1, 1] - mat[:, 0, 1] * mat[:, 1, 0]
    first = jnp.stack([mat[:, 1, 1], -mat[:, 0, 1]], -1)
    second = jnp.stack([-mat[:, 1, 0], mat[:, 0, 0]], -1)
    return jnp.stack([first, second], 1) / det[:, None, None]


def eliminate(current, lower_eq, upper_eq):
    rows, coup_lo, coup_hi = current
    eye_pair = jnp.eye(2, dtype=jnp.float32)[None]
    pivot = eye_pair - mat_mat(coup_lo, lower_eq[2]) - mat_mat(coup_hi, upper_eq[1])
    pivot_inv = invert_pair(pivot)
    new_rows = mat_vec(
        pivot_inv, rows + mat_vec(coup_lo, lower_eq[0]) + mat_vec(coup_hi, upper_eq[0])
    )
    new_lo = mat_mat(pivot_inv, mat_mat(coup_lo, lower_eq[1]))
    new_hi = mat_mat(pivot_inv, mat_mat(coup_hi, upper_eq[2]))
    return (new_rows, new_lo, new_hi)


def push_down(stacked, span):
    return jnp.concatenate([jnp.zeros_like(stacked[:span]), stacked[:-span]], 0)


def push_up(stacked, span):
    return jnp.concatenate([stacked[span:], jnp.zeros_like(stacked[:span])], 0)


def on_device(density, momentum, lower_face):
    state = jnp.concatenate([density[None], momentum], 0)
    cells = state.shape[1]
    count_y = state.shape[2]
    count_z = state.shape[3]
    padded = with_halo(state, (("gy", 2), ("gz", 3)), 3)
    y_band = padded[:, :, :, 3 : 3 + count_z]
    z_band = padded[:, :, 3 : 3 + count_y, :]
    flux_y = y_band * (y_band[1] / y_band[0])[None]
    flux_z = z_band * (z_band[2] / z_band[0])[None]
    rhs = state - time_step * (
        central_sixth(flux_y, 2, count_y) + central_sixth(flux_z, 3, count_z)
    )
    position = lax.axis_index("gx")
    devices = lax.axis_size("gx")
    after = passed_along(lower_face[:1], "gx", -1)
    upper_last = jnp.where(position == devices - 1, lower_face[-1], after[0])
    upper = jnp.concatenate([lower_face[1:], upper_last[None]])
    diagonal = 1.0 + lower_face + upper
    block = jnp.diag(diagonal) - jnp.diag(lower_face[1:], -1) - jnp.diag(lower_face[1:], 1)
    factor = jnp.linalg.cholesky(block)
    inverse = jax.scipy.linalg.cho_solve((factor, True), jnp.eye(cells, dtype=jnp.float32))
    local = jnp.einsum("ij,kjab->kiab", inverse, rhs, precision=lax.Precision.HIGHEST)
    coup_left = lower_face[0]
    zero = jnp.zeros((), jnp.float32)
    first_a = coup_left * inverse[0, 0]
    first_b = upper_last * inverse[0, -1]
    last_a = coup_left * inverse[-1, 0]
    last_b = upper_last * inverse[-1, -1]
    coup_lo = jnp.stack([jnp.stack([zero, first_a]), jnp.stack([zero, last_a])])[None]
    coup_hi = jnp.stack([jnp.stack([first_b, zero]), jnp.stack([last_b, zero])])[None]
    rows = jnp.stack([local[:, 0], local[:, -1]], 0).reshape(1, 2, 3 * count_y, count_z)
    levels = (devices - 1).bit_length()
    current = (
        lax.all_gather(rows, "gx", axis=0, tiled=True),
        lax.all_gather(coup_lo, "gx", axis=0, tiled=True),
        lax.all_gather(coup_hi, "gx", axis=0, tiled=True),
    )
    for level in range(levels):
        span = 1 << level
        lower_eq = tuple((push_down(item, span) for item in current))
        upper_eq = tuple((push_up(item, span) for item in current))
        current = eliminate(current, lower_eq, upper_eq)
    solved = current[0]
    extended = jnp.concatenate([jnp.zeros_like(solved[:1]), solved, jnp.zeros_like(solved[:1])], 0)
    last_below = lax.dynamic_index_in_dim(extended, position, 0, False)[1]
    first_above = lax.dynamic_index_in_dim(extended, position + 2, 0, False)[0]
    col_low = coup_left * inverse[:, 0]
    col_high = upper_last * inverse[:, -1]
    below_vals = last_below.reshape(3, 1, count_y, count_z)
    above_vals = first_above.reshape(3, 1, count_y, count_z)
    return (
        local
        + col_low[None, :, None, None] * below_vals
        + col_high[None, :, None, None] * above_vals
    )


def solution(mesh):
    placed = (P("gx", "gy", "gz"), P(None, "gx", "gy", "gz"), P("gx"))
    return jax.shard_map(
        on_device, mesh=mesh, in_specs=placed, out_specs=P(None, "gx", "gy", "gz"), check_vma=False
    )
```

profile of v0, /device:TPU:0, one launch (start us, length us, event | category | flops | bytes accessed | tf_op | source)
XLA Modules:
  0.0 81.3 jit_solution(5060148734911130925)
XLA Ops:
  0.0 1.2 %fusion.14 = (f32[3,32,3,128]{3,2,1,0:T(4,128)S(1)}, f32[3,32,3,128]{3,2,1,0:T(4,128)S(1)}) fusion(f32[2,32,16,128]{3,2,1,0:T(8,128)} %param.4, f32[1,32,16,128]{3,2,1,0:T(8,128)} %bitcast.104), kind=kLoop, calls=%fused_computation.42 | loop fusion | flops 73728 | bytes 1081344 | tf_op jit(solution)/shard_map/concatenate | solution.py:74
  1.2 3.0 %collective-permute-start = (f32[3,32,3,128]{3,1,2,0:T(8,128)S(1)}, f32[3,32,3,128]{3,1,2,0:T(8,128)S(1)}, u32[]{:S(2)}, u32[]{:S(2)}) collective-permute-start(f32[3,32,3,128]{3,1,2,0:T(8,128)S(1)} %copy.101), channel_id=1, source_target_pairs={{0,2},{2,4},{4,6},{6,0},{1,3},{3,5},{5,7},{7,1},{8,10},{10,12},{12... | collective-permute-start | bytes 442376 | tf_op jit(solution)/shard_map/ppermute | solution.py:15
  4.2 1.0 %collective-permute-start.1 = (f32[3,32,3,128]{3,1,2,0:T(8,128)S(1)}, f32[3,32,3,128]{3,1,2,0:T(8,128)S(1)}, u32[]{:S(2)}, u32[]{:S(2)}) collective-permute-start(f32[3,32,3,128]{3,1,2,0:T(8,128)S(1)} %copy.102), channel_id=1, source_target_pairs={{2,0},{4,2},{6,4},{0,6},{3,1},{5,3},{7,5},{1,7},{10,8},{12,10},{14... | collective-permute-start | bytes 442376 | tf_op jit(solution)/shard_map/ppermute | solution.py:18
  5.3 0.6 fusion.62
  5.8 1.3 %collective-permute-start.4 = (f32[1]{0:T(128)}, f32[1]{0:T(128)}, u32[]{:S(2)}, u32[]{:S(2)}) collective-permute-start(f32[1]{0:T(128)} %get-tuple-element.40), channel_id=1, source_target_pairs={{8,0},{16,8},{24,16},{9,1},{17,9},{25,17},{10,2},{18,10},{26,18},{... | collective-permute-start | bytes 20 | tf_op jit(solution)/shard_map/ppermute | solution.py:26
  7.2 4.3 %collective-permute-done.4 = f32[1]{0:T(128)} collective-permute-done((f32[1]{0:T(128)}, f32[1]{0:T(128)}, u32[]{:S(2)}, u32[]{:S(2)}) %collective-permute-start.4) | collective-permute-done | bytes 36 | tf_op jit(solution)/shard_map/ppermute | solution.py:26
  12.9 2.9 %cholesky.17 = f32[32,32]{1,0:T(8,128)S(1)} custom-call(f32[32,32]{1,0:T(8,128)S(1)} %add_multiply_fusion), custom_call_target="Cholesky" | custom-call | tf_op jit(solution)/shard_map/jit(cholesky)/cholesky | solution.py:93
  15.8 0.6 compare_reduce_fusion
  16.5 0.6 fusion.20
  17.1 2.4 %custom-call.10 = f32[1,32,32]{1,2,0:T(8,128)S(1)} custom-call(f32[1,32,32]{2,1,0:T(8,128)S(1)} %fusion.20), custom_call_target="InvertDiagBlocksLowerTriangular" | custom-call | tf_op jit(solution)/shard_map/jit(_cho_solve)/triangular_solve | solution.py:94
  20.0 0.7 fusion.59
  24.7 9.7 %all-gather.2 = f32[4,2,2]{2,1,0:T(2,128)S(1)} all-gather(f32[1,2,2]{2,1,0:T(2,128)S(1)} %maximum_bitcast_fusion), channel_id=2, replica_groups=mesh['gx'=4,'gy'=4,'gz'=2] {'gx'}, dimensions={0}, use_global_device_ids=true | all-gather | bytes 80 | tf_op jit(solution)/shard_map/all_gather | solution.py:108
  34.4 8.1 %all-gather.3 = f32[4,2,2]{2,1,0:T(2,128)S(1)} all-gather(f32[1,2,2]{2,1,0:T(2,128)S(1)} %maximum_bitcast_fusion.1), channel_id=3, replica_groups=mesh['gx'=4,'gy'=4,'gz'=2] {'gx'}, dimensions={0}, use_global_device_ids=true | all-gather | bytes 80 | tf_op jit(solution)/shard_map/all_gather | solution.py:109
  44.5 0.7 copy.95
  45.2 1.2 %fusion.44 = (f32[32]{0:T(128)}, f32[32]{0:T(128)}) fusion(f32[32,32]{0,1:T(8,128)S(1)} %fusion.22, f32[]{:T(128)} %bitcast.10, f32[]{:T(128)} %select_n.37), kind=kLoop, calls=%fused_computation.109 | loop fusion | flops 64 | bytes 520 | tf_op jit(solution)/shard_map/mul | solution.py:120
  47.3 0.8 fusion.13
  48.1 1.1 %copy.75 = f32[3,32,22,3]{1,2,3,0:T(8,128)} copy(f32[3,32,22,3]{3,2,1,0:T(8,128)S(1)} %get-tuple-element.15) | data formatting | bytes 50688 | tf_op jit(solution)/shard_map/slice | solution.py:16
  49.2 1.1 %copy.76 = f32[3,32,22,3]{1,2,3,0:T(8,128)} copy(f32[3,32,22,3]{3,2,1,0:T(8,128)S(1)} %get-tuple-element.16) | data formatting | bytes 50688 | tf_op jit(solution)/shard_map/slice | solution.py:18
  51.1 1.4 %copy.77 = f32[3,32,22,3]{3,2,1,0:T(8,128)S(1)} copy(f32[3,32,22,3]{1,2,3,0:T(8,128)} %collective-permute-done.2) | data formatting | bytes 50688 | tf_op jit(solution)/shard_map/ppermute | solution.py:15
  52.5 2.4 %copy.78 = f32[3,32,22,3]{3,2,1,0:T(8,128)} copy(f32[3,32,22,3]{1,2,3,0:T(8,128)} %collective-permute-done.3) | data formatting | bytes 50688 | tf_op jit(solution)/shard_map/ppermute | solution.py:18
  54.9 1.8 %fusion.12 = f32[32,16,134]{2,1,0:T(8,128)S(1)} fusion(f32[3,32,22,3]{3,2,1,0:T(8,128)} %copy.78, f32[3,32,22,3]{3,2,1,0:T(8,128)S(1)} %copy.77, f32[3,32,3,128]{3,2,1,0:T(4,128)S(1)} %copy.74, f32[3,32,3,128]{3,2,1,0:T(4,128)S(1)} %copy.73, f32[2,32,16,128]{3,2,1,0:T(8,128)S(1)} %copy-done, f32[1,32,16,128]{3,2,1,0:T(8,128)S(1)} %bitcast.107), kind=kLoop, calls=%fused_computation.38 | loop fusion | flops 754688 | bytes 1406464 | tf_op jit(solution)/shard_map/mul | solution.py:82
  56.8 1.4 %pad_maximum_fusion = f32[3,32,22,134]{3,2,1,0:T(8,128)S(1)} fusion(f32[3,32,22,3]{3,2,1,0:T(8,128)S(1)} %copy-done.1, f32[3,32,3,128]{3,2,1,0:T(4,128)S(1)} %copy.74, f32[2,32,16,128]{3,2,1,0:T(8,128)S(1)} %copy-done, f32[1,32,16,128]{3,2,1,0:T(8,128)S(1)} %bitcast.108, f32[3,32,3,128]{3,2,1,0:T(4,128)S(1)} %copy.73, f32[3,32,22,3]{3,2,1,0:T(8,128)S(1)} %copy.77), kind=kLoop, calls=%fused_computation | loop fusion | flops 1415040 | bytes 2264064 | tf_op jit(solution)/shard_map/concatenate | solution.py:19
  58.5 1.1 %fusion = f32[3,32,16,128]{3,2,1,0:T(8,128)S(1)} fusion(f32[2,32,16,128]{3,2,1,0:T(8,128)S(1)} %copy-done, f32[1,32,16,128]{3,2,1,0:T(8,128)S(1)} %bitcast.109, f32[3,32,16,134]{3,2,1,0:T(8,128)S(1)} %slice_multiply_fusion, f32[3,32,22,128]{3,2,1,0:T(8,128)S(1)} %broadcast_multiply_fusion), kind=kLoop, calls=%fused_computation.17 | loop fusion | flops 3538944 | bytes 11010048 | tf_op jit(solution)/shard_map/sub | solution.py:83
  59.6 1.0 %convolution_bitcast_fusion = f32[3,32,16,128]{3,1,2,0:T(8,128)S(1)} fusion(f32[3,32,16,128]{3,2,1,0:T(8,128)S(1)} %fusion, f32[32,32]{0,1:T(8,128)S(1)} %copy-done.5), kind=kOutput, calls=%fused_computation.2 | convolution fusion | flops 75497472 | bytes 1576960 | tf_op jit(solution)/shard_map/ij,kjab->kiab/dot_general | solution.py:95
  60.8 13.7 %all_gather.11 = f32[4,2,48,128]{3,2,1,0:T(8,128)S(1)} all-gather(f32[1,2,48,128]{3,2,1,0:T(8,128)S(1)} %pad_maximum_fusion.4), channel_id=1, replica_groups=mesh['gx'=4,'gy'=4,'gz'=2] {'gx'}, dimensions={0}, use_global_device_ids=true | all-gather | bytes 245760 | tf_op jit(solution)/shard_map/all_gather | solution.py:107
  74.6 0.8 convolution_add_fusion.3
  75.5 0.8 convolution_add_fusion.2
  76.3 0.8 fusion.65
  77.1 0.8 convolution_add_fusion.1
  77.9 0.8 convolution_add_fusion
  78.7 0.8 fusion.66
  79.9 1.3 %copy.88 = f32[3,32,16,128]{3,2,1,0:T(8,128)} copy(f32[3,32,16,128]{3,1,2,0:T(8,128)S(1)} %multiply_add_fusion) | data formatting | bytes 1572864 | tf_op jit(solution)/shard_map/add | solution.py:125
  (85 shorter events, 5.5 us)
Async XLA Ops:
  0.0 5.3 %copy-start.9 = (f32[32]{0:T(128)S(1)}, f32[32]{0:T(128)}, u32[]{:S(2)}) copy-start(f32[32]{0:T(128)} %param.5) | copy-start | bytes 388
  1.2 45.5 %copy-start = (f32[2,32,16,128]{3,2,1,0:T(8,128)S(1)}, f32[2,32,16,128]{3,2,1,0:T(8,128)}, u32[]{:S(2)}) copy-start(f32[2,32,16,128]{3,2,1,0:T(8,128)} %param.4) | copy-start | bytes 1572868
  1.2 45.5 %copy-start.2 = (f32[32,16,128]{2,1,0:T(8,128)S(1)}, f32[32,16,128]{2,1,0:T(8,128)}, u32[]{:S(2)}) copy-start(f32[32,16,128]{2,1,0:T(8,128)} %param.3) | copy-start | bytes 786436
  1.2 45.2 %collective-permute-start = (f32[3,32,3,128]{3,1,2,0:T(8,128)S(1)}, f32[3,32,3,128]{3,1,2,0:T(8,128)S(1)}, u32[]{:S(2)}, u32[]{:S(2)}) collective-permute-start(f32[3,32,3,128]{3,1,2,0:T(8,128)S(1)} %copy.101), channel_id=1, source_target_pairs={{0,2},{2,4},{4,6},{6,0},{1,3},{3,5},{5,7},{7,1},{8,10},{10,12},{12... | collective-permute-start | bytes 442376 | tf_op jit(solution)/shard_map/ppermute | solution.py:15
  4.2 42.3 %collective-permute-start.1 = (f32[3,32,3,128]{3,1,2,0:T(8,128)S(1)}, f32[3,32,3,128]{3,1,2,0:T(8,128)S(1)}, u32[]{:S(2)}, u32[]{:S(2)}) collective-permute-start(f32[3,32,3,128]{3,1,2,0:T(8,128)S(1)} %copy.102), channel_id=1, source_target_pairs={{2,0},{4,2},{6,4},{0,6},{3,1},{5,3},{7,5},{1,7},{10,8},{12,10},{14... | collective-permute-start | bytes 442376 | tf_op jit(solution)/shard_map/ppermute | solution.py:18
  5.8 5.7 %collective-permute-start.4 = (f32[1]{0:T(128)}, f32[1]{0:T(128)}, u32[]{:S(2)}, u32[]{:S(2)}) collective-permute-start(f32[1]{0:T(128)} %get-tuple-element.40), channel_id=1, source_target_pairs={{8,0},{16,8},{24,16},{9,1},{17,9},{25,17},{10,2},{18,10},{26,18},{... | collective-permute-start | bytes 20 | tf_op jit(solution)/shard_map/ppermute | solution.py:26
  19.9 26.5 %copy-start.4 = (f32[32,32]{0,1:T(8,128)}, f32[32,32]{0,1:T(8,128)S(1)}, u32[]{:S(2)}) copy-start(f32[32,32]{0,1:T(8,128)S(1)} %fusion.22) | copy-start | bytes 12292
  43.9 2.5 %copy-start.7 = (f32[4,2,2]{2,1,0:T(2,128)}, f32[4,2,2]{2,1,0:T(2,128)S(1)}, u32[]{:S(2)}) copy-start(f32[4,2,2]{2,1,0:T(2,128)S(1)} %fusion.64) | copy-start | bytes 196
  49.2 1.7 %copy-start.3 = (f32[32,22,128]{2,1,0:T(8,128)S(1)}, f32[32,22,128]{2,1,0:T(8,128)}, u32[]{:S(2)}) copy-start(f32[32,22,128]{2,1,0:T(8,128)} %fusion.13) | copy-start | bytes 1081348
  49.2 1.9 %collective-permute-start.2 = (f32[3,32,22,3]{1,2,3,0:T(8,128)}, f32[3,32,22,3]{1,2,3,0:T(8,128)}, u32[]{:S(2)}, u32[]{:S(2)}) collective-permute-start(f32[3,32,22,3]{1,2,3,0:T(8,128)} %copy.75), channel_id=1, source_target_pairs={{0,1},{1,0},{2,3},{3,2},{4,5},{5,4},{6,7},{7,6},{8,9},{9,8},{10,11... | collective-permute-start | bytes 76040 | tf_op jit(solution)/shard_map/ppermute | solution.py:15
  50.4 2.1 %collective-permute-start.3 = (f32[3,32,22,3]{1,2,3,0:T(8,128)}, f32[3,32,22,3]{1,2,3,0:T(8,128)}, u32[]{:S(2)}, u32[]{:S(2)}) collective-permute-start(f32[3,32,22,3]{1,2,3,0:T(8,128)} %copy.76), channel_id=1, source_target_pairs={{1,0},{0,1},{3,2},{2,3},{5,4},{4,5},{7,6},{6,7},{9,8},{8,9},{11,10... | collective-permute-start | bytes 76040 | tf_op jit(solution)/shard_map/ppermute | solution.py:18
  54.9 1.8 %copy-start.1 = (f32[3,32,22,3]{3,2,1,0:T(8,128)S(1)}, f32[3,32,22,3]{3,2,1,0:T(8,128)}, u32[]{:S(2)}) copy-start(f32[3,32,22,3]{3,2,1,0:T(8,128)} %copy.78) | copy-start | bytes 76036
  58.5 1.1 %copy-start.5 = (f32[32,32]{0,1:T(8,128)S(1)}, f32[32,32]{0,1:T(8,128)}, u32[]{:S(2)}) copy-start(f32[32,32]{0,1:T(8,128)} %copy-done.4) | copy-start | bytes 12292
  75.4 2.5 %copy-start.8 = (f32[4,2,2]{2,1,0:T(2,128)S(1)}, f32[4,2,2]{2,1,0:T(2,128)}, u32[]{:S(2)}) copy-start(f32[4,2,2]{2,1,0:T(2,128)} %copy-done.7) | copy-start | bytes 196
  75.5 3.2 %copy-start.6 = (f32[4,2,2,1]{2,1,3,0:T(2,128)S(1)}, f32[4,2,2,1]{2,1,3,0:T(2,128)}, u32[]{:S(2)}) copy-start(f32[4,2,2,1]{2,1,3,0:T(2,128)} %copy.95) | copy-start | bytes 196
  77.1 2.6 %copy-start.10 = (f32[32]{0:T(128)S(1)}, f32[32]{0:T(128)}, u32[]{:S(2)}) copy-start(f32[32]{0:T(128)} %get-tuple-element.27) | copy-start | bytes 388
  77.1 2.6 %copy-start.11 = (f32[32]{0:T(128)S(1)}, f32[32]{0:T(128)}, u32[]{:S(2)}) copy-start(f32[32]{0:T(128)} %get-tuple-element.28) | copy-start | bytes 388
where the time goes:
time: 81.6 us; the launch traced here: 81.3 us
  blocking collectives  31.6 us (39%)
  other arithmetic  16.1 us (20%)
  local copies, waits for them, and re-layouts  10.6 us (13%)
  matrix products  7.43 us (9%)
  starting transfers between devices  5.81 us (7%)
  between operations  5.44 us (7%)
  waiting for transfers between devices  4.32 us (5%)
    all_gather x1, blocking collectives, on_device(): lax.all_gather(rows, 'gx', axis=0, tiled=True)  13.7 us
    all_gather x1, blocking collectives, on_device(): lax.all_gather(coup_lo, 'gx', axis=0, tiled=True)  9.7 us
    all_gather x1, blocking collectives, on_device(): lax.all_gather(coup_hi, 'gx', axis=0, tiled=True)  8.11 us
    dot_general x6, matrix products, mat_vec(): jnp.einsum('nij,njab->niab', left, vec, precision=lax.Precision.HIGHEST)  4.65 us
    ppermute x1, waiting for transfers between devices, passed_along(): lax.ppermute(value, axis, [(source, source + steps) for source in range(f...  4.31 us
    another operation x3, other arithmetic, on_device(): factor = jnp.linalg.cholesky(block)  3.59 us
    another operation x2, other arithmetic, on_device(): jax.scipy.linalg.cho_solve((factor, True), jnp.eye(cells, dtype=jnp.float...  3 us
    ppermute x2, starting transfers between devices, with_halo(): lax.ppermute(lax.slice_in_dim(block, block.shape[dim] - width, None, axis...  2.99 us
  transfers between devices with their start and end apart: 5, of which 1 were waited for; matrix products, arithmetic and copies ran while one was open for 19% of the time, Pallas kernels for 0%

commit v1 on v0

v1 whole, which is shorter than its diff:
```python
import functools

import jax
import jax.numpy as jnp
from jax import lax
from jax.experimental import pallas as pl
from jax.experimental.pallas import tpu as pltpu
from jax.sharding import PartitionSpec as P

time_step = 0.2
scale = time_step / 60.0
ROWS = 8
F32 = jnp.float32
VMEM = pl.BlockSpec(memory_space=pltpu.VMEM)
SMEM = pl.BlockSpec(memory_space=pltpu.SMEM)
ANY = pl.BlockSpec(memory_space=pl.ANY)


def pairing(count, odd):
    pairs = []
    for low in range(1 if odd else 0, count, 2):
        high = (low + 1) % count
        pairs += [(low, high), (high, low)]
    return pairs


def partner_by(count, step):
    return [(i, i ^ step) for i in range(count)]


def rows_of(block):
    return block.reshape(block.shape[0] * block.shape[1], block.shape[2])


def shifted_z(own, low, high, k):
    nz = own.shape[-1]
    if nz % 128 == 0:
        lane = lax.broadcasted_iota(jnp.int32, own.shape, own.ndim - 1)
        if k > 0:
            return pltpu.roll(jnp.where(lane < k, high, own), nz - k, own.ndim - 1)
        return pltpu.roll(jnp.where(lane >= nz + k, low, own), -k, own.ndim - 1)
    if k > 0:
        return jnp.concatenate([own[..., k:], high[..., :k]], -1)
    return jnp.concatenate([low[..., nz + k :], own[..., : nz + k]], -1)


def sixth(take):
    return 45.0 * (take(1) - take(-1)) - 9.0 * (take(2) - take(-2)) + (take(3) - take(-3))


def sixth_z(own, low, high):
    return sixth(lambda k: shifted_z(own, low, high, k))


def join(left, right):
    inv_delta = 1.0 / (right[5] + right[2] + left[3])
    jump = (right[0] - left[1]) * inv_delta
    from_in = left[4] * inv_delta
    from_out = right[4] * inv_delta
    group = (
        left[0] + left[4] * jump,
        right[1] - right[4] * jump,
        left[2] - left[4] * from_in,
        right[3] - right[4] * from_out,
        left[4] * from_out,
        left[5],
        right[6],
    )
    return group, (jump, from_in, from_out)


def pick(cond, yes, no):
    return tuple(jnp.where(cond, a, b) for a, b in zip(yes, no))


def join_own(is_left, own, other, forms):
    left = pick(is_left, own, other)
    right = pick(is_left, other, own)
    group, (jump, from_in, from_out) = join(left, right)
    new = []
    for c0, c1, c2 in forms:
        through = jnp.where(is_left, c2, c1)
        new.append(
            (
                c0 + through * jump,
                jnp.where(is_left, c1, 0.0) + through * from_in,
                jnp.where(is_left, 0.0, c2) + through * from_out,
            )
        )
    return group, new


def closing(is_left, group, forms):
    first, last, alpha, beta, m, inv_first, inv_last = group
    kappa = 1.0 / jnp.where(is_left, inv_first + alpha, inv_last + beta)
    outer = jnp.where(is_left, first, -last) * kappa
    gain = kappa * m
    facing = jnp.where(is_left, last - m * outer, first + m * outer)
    resist = jnp.where(is_left, beta, alpha + inv_first) - m * gain
    out = []
    for c0, c1, c2 in forms:
        far = jnp.where(is_left, c1, c2)
        near = jnp.where(is_left, c2, c1)
        out.append((c0 + far * outer, far * gain + near))
    return facing, resist, out


def put_scalars(ref, block, values):
    for row, value in enumerate(values):
        ref[block, row : row + 1] = value


def get_scalars(ref, block, count):
    return [ref[block, row : row + 1] for row in range(count)]


def store_group(ref, group, tiles):
    for f in range(3):
        ref[f * tiles : (f + 1) * tiles] = group[0][f]
        ref[(3 + f) * tiles : (4 + f) * tiles] = group[1][f]
    put_scalars(ref, 6 * tiles, group[2:])


def load_group(ref, tiles):
    shape = (3, tiles) + ref.shape[1:]
    first = ref[: 3 * tiles].reshape(shape)
    last = ref[3 * tiles : 6 * tiles].reshape(shape)
    return (first, last, *get_scalars(ref, 6 * tiles, 5))


def store_closing(msg_ref, own_ref, facing, resist, out, tiles):
    for f in range(3):
        msg_ref[f * tiles : (f + 1) * tiles] = facing[f]
        own_ref[f * tiles : (f + 1) * tiles] = out[0][0][f]
        own_ref[(3 + f) * tiles : (4 + f) * tiles] = out[1][0][f]
    put_scalars(msg_ref, 3 * tiles, [resist])
    put_scalars(own_ref, 6 * tiles, [out[0][1], out[1][1]])


def store_forms(ref, forms, tiles):
    for f in range(3):
        ref[f * tiles : (f + 1) * tiles] = forms[0][0][f]
        ref[(3 + f) * tiles : (4 + f) * tiles] = forms[1][0][f]
    put_scalars(ref, 6 * tiles, [*forms[0][1:], *forms[1][1:]])


def load_forms(ref, tiles):
    shape = (3, tiles) + ref.shape[1:]
    scalars = get_scalars(ref, 6 * tiles, 4)
    return [
        (ref[: 3 * tiles].reshape(shape), scalars[0], scalars[1]),
        (ref[3 * tiles : 6 * tiles].reshape(shape), scalars[2], scalars[3]),
    ]


def first_kernel(
    faces, density, momentum,
    flux_y, flux_z, sums, small_a, small_b, edge_a, edge_b, coefs, scalars,
    rho_v, mom_v, sems,
):
    nx, tiles, _, nz = density.shape
    ny = tiles * ROWS
    copies = [
        pltpu.make_async_copy(density, rho_v, sems.at[0]),
        pltpu.make_async_copy(momentum, mom_v, sems.at[1]),
    ]
    for copy in copies:
        copy.start()
    tile = (ROWS, nz)
    inv = [1.0 / jnp.full(tile, faces[i], F32) for i in range(nx)]
    phi = [jnp.ones(tile, F32)]
    flux = phi[0]
    for i in range(1, nx):
        phi.append(phi[-1] + flux * inv[i])
        flux = flux + phi[-1]
    m = 1.0 / flux
    psi = [jnp.ones(tile, F32)]
    flux = psi[0]
    for i in range(nx - 1, 0, -1):
        psi.append(psi[-1] + flux * inv[i])
        flux = flux + psi[-1]
    psi = psi[::-1]
    for i in range(nx):
        coefs[i] = phi[i]
        coefs[nx + i] = psi[i] * m
    scalars[0:1] = (psi[0] * m)[0:1]
    scalars[1:2] = (phi[nx - 1] * m)[0:1]
    scalars[2:3] = m[0:1]
    scalars[3:4] = inv[0][0:1]
    scalars[4:5] = inv[nx - 1][0:1]
    scalars[5:8] = jnp.zeros((3, nz), F32)
    for copy in copies:
        copy.wait()
    total = [[None] * 9, [None] * 9]
    for x in range(nx):
        rho, m0, m1 = rho_v[x], mom_v[0, x], mom_v[1, x]
        inv_rho = 1.0 / rho
        v0, v1 = m0 * inv_rho, m1 * inv_rho
        cross = m0 * v1
        values = (rho, m0, m1, m0, m0 * v0, cross, m1, cross, m1 * v1)
        for f in range(3):
            flux_y[f, x] = values[3 + f]
            flux_z[f, x] = values[6 + f]
        for side, weight in enumerate((coefs[nx + x], coefs[x])):
            for k, value in enumerate(values):
                term = value * weight
                total[side][k] = term if x == 0 else total[side][k] + term
    for side in range(2):
        for f in range(3):
            at = (3 * side + f) * tiles
            sums[at : at + tiles] = total[side][f]
            sums[6 * tiles + at : 6 * tiles + at + tiles] = total[side][3 + f]
            flux_z[3, (3 * side + f)] = total[side][6 + f]
    odd = lax.rem(lax.axis_index("gy"), 2)
    for ref_small, ref_edge, high in ((small_a, edge_a, 1 - odd), (small_b, edge_b, odd)):
        for k in range(6):
            at = (6 + k) * tiles + high * (tiles - 1)
            ref_small[k] = sums[pl.ds(at, 1)][0]
        start = high * (ny - 3)
        for f in range(3):
            for x in range(nx):
                for k in range(3):
                    ref_edge[3 * f + k, x : x + 1] = flux_y.at[f, x].reshape(ny, nz)[pl.ds(start + k, 1)]


def halos_y(is_odd, from_a, from_b):
    low = jnp.where(is_odd, from_a, from_b)
    high = jnp.where(is_odd, from_b, from_a)
    return low, high


def second_kernel(
    stages, nx, sums, scalars, zsum, zsum_low, zsum_high, small_a, small_b, msg, own, pad
):
    nblocks, _, nz = sums.shape
    tiles = nblocks // 12
    ny = tiles * ROWS
    is_odd = lax.rem(lax.axis_index("gy"), 2) == 1
    low, high = halos_y(is_odd, small_a[...], small_b[...])
    alpha, beta, m, inv_first, inv_last = [scalars[i : i + 1] for i in range(5)]
    values = []
    for k in range(6):
        pad[k, 0:ROWS] = low[k]
        pad[k, ROWS : ROWS + ny] = sums[(6 + k) * tiles : (7 + k) * tiles].reshape(ny, nz)
        pad[k, ROWS + ny : 2 * ROWS + ny] = high[k]
        dy = sixth(lambda s: pad[k, ROWS + s : ROWS + s + ny])
        zs = [r[k].reshape(ny, nz) for r in (zsum, zsum_low, zsum_high)]
        dz = sixth_z(*zs)
        state = sums[k * tiles : (k + 1) * tiles].reshape(ny, nz)
        values.append((state - scale * (dy + dz)).reshape(tiles, ROWS, nz))
    first = jnp.stack(values[:3])
    last = jnp.stack(values[3:]) * m
    group = (first, last, alpha, beta, m, inv_first, inv_last)
    forms = [(0.0, 1.0, 0.0), (0.0, 0.0, 1.0)]
    if stages == 1:
        is_left = lax.rem(lax.axis_index("gx"), 2) == 0
        zero = jnp.zeros_like(first)
        one = jnp.ones_like(alpha)
        forms = [(zero, one, 0.0 * one), (zero, 0.0 * one, one)]
        facing, resist, out = closing(is_left, group, forms)
        store_closing(msg, own, facing, resist, out, tiles)
    else:
        store_group(msg, group, tiles)


def join_kernel(stage, stages, tiles, *refs):
    if stage == 0:
        mine, other, msg, own = refs
        shape = (3, tiles) + mine.shape[1:]
        zero, one = jnp.zeros(shape, F32), jnp.ones((1, shape[-1]), F32)
        forms = [(zero, one, 0.0 * one), (zero, 0.0 * one, one)]
    else:
        mine, other, forms_ref, msg, own = refs
        forms = load_forms(forms_ref, tiles)
    at = lax.axis_index("gx")
    is_left = lax.rem(lax.div(at, 1 << stage), 2) == 0
    group, forms = join_own(is_left, load_group(mine, tiles), load_group(other, tiles), forms)
    if stage + 2 == stages:
        is_left = lax.rem(lax.div(at, 2 << stage), 2) == 0
        facing, resist, out = closing(is_left, group, forms)
        store_closing(msg, own, facing, resist, out, tiles)
    else:
        store_group(msg, group, tiles)
        store_forms(own, forms, tiles)


def last_kernel(
    stages, density, momentum, flux_y, flux_z, flux_z_low, flux_z_high, edge_a, edge_b, coefs, scalars,
    mine, other, own, updated, rho_v, mom_v, out_v, pad, rhs, sems,
):
    nx, tiles, _, nz = density.shape
    ny = tiles * ROWS
    copies = [
        pltpu.make_async_copy(density, rho_v, sems.at[0]),
        pltpu.make_async_copy(momentum, mom_v, sems.at[1]),
    ]
    for copy in copies:
        copy.start()
    is_odd = lax.rem(lax.axis_index("gy"), 2) == 1
    low, high = halos_y(is_odd, edge_a[...], edge_b[...])
    for f in range(3):
        for x in range(nx):
            pad[f, x, ROWS : ROWS + ny] = flux_y[f, x].reshape(ny, nz)
            for k in range(3):
                pad[f, x, ROWS - 3 + k : ROWS - 2 + k] = low[3 * f + k, x : x + 1]
                pad[f, x, ROWS + ny + k : ROWS + ny + k + 1] = high[3 * f + k, x : x + 1]
    is_left = lax.rem(lax.div(lax.axis_index("gx"), 1 << (stages - 1)), 2) == 0
    sign = jnp.where(is_left, 1.0, -1.0)
    inv = sign / (mine[3 * tiles, 0:1] + other[3 * tiles, 0:1])
    m = scalars[2:3]
    jin, jout = [], []
    for f in range(3):
        at = slice(f * tiles, (f + 1) * tiles)
        mid = (other[at] - mine[at]) * inv
        jin.append(own[at] + own[6 * tiles, 0:1] * mid)
        jout.append(own[(3 + f) * tiles : (4 + f) * tiles] + own[6 * tiles, 1:2] * mid)
    for copy in copies:
        copy.wait()
    outs = []
    for f in range(3):
        total = -jin[f]
        for x in range(nx):
            dy = sixth(lambda s: pad[f, x, ROWS + s : ROWS + s + ny])
            dz = sixth_z(*[r[f, x].reshape(ny, nz) for r in (flux_z, flux_z_low, flux_z_high)])
            state = rho_v[x] if f == 0 else mom_v[f - 1, x]
            r = state - scale * (dy + dz).reshape(tiles, ROWS, nz)
            rhs[x] = r
            total = total + coefs[x] * r
            out_v[f, x] = total
        total = m * jout[f]
        for x in range(nx - 1, -1, -1):
            out_v[f, x] = coefs[nx + x] * out_v[f, x] + coefs[x] * total
            if x > 0:
                total = total + coefs[nx + x] * rhs[x]
        copy = pltpu.make_async_copy(out_v.at[f], updated.at[f], sems.at[2 + f])
        copy.start()
        outs.append(copy)
    for copy in outs:
        copy.wait()


def params(limit=48):
    return pltpu.CompilerParams(vmem_limit_bytes=limit * 1024 * 1024)


def swap_edges(block_a, block_b, axis):
    count = lax.axis_size(axis)
    return (
        lax.ppermute(block_a, axis, pairing(count, False)),
        lax.ppermute(block_b, axis, pairing(count, True)),
    )


def on_device(density, momentum, lower_face):
    nx, ny, nz = density.shape
    tiles = ny // ROWS
    density = density.reshape(nx, tiles, ROWS, nz)
    momentum = momentum.reshape(2, nx, tiles, ROWS, nz)
    devices = lax.axis_size("gx")
    stages = (devices - 1).bit_length()
    full = lambda *lead: jax.ShapeDtypeStruct(lead + (ROWS, nz), F32)
    flux_y, flux_z, sums, small_a, small_b, edge_a, edge_b, coefs, scalars = pl.pallas_call(
        first_kernel,
        in_specs=[SMEM, ANY, ANY],
        out_specs=[VMEM] * 9,
        out_shape=[
            full(3, nx, tiles),
            full(4, nx, tiles),
            full(12 * tiles),
            full(6),
            full(6),
            jax.ShapeDtypeStruct((9, nx, nz), F32),
            jax.ShapeDtypeStruct((9, nx, nz), F32),
            full(2 * nx),
            full(),
        ],
        scratch_shapes=[
            pltpu.VMEM((nx, tiles, ROWS, nz), F32),
            pltpu.VMEM((2, nx, tiles, ROWS, nz), F32),
            pltpu.SemaphoreType.DMA((2,)),
        ],
        compiler_params=params(),
        name="fluxes",
    )(lower_face, density, momentum)
    count_z = lax.axis_size("gz")
    if count_z == 2:
        z_low = z_high = lax.ppermute(flux_z, "gz", [(0, 1), (1, 0)])
    else:
        ring = [(i, (i + 1) % count_z) for i in range(count_z)]
        z_low = lax.ppermute(flux_z, "gz", ring)
        z_high = lax.ppermute(flux_z, "gz", [(b, a) for a, b in ring])
    got_a, got_b = swap_edges(small_a, small_b, "gy")
    far_a, far_b = swap_edges(edge_a, edge_b, "gy")
    msg_shapes = [full(6 * tiles + 1), full(3 * tiles + 1)]
    msg, own = pl.pallas_call(
        functools.partial(second_kernel, stages, nx),
        in_specs=[VMEM] * 7,
        out_specs=[VMEM] * 2,
        out_shape=[msg_shapes[stages == 1], full(6 * tiles + 1)],
        scratch_shapes=[pltpu.VMEM((6, ny + 2 * ROWS, nz), F32)],
        compiler_params=params(),
        name="interface",
    )(sums, scalars, flux_z[3, :6], z_low[3, :6], z_high[3, :6], got_a, got_b)
    other = lax.ppermute(msg, "gx", partner_by(devices, 1))
    for stage in range(stages - 1):
        extra = () if stage == 0 else (own,)
        msg, own = pl.pallas_call(
            functools.partial(join_kernel, stage, stages, tiles),
            in_specs=[VMEM] * (2 + len(extra)),
            out_specs=[VMEM] * 2,
            out_shape=[msg_shapes[stage + 2 == stages], full(6 * tiles + 1)],
            compiler_params=params(),
            name="join",
        )(msg, other, *extra)
        other = lax.ppermute(msg, "gx", partner_by(devices, 2 << stage))
    updated = pl.pallas_call(
        functools.partial(last_kernel, stages),
        in_specs=[ANY, ANY] + [VMEM] * 11,
        out_specs=ANY,
        out_shape=full(3, nx, tiles),
        scratch_shapes=[
            pltpu.VMEM((nx, tiles, ROWS, nz), F32),
            pltpu.VMEM((2, nx, tiles, ROWS, nz), F32),
            pltpu.VMEM((3, nx, tiles, ROWS, nz), F32),
            pltpu.VMEM((3, nx, ny + 2 * ROWS, nz), F32),
            pltpu.VMEM((nx, tiles, ROWS, nz), F32),
            pltpu.SemaphoreType.DMA((5,)),
        ],
        compiler_params=params(),
        name="solve",
    )(density, momentum, flux_y, flux_z, z_low, z_high, far_a, far_b, coefs, scalars, msg, other, own)
    return updated.reshape(3, nx, ny, nz)


def solution(mesh):
    placed = (P("gx", "gy", "gz"), P(None, "gx", "gy", "gz"), P("gx"))
    return jax.shard_map(
        on_device, mesh=mesh, in_specs=placed, out_specs=P(None, "gx", "gy", "gz"), check_vma=False
    )
```

time: 81.6 us -> 24.3 us (0.30)
  blocking collectives: 31.6 us -> 0 us
  other arithmetic: 16.1 us -> 0 us
  local copies, waits for them, and re-layouts: 10.6 us -> 2.66 us
  matrix products: 7.43 us -> 0 us
  between operations: 5.44 us -> 0.05 us
  starting transfers between devices: 5.81 us -> 10.3 us
  Pallas kernels: 0 us -> 4.42 us
  waiting for transfers between devices: 4.32 us -> 6.66 us
    all_gather x3 -> x0, blocking collectives: 31.6 us -> none  [the longest x1 13.7 us: on_device(): lax.all_gather(rows, 'gx', axis=0, tiled=True)]
    dot_general x15 -> x0, matrix products: 6.99 us -> none  [the longest x6 4.65 us: mat_vec(): jnp.einsum('nij,njab->niab', left, vec, precision=lax.Precision.HIGHEST)]
    another operation x14 -> x0, other arithmetic: 6.93 us -> none  [the longest x3 3.59 us: on_device(): factor = jnp.linalg.cholesky(block)]
    ppermute x5 -> x7, starting transfers between devices: 5.81 us -> 10.3 us  [the longest x2 4.05 us: swap_edges(): lax.ppermute(block_a, axis, pairing(count, False))]
    pallas_call x0 -> x4, Pallas kernels: none -> 4.42 us  [the longest x1 2.48 us: on_device(): pl.pallas_call(functools.partial(last_kernel, stages), in_specs=[ANY, ANY...]
    mul x5 -> x0, other arithmetic: 4.36 us -> none  [the longest x2 2.13 us: on_device(): flux_z = z_band * (z_band[2] / z_band[0])[None]]
    slice x14 -> x0, local copies, waits for them, and re-layouts: 4.11 us -> none  [the longest x2 1.52 us: with_halo(): lax.slice_in_dim(block, block.shape[dim] - width, None, axis=dim)]
    ppermute x4 -> x0, local copies, waits for them, and re-layouts: 4.02 us -> none  [the longest x2 2.51 us: with_halo(): lax.ppermute(lax.slice_in_dim(block, 0, width, axis=dim), axis, backward)]
  transfers between devices with their start and end apart: 5 -> 7, of which waited for: 1 -> 3; matrix products, arithmetic and copies ran while one was open for 19% -> 0% of each run, Pallas kernels for 0% -> 3%
where the time goes in v1:
time: 24.3 us; the launch traced here: 24.1 us
  starting transfers between devices  10.3 us (42%)
  waiting for transfers between devices  6.66 us (27%)
  Pallas kernels  4.42 us (18%)
  local copies, waits for them, and re-layouts  2.66 us (11%)
    ppermute x2, starting transfers between devices, swap_edges(): lax.ppermute(block_a, axis, pairing(count, False))  4.05 us
    ppermute x1, starting transfers between devices, on_device(): other = lax.ppermute(msg, 'gx', partner_by(devices, 2 << stage))  2.65 us
    unnamed x10, local copies, waits for them, and re-layouts  2.65 us
    ppermute x1, waiting for transfers between devices, on_device(): other = lax.ppermute(msg, 'gx', partner_by(devices, 1))  2.56 us
    pallas_call x1, Pallas kernels, on_device(): pl.pallas_call(functools.partial(last_kernel, stages), in_specs=[ANY, ANY...  2.48 us
    ppermute x1, waiting for transfers between devices, on_device(): other = lax.ppermute(msg, 'gx', partner_by(devices, 2 << stage))  2.17 us
    ppermute x2, waiting for transfers between devices, swap_edges(): lax.ppermute(block_b, axis, pairing(count, True))  1.92 us
    ppermute x1, starting transfers between devices, on_device(): other = lax.ppermute(msg, 'gx', partner_by(devices, 1))  1.58 us
  transfers between devices with their start and end apart: 7, of which 3 were waited for; matrix products, arithmetic and copies ran while one was open for 0% of the time, Pallas kernels for 3%

profile of v1, /device:TPU:0, one launch (start us, length us, event | category | flops | bytes accessed | tf_op | source)
XLA Modules:
  0.0 24.1 jit_solution(1516387005769772327)
XLA Ops:
  0.0 0.0 copy-start.4
  0.0 0.7 %copy-done.4 = f32[32]{0:T(128)S(1)} copy-done((f32[32]{0:T(128)S(1)}, f32[32]{0:T(128)}, u32[]{:S(2)}) %copy-start.4) | copy-done | bytes 152
  0.7 0.0 copy-start
  0.7 1.0 %copy-done = f32[2,32,16,128]{3,2,1,0:T(8,128)S(1)} copy-done((f32[2,32,16,128]{3,2,1,0:T(8,128)S(1)}, f32[2,32,16,128]{3,2,1,0:T(8,128)}, u32[]{:S(2)}) %copy-start) | copy-done | bytes 524312
  1.7 0.0 copy-start.2
  1.7 0.9 %copy-done.2 = f32[32,16,128]{2,1,0:T(8,128)S(1)} copy-done((f32[32,16,128]{2,1,0:T(8,128)S(1)}, f32[32,16,128]{2,1,0:T(8,128)}, u32[]{:S(2)}) %copy-start.2) | copy-done | bytes 262168
  2.6 0.0 copy-start.1
  2.7 1.2 %fluxes.1 = (f32[3,32,2,8,128]{4,3,2,1,0:T(8,128)S(1)}, f32[4,32,2,8,128]{4,3,2,1,0:T(8,128)S(1)}, f32[24,8,128]{2,1,0:T(8,128)S(1)}, f32[6,8,128]{2,1,0:T(8,128...) custom-call(f32[32]{0:T(128)S(1)} %copy-done.4, ...), custom_call_target="tpu_custom_call" | custom-call | tf_op jit(solution)/shard_map/fluxes/pallas_call | solution.py:362
  3.9 0.5 %collective-permute-start = (f32[4,32,2,8,128]{4,3,2,1,0:T(8,128)S(1)}, f32[4,32,2,8,128]{4,3,2,1,0:T(8,128)S(1)}, u32[]{:S(2)}, u32[]{:S(2)}) collective-permute-start(f32[4,32,2,8,128]{4,3,2,1,0:T(8,128)S(1)} %get-tuple-element.18.flux_z), channel_id=1, source_target_pairs={{0,1},{1,0},{2,3},{3,2},{4,5},{5,4},{6,7},{7,6},{8,9},{9,8},{10,11... | collective-permute-start | bytes 3145736 | tf_op jit(solution)/shard_map/ppermute | solution.py:387
  4.4 2.6 %collective-permute-start.3 = (f32[6,8,128]{2,1,0:T(8,128)S(1)}, f32[6,8,128]{2,1,0:T(8,128)S(1)}, u32[]{:S(2)}, u32[]{:S(2)}) collective-permute-start(f32[6,8,128]{2,1,0:T(8,128)S(1)} %get-tuple-element.24), channel_id=1, source_target_pairs={{0,2},{2,0},{4,6},{6,4},{1,3},{3,1},{5,7},{7,5},{8,10},{10,8},{12,... | collective-permute-start | bytes 73736 | tf_op jit(solution)/shard_map/ppermute | solution.py:349
  6.9 1.5 %collective-permute-start.4 = (f32[6,8,128]{2,1,0:T(8,128)S(1)}, f32[6,8,128]{2,1,0:T(8,128)S(1)}, u32[]{:S(2)}, u32[]{:S(2)}) collective-permute-start(f32[6,8,128]{2,1,0:T(8,128)S(1)} %get-tuple-element.25), channel_id=1, source_target_pairs={{2,4},{4,2},{6,0},{0,6},{3,5},{5,3},{7,1},{1,7},{10,12},{12,10},{1... | collective-permute-start | bytes 73736 | tf_op jit(solution)/shard_map/ppermute | solution.py:350
  8.4 1.5 %collective-permute-start.1 = (f32[9,32,128]{2,1,0:T(8,128)S(1)}, f32[9,32,128]{2,1,0:T(8,128)S(1)}, u32[]{:S(2)}, u32[]{:S(2)}) collective-permute-start(f32[9,32,128]{2,1,0:T(8,128)S(1)} %get-tuple-element.19), channel_id=1, source_target_pairs={{0,2},{2,0},{4,6},{6,4},{1,3},{3,1},{5,7},{7,5},{8,10},{10,8},{12,... | collective-permute-start | bytes 442376 | tf_op jit(solution)/shard_map/ppermute | solution.py:349
  9.9 0.0 collective-permute-start.2
  10.0 0.0 copy-start.3
  10.0 0.0 collective-permute-done.flux_z_low.flux_z_high
  10.0 0.0 collective-permute-done.3.small_a
  10.0 1.9 %collective-permute-done.4.small_b = f32[6,8,128]{2,1,0:T(8,128)S(1)} collective-permute-done((f32[6,8,128]{2,1,0:T(8,128)S(1)}, f32[6,8,128]{2,1,0:T(8,128)S(1)}, u32[]{:S(2)}, u32[]{:S(2)}) %collective-permute-start.4) | collective-permute-done | bytes 24608 | tf_op jit(solution)/shard_map/ppermute | solution.py:350
  11.9 0.7 %interface.1 = (f32[13,8,128]{2,1,0:T(8,128)S(1)}, f32[13,8,128]{2,1,0:T(8,128)}) custom-call(f32[24,8,128]{2,1,0:T(8,128)S(1)} %get-tuple-element.23.sums, f32[8,128]{1,0:T(8,128)S(1)} %get-tuple-element.22.scalars, f32[6,2,8,128]{3,2,1,0:T(8,128)S(1)} %slice_bitcast_fusion.1.zsum, f32[6,2,8,128]{3,2,1,0:T(8,128)S(1)} %slice_bitcast_fusion.zsum_low.zsum_high, ...), custom_call_target="tpu_custom_call" | custom-call | tf_op jit(solution)/shard_map/interface/pallas_call | solution.py:395
  12.6 1.6 %collective-permute-start.5 = (f32[13,8,128]{2,1,0:T(8,128)S(1)}, f32[13,8,128]{2,1,0:T(8,128)S(1)}, u32[]{:S(2)}, u32[]{:S(2)}) collective-permute-start(f32[13,8,128]{2,1,0:T(8,128)S(1)} %get-tuple-element.26.refs_0_), channel_id=1, source_target_pairs={{0,8},{8,0},{16,24},{24,16},{1,9},{9,1},{17,25},{25,17},{2,10},{10... | collective-permute-start | bytes 159752 | tf_op jit(solution)/shard_map/ppermute | solution.py:404
  14.2 2.6 %collective-permute-done.5.refs_1_ = f32[13,8,128]{2,1,0:T(8,128)S(1)} collective-permute-done((f32[13,8,128]{2,1,0:T(8,128)S(1)}, f32[13,8,128]{2,1,0:T(8,128)S(1)}, u32[]{:S(2)}, u32[]{:S(2)}) %collective-permute-start.5) | collective-permute-done | bytes 53280 | tf_op jit(solution)/shard_map/ppermute | solution.py:404
  16.8 2.7 %collective-permute-start.6 = (f32[7,8,128]{2,1,0:T(8,128)S(1)}, f32[7,8,128]{2,1,0:T(8,128)S(1)}, u32[]{:S(2)}, u32[]{:S(2)}) collective-permute-start(f32[7,8,128]{2,1,0:T(8,128)S(1)} %get-tuple-element.27.mine), channel_id=1, source_target_pairs={{0,16},{8,24},{16,0},{24,8},{1,17},{9,25},{17,1},{25,9},{2,18},{10... | collective-permute-start | bytes 86024 | tf_op jit(solution)/shard_map/ppermute | solution.py:415
  19.4 0.0 collective-permute-done.1.edge_a
  19.4 0.0 collective-permute-done.2.edge_b
  19.4 2.2 %collective-permute-done.6.other = f32[7,8,128]{2,1,0:T(8,128)S(1)} collective-permute-done((f32[7,8,128]{2,1,0:T(8,128)S(1)}, f32[7,8,128]{2,1,0:T(8,128)S(1)}, u32[]{:S(2)}, u32[]{:S(2)}) %collective-permute-start.6) | collective-permute-done | bytes 28704 | tf_op jit(solution)/shard_map/ppermute | solution.py:415
  21.6 0.0 copy-done.1
  21.6 0.0 copy-done.3
  21.6 2.5 %solve.1 = f32[3,32,2,8,128]{4,3,2,1,0:T(8,128)} custom-call(f32[32,2,8,128]{3,2,1,0:T(8,128)S(1)} %bitcast.10, f32[2,32,2,8,128]{4,3,2,1,0:T(8,128)S(1)} %bitcast.8, f32[3,32,2,8,128]{4,3,2,1,0:T(8,128)S(1)} %get-tuple-element.17.flux_y, f32[4,32,2,8,128]{4,3,2,1,0:T(8,128)S(1)} %get-tuple-element.18.flux_z, ...), custom_call_target="tpu_custom_call" | custom-call | tf_op jit(solution)/shard_map/solve/pallas_call | solution.py:416
  (3 shorter events, 0.0 us)
Async XLA Ops:
  0.0 0.7 %copy-start.4 = (f32[32]{0:T(128)S(1)}, f32[32]{0:T(128)}, u32[]{:S(2)}) copy-start(f32[32]{0:T(128)} %faces.1) | copy-start | bytes 388
  0.7 1.0 %copy-start = (f32[2,32,16,128]{3,2,1,0:T(8,128)S(1)}, f32[2,32,16,128]{3,2,1,0:T(8,128)}, u32[]{:S(2)}) copy-start(f32[2,32,16,128]{3,2,1,0:T(8,128)} %param.4) | copy-start | bytes 1572868
  1.7 0.9 %copy-start.2 = (f32[32,16,128]{2,1,0:T(8,128)S(1)}, f32[32,16,128]{2,1,0:T(8,128)}, u32[]{:S(2)}) copy-start(f32[32,16,128]{2,1,0:T(8,128)} %param.3) | copy-start | bytes 786436
  2.6 19.0 %copy-start.1 = (f32[2,32,16,128]{3,2,1,0:T(8,128)S(1)}, f32[2,32,16,128]{3,2,1,0:T(8,128)}, u32[]{:S(2)}) copy-start(f32[2,32,16,128]{3,2,1,0:T(8,128)} %param.4) | copy-start | bytes 1572868
  3.9 6.1 %collective-permute-start = (f32[4,32,2,8,128]{4,3,2,1,0:T(8,128)S(1)}, f32[4,32,2,8,128]{4,3,2,1,0:T(8,128)S(1)}, u32[]{:S(2)}, u32[]{:S(2)}) collective-permute-start(f32[4,32,2,8,128]{4,3,2,1,0:T(8,128)S(1)} %get-tuple-element.18.flux_z), channel_id=1, source_target_pairs={{0,1},{1,0},{2,3},{3,2},{4,5},{5,4},{6,7},{7,6},{8,9},{9,8},{10,11... | collective-permute-start | bytes 3145736 | tf_op jit(solution)/shard_map/ppermute | solution.py:387
  4.4 5.6 %collective-permute-start.3 = (f32[6,8,128]{2,1,0:T(8,128)S(1)}, f32[6,8,128]{2,1,0:T(8,128)S(1)}, u32[]{:S(2)}, u32[]{:S(2)}) collective-permute-start(f32[6,8,128]{2,1,0:T(8,128)S(1)} %get-tuple-element.24), channel_id=1, source_target_pairs={{0,2},{2,0},{4,6},{6,4},{1,3},{3,1},{5,7},{7,5},{8,10},{10,8},{12,... | collective-permute-start | bytes 73736 | tf_op jit(solution)/shard_map/ppermute | solution.py:349
  6.9 5.0 %collective-permute-start.4 = (f32[6,8,128]{2,1,0:T(8,128)S(1)}, f32[6,8,128]{2,1,0:T(8,128)S(1)}, u32[]{:S(2)}, u32[]{:S(2)}) collective-permute-start(f32[6,8,128]{2,1,0:T(8,128)S(1)} %get-tuple-element.25), channel_id=1, source_target_pairs={{2,4},{4,2},{6,0},{0,6},{3,5},{5,3},{7,1},{1,7},{10,12},{12,10},{1... | collective-permute-start | bytes 73736 | tf_op jit(solution)/shard_map/ppermute | solution.py:350
  8.4 11.0 %collective-permute-start.1 = (f32[9,32,128]{2,1,0:T(8,128)S(1)}, f32[9,32,128]{2,1,0:T(8,128)S(1)}, u32[]{:S(2)}, u32[]{:S(2)}) collective-permute-start(f32[9,32,128]{2,1,0:T(8,128)S(1)} %get-tuple-element.19), channel_id=1, source_target_pairs={{0,2},{2,0},{4,6},{6,4},{1,3},{3,1},{5,7},{7,5},{8,10},{10,8},{12,... | collective-permute-start | bytes 442376 | tf_op jit(solution)/shard_map/ppermute | solution.py:349
  9.9 9.5 %collective-permute-start.2 = (f32[9,32,128]{2,1,0:T(8,128)S(1)}, f32[9,32,128]{2,1,0:T(8,128)S(1)}, u32[]{:S(2)}, u32[]{:S(2)}) collective-permute-start(f32[9,32,128]{2,1,0:T(8,128)S(1)} %get-tuple-element.20), channel_id=1, source_target_pairs={{2,4},{4,2},{6,0},{0,6},{3,5},{5,3},{7,1},{1,7},{10,12},{12,10},{1... | collective-permute-start | bytes 442376 | tf_op jit(solution)/shard_map/ppermute | solution.py:350
  10.0 11.7 %copy-start.3 = (f32[32,16,128]{2,1,0:T(8,128)S(1)}, f32[32,16,128]{2,1,0:T(8,128)}, u32[]{:S(2)}) copy-start(f32[32,16,128]{2,1,0:T(8,128)} %param.3) | copy-start | bytes 786436
  12.6 4.1 %collective-permute-start.5 = (f32[13,8,128]{2,1,0:T(8,128)S(1)}, f32[13,8,128]{2,1,0:T(8,128)S(1)}, u32[]{:S(2)}, u32[]{:S(2)}) collective-permute-start(f32[13,8,128]{2,1,0:T(8,128)S(1)} %get-tuple-element.26.refs_0_), channel_id=1, source_target_pairs={{0,8},{8,0},{16,24},{24,16},{1,9},{9,1},{17,25},{25,17},{2,10},{10... | collective-permute-start | bytes 159752 | tf_op jit(solution)/shard_map/ppermute | solution.py:404
  16.8 4.8 %collective-permute-start.6 = (f32[7,8,128]{2,1,0:T(8,128)S(1)}, f32[7,8,128]{2,1,0:T(8,128)S(1)}, u32[]{:S(2)}, u32[]{:S(2)}) collective-permute-start(f32[7,8,128]{2,1,0:T(8,128)S(1)} %get-tuple-element.27.mine), channel_id=1, source_target_pairs={{0,16},{8,24},{16,0},{24,8},{1,17},{9,25},{17,1},{25,9},{2,18},{10... | collective-permute-start | bytes 86024 | tf_op jit(solution)/shard_map/ppermute | solution.py:415

commit v2 on v1

--- a/solution.py
+++ b/solution.py
@@ -12,8 +12,8 @@
 ROWS = 8
 F32 = jnp.float32
 VMEM = pl.BlockSpec(memory_space=pltpu.VMEM)
-SMEM = pl.BlockSpec(memory_space=pltpu.SMEM)
 ANY = pl.BlockSpec(memory_space=pl.ANY)
+HBM = pl.BlockSpec(memory_space=pltpu.HBM)
 
 
 def pairing(count, odd):
@@ -156,18 +156,23 @@
 def first_kernel(
     faces, density, momentum,
     flux_y, flux_z, sums, small_a, small_b, edge_a, edge_b, coefs, scalars,
-    rho_v, mom_v, sems,
+    face_s, rho_v, mom_v, sems,
 ):
     nx, tiles, _, nz = density.shape
     ny = tiles * ROWS
+    pitch = ny + ROWS
     copies = [
-        pltpu.make_async_copy(density, rho_v, sems.at[0]),
-        pltpu.make_async_copy(momentum, mom_v, sems.at[1]),
+        pltpu.make_async_copy(faces, face_s, sems.at[0]),
+        pltpu.make_async_copy(density, rho_v, sems.at[1]),
+        pltpu.make_async_copy(momentum, mom_v, sems.at[2]),
     ]
     for copy in copies:
         copy.start()
     tile = (ROWS, nz)
-    inv = [1.0 / jnp.full(tile, faces[i], F32) for i in range(nx)]
+    for line in range(3 * nx + 1):
+        flux_y[line * pitch : line * pitch + ROWS] = jnp.zeros(tile, F32)
+    copies[0].wait()
+    inv = [1.0 / jnp.full(tile, face_s[i], F32) for i in range(nx)]
     phi = [jnp.ones(tile, F32)]
     flux = phi[0]
     for i in range(1, nx):
@@ -189,7 +194,7 @@
     scalars[3:4] = inv[0][0:1]
     scalars[4:5] = inv[nx - 1][0:1]
     scalars[5:8] = jnp.zeros((3, nz), F32)
-    for copy in copies:
+    for copy in copies[1:]:
         copy.wait()
     total = [[None] * 9, [None] * 9]
     for x in range(nx):
@@ -199,13 +204,16 @@
         cross = m0 * v1
         values = (rho, m0, m1, m0, m0 * v0, cross, m1, cross, m1 * v1)
         for f in range(3):
-            flux_y[f, x] = values[3 + f]
+            at = (f * nx + x) * pitch + ROWS
+            flux_y[at : at + ny] = values[3 + f].reshape(ny, nz)
             flux_z[f, x] = values[6 + f]
         for side, weight in enumerate((coefs[nx + x], coefs[x])):
             for k, value in enumerate(values):
-                term = value * weight
-                total[side][k] = term if x == 0 else total[side][k] + term
+                if k not in (3, 6):
+                    term = value * weight
+                    total[side][k] = term if x == 0 else total[side][k] + term
     for side in range(2):
+        total[side][3], total[side][6] = total[side][1], total[side][2]
         for f in range(3):
             at = (3 * side + f) * tiles
             sums[at : at + tiles] = total[side][f]
@@ -216,11 +224,10 @@
         for k in range(6):
             at = (6 + k) * tiles + high * (tiles - 1)
             ref_small[k] = sums[pl.ds(at, 1)][0]
-        start = high * (ny - 3)
+        start = ROWS + high * (ny - 3)
         for f in range(3):
-            for x in range(nx):
-                for k in range(3):
-                    ref_edge[3 * f + k, x : x + 1] = flux_y.at[f, x].reshape(ny, nz)[pl.ds(start + k, 1)]
+            for k in range(3):
+                ref_edge[3 * f + k] = flux_y[pl.ds(start + f * nx * pitch + k, nx, stride=pitch)]
 
 
 def halos_y(is_odd, from_a, from_b):
@@ -230,8 +237,9 @@
 
 
 def second_kernel(
-    stages, nx, sums, scalars, zsum, zsum_low, zsum_high, small_a, small_b, msg, own, pad
+    stages, sums, scalars, zsum, zsum_low, zsum_high, small_a, small_b, *refs
 ):
+    msg, pad = refs[0], refs[-1]
     nblocks, _, nz = sums.shape
     tiles = nblocks // 12
     ny = tiles * ROWS
@@ -251,14 +259,13 @@
     first = jnp.stack(values[:3])
     last = jnp.stack(values[3:]) * m
     group = (first, last, alpha, beta, m, inv_first, inv_last)
-    forms = [(0.0, 1.0, 0.0), (0.0, 0.0, 1.0)]
     if stages == 1:
         is_left = lax.rem(lax.axis_index("gx"), 2) == 0
         zero = jnp.zeros_like(first)
         one = jnp.ones_like(alpha)
         forms = [(zero, one, 0.0 * one), (zero, 0.0 * one, one)]
         facing, resist, out = closing(is_left, group, forms)
-        store_closing(msg, own, facing, resist, out, tiles)
+        store_closing(msg, refs[1], facing, resist, out, tiles)
     else:
         store_group(msg, group, tiles)
 
@@ -284,55 +291,67 @@
         store_forms(own, forms, tiles)
 
 
-def last_kernel(
-    stages, density, momentum, flux_y, flux_z, flux_z_low, flux_z_high, edge_a, edge_b, coefs, scalars,
-    mine, other, own, updated, rho_v, mom_v, out_v, pad, rhs, sems,
-):
+def rhs_kernel(density, momentum, flux_y, flux_z, flux_z_low, flux_z_high, after, rhs):
     nx, tiles, _, nz = density.shape
     ny = tiles * ROWS
-    copies = [
-        pltpu.make_async_copy(density, rho_v, sems.at[0]),
-        pltpu.make_async_copy(momentum, mom_v, sems.at[1]),
-    ]
-    for copy in copies:
-        copy.start()
+    pitch = ny + ROWS
+    for f in range(3):
+        for x in range(nx):
+            at = (f * nx + x) * pitch + ROWS
+            dy = sixth(lambda s: flux_y[at + s : at + s + ny])
+            dz = sixth_z(*[r[f, x].reshape(ny, nz) for r in (flux_z, flux_z_low, flux_z_high)])
+            state = density[x] if f == 0 else momentum[f - 1, x]
+            rhs[f, x] = state - scale * (dy + dz).reshape(tiles, ROWS, nz)
+
+
+def sums_kernel(rhs, edge_a, edge_b, coefs, ahead, behind, lines):
+    _, nx, tiles, _, nz = rhs.shape
+    ny = tiles * ROWS
     is_odd = lax.rem(lax.axis_index("gy"), 2) == 1
     low, high = halos_y(is_odd, edge_a[...], edge_b[...])
     for f in range(3):
         for x in range(nx):
-            pad[f, x, ROWS : ROWS + ny] = flux_y[f, x].reshape(ny, nz)
-            for k in range(3):
-                pad[f, x, ROWS - 3 + k : ROWS - 2 + k] = low[3 * f + k, x : x + 1]
-                pad[f, x, ROWS + ny + k : ROWS + ny + k + 1] = high[3 * f + k, x : x + 1]
+            lines[x * ny : (x + 1) * ny] = rhs[f, x].reshape(ny, nz)
+        l3, l2, l1 = [low[3 * f + k] * scale for k in range(3)]
+        h1, h2, h3 = [high[3 * f + k] * scale for k in range(3)]
+        for row, value in (
+            (0, 45.0 * l1 - 9.0 * l2 + l3),
+            (1, l2 - 9.0 * l1),
+            (2, l1),
+            (ny - 3, -h1),
+            (ny - 2, 9.0 * h1 - h2),
+            (ny - 1, 9.0 * h2 - 45.0 * h1 - h3),
+        ):
+            at = pl.ds(row, nx, stride=ny)
+            lines[at] = lines[at] + value
+        total = None
+        for x in range(nx):
+            r = lines[x * ny : (x + 1) * ny].reshape(tiles, ROWS, nz)
+            total = coefs[x] * r if x == 0 else total + coefs[x] * r
+            ahead[f, x] = total
+        total = jnp.zeros((tiles, ROWS, nz), F32)
+        for x in range(nx - 1, -1, -1):
+            behind[f, x] = total
+            if x > 0:
+                r = lines[x * ny : (x + 1) * ny].reshape(tiles, ROWS, nz)
+                total = total + coefs[nx + x] * r
+
+
+def last_kernel(stages, ahead, behind, coefs, scalars, mine, other, own, updated, out_v, sems):
+    _, nx, tiles, _, nz = ahead.shape
     is_left = lax.rem(lax.div(lax.axis_index("gx"), 1 << (stages - 1)), 2) == 0
     sign = jnp.where(is_left, 1.0, -1.0)
     inv = sign / (mine[3 * tiles, 0:1] + other[3 * tiles, 0:1])
     m = scalars[2:3]
-    jin, jout = [], []
+    outs = []
     for f in range(3):
         at = slice(f * tiles, (f + 1) * tiles)
         mid = (other[at] - mine[at]) * inv
-        jin.append(own[at] + own[6 * tiles, 0:1] * mid)
-        jout.append(own[(3 + f) * tiles : (4 + f) * tiles] + own[6 * tiles, 1:2] * mid)
-    for copy in copies:
-        copy.wait()
-    outs = []
-    for f in range(3):
-        total = -jin[f]
+        jin = own[at] + own[6 * tiles, 0:1] * mid
+        jout = m * (own[(3 + f) * tiles : (4 + f) * tiles] + own[6 * tiles, 1:2] * mid)
         for x in range(nx):
-            dy = sixth(lambda s: pad[f, x, ROWS + s : ROWS + s + ny])
-            dz = sixth_z(*[r[f, x].reshape(ny, nz) for r in (flux_z, flux_z_low, flux_z_high)])
-            state = rho_v[x] if f == 0 else mom_v[f - 1, x]
-            r = state - scale * (dy + dz).reshape(tiles, ROWS, nz)
-            rhs[x] = r
-            total = total + coefs[x] * r
-            out_v[f, x] = total
-        total = m * jout[f]
-        for x in range(nx - 1, -1, -1):
-            out_v[f, x] = coefs[nx + x] * out_v[f, x] + coefs[x] * total
-            if x > 0:
-                total = total + coefs[nx + x] * rhs[x]
-        copy = pltpu.make_async_copy(out_v.at[f], updated.at[f], sems.at[2 + f])
+            out_v[f, x] = coefs[nx + x] * (ahead[f, x] - jin) + coefs[x] * (behind[f, x] + jout)
+        copy = pltpu.make_async_copy(out_v.at[f], updated.at[f], sems.at[f])
         copy.start()
         outs.append(copy)
     for copy in outs:
@@ -361,10 +380,10 @@
     full = lambda *lead: jax.ShapeDtypeStruct(lead + (ROWS, nz), F32)
     flux_y, flux_z, sums, small_a, small_b, edge_a, edge_b, coefs, scalars = pl.pallas_call(
         first_kernel,
-        in_specs=[SMEM, ANY, ANY],
+        in_specs=[HBM] * 3,
         out_specs=[VMEM] * 9,
         out_shape=[
-            full(3, nx, tiles),
+            jax.ShapeDtypeStruct((3 * nx * (ny + ROWS) + ROWS, nz), F32),
             full(4, nx, tiles),
             full(12 * tiles),
             full(6),
@@ -375,13 +394,14 @@
             full(),
         ],
         scratch_shapes=[
+            pltpu.SMEM((nx,), F32),
             pltpu.VMEM((nx, tiles, ROWS, nz), F32),
             pltpu.VMEM((2, nx, tiles, ROWS, nz), F32),
-            pltpu.SemaphoreType.DMA((2,)),
+            pltpu.SemaphoreType.DMA((3,)),
         ],
         compiler_params=params(),
         name="fluxes",
-    )(lower_face, density, momentum)
+    )(*(pltpu.with_memory_space_constraint(x, pltpu.HBM) for x in (lower_face, density, momentum)))
     count_z = lax.axis_size("gz")
     if count_z == 2:
         z_low = z_high = lax.ppermute(flux_z, "gz", [(0, 1), (1, 0)])
@@ -392,43 +412,58 @@
     got_a, got_b = swap_edges(small_a, small_b, "gy")
     far_a, far_b = swap_edges(edge_a, edge_b, "gy")
     msg_shapes = [full(6 * tiles + 1), full(3 * tiles + 1)]
-    msg, own = pl.pallas_call(
-        functools.partial(second_kernel, stages, nx),
+    msg, *own = pl.pallas_call(
+        functools.partial(second_kernel, stages),
         in_specs=[VMEM] * 7,
-        out_specs=[VMEM] * 2,
-        out_shape=[msg_shapes[stages == 1], full(6 * tiles + 1)],
+        out_specs=[VMEM] * (1 + (stages == 1)),
+        out_shape=[msg_shapes[1], full(6 * tiles + 1)] if stages == 1 else msg_shapes[:1],
         scratch_shapes=[pltpu.VMEM((6, ny + 2 * ROWS, nz), F32)],
         compiler_params=params(),
         name="interface",
     )(sums, scalars, flux_z[3, :6], z_low[3, :6], z_high[3, :6], got_a, got_b)
+    cells = 3 * nx * ny * nz
+    rhs = pl.pallas_call(
+        rhs_kernel,
+        in_specs=[VMEM] * 6 + [ANY],
+        out_specs=VMEM,
+        out_shape=full(3, nx, tiles),
+        compiler_params=params(),
+        cost_estimate=pl.CostEstimate(flops=20 * cells, bytes_accessed=16 * cells, transcendentals=0),
+        name="rhs",
+    )(density, momentum, flux_y, flux_z, z_low, z_high, msg)
     other = lax.ppermute(msg, "gx", partner_by(devices, 1))
     for stage in range(stages - 1):
-        extra = () if stage == 0 else (own,)
-        msg, own = pl.pallas_call(
+        msg, *own = pl.pallas_call(
             functools.partial(join_kernel, stage, stages, tiles),
-            in_specs=[VMEM] * (2 + len(extra)),
+            in_specs=[VMEM] * (2 + len(own)),
             out_specs=[VMEM] * 2,
             out_shape=[msg_shapes[stage + 2 == stages], full(6 * tiles + 1)],
             compiler_params=params(),
             name="join",
-        )(msg, other, *extra)
+        )(msg, other, *own)
         other = lax.ppermute(msg, "gx", partner_by(devices, 2 << stage))
+    ahead, behind = pl.pallas_call(
+        sums_kernel,
+        in_specs=[VMEM] * 4,
+        out_specs=[VMEM] * 2,
+        out_shape=[full(3, nx, tiles)] * 2,
+        scratch_shapes=[pltpu.VMEM((nx * ny, nz), F32)],
+        compiler_params=params(),
+        cost_estimate=pl.CostEstimate(flops=6 * cells, bytes_accessed=12 * cells, transcendentals=0),
+        name="sums",
+    )(rhs, far_a, far_b, coefs)
     updated = pl.pallas_call(
         functools.partial(last_kernel, stages),
-        in_specs=[ANY, ANY] + [VMEM] * 11,
-        out_specs=ANY,
+        in_specs=[VMEM] * 7,
+        out_specs=HBM,
         out_shape=full(3, nx, tiles),
         scratch_shapes=[
-            pltpu.VMEM((nx, tiles, ROWS, nz), F32),
-            pltpu.VMEM((2, nx, tiles, ROWS, nz), F32),
             pltpu.VMEM((3, nx, tiles, ROWS, nz), F32),
-            pltpu.VMEM((3, nx, ny + 2 * ROWS, nz), F32),
-            pltpu.VMEM((nx, tiles, ROWS, nz), F32),
-            pltpu.SemaphoreType.DMA((5,)),
+            pltpu.SemaphoreType.DMA((3,)),
         ],
         compiler_params=params(),
         name="solve",
-    )(density, momentum, flux_y, flux_z, z_low, z_high, far_a, far_b, coefs, scalars, msg, other, own)
+    )(ahead, behind, coefs, scalars, msg, other, own[0])
     return updated.reshape(3, nx, ny, nz)
 
 

time: 24.3 us -> 20 us (0.82)
  local copies, waits for them, and re-layouts: 2.66 us -> 0.02 us
  waiting for transfers between devices: 6.66 us -> 4.9 us
    unnamed x10 -> x4, local copies, waits for them, and re-layouts: 2.65 us -> 0.01 us
    ppermute x1, waiting for transfers between devices: 2.17 us -> 0.41 us  [on_device(): other = lax.ppermute(msg, 'gx', partner_by(devices, 2 << stage))]
    pallas_call x3 -> x5, Pallas kernels: 4.38 us -> 4.41 us  [the longest x1 1.55 us: on_device(): pl.pallas_call(first_kernel, in_specs=[HBM] * 3, out_specs=[VMEM] * 9, ou...]
  transfers between devices with their start and end apart: 7 -> 7, of which waited for: 3 -> 3; matrix products, arithmetic and copies ran while one was open for 0% -> 0% of each run, Pallas kernels for 3% -> 10%
where the time goes in v2:
time: 20 us; the launch traced here: 19.8 us
  starting transfers between devices  10.4 us (52%)
  waiting for transfers between devices  4.9 us (25%)
  Pallas kernels  4.44 us (22%)
    ppermute x2, starting transfers between devices, swap_edges(): lax.ppermute(block_a, axis, pairing(count, False))  4.06 us
    ppermute x1, starting transfers between devices, on_device(): other = lax.ppermute(msg, 'gx', partner_by(devices, 2 << stage))  2.65 us
    ppermute x1, waiting for transfers between devices, on_device(): other = lax.ppermute(msg, 'gx', partner_by(devices, 1))  2.56 us
    ppermute x2, waiting for transfers between devices, swap_edges(): lax.ppermute(block_b, axis, pairing(count, True))  1.93 us
    ppermute x1, starting transfers between devices, on_device(): other = lax.ppermute(msg, 'gx', partner_by(devices, 1))  1.64 us
    pallas_call x1, Pallas kernels, on_device(): pl.pallas_call(first_kernel, in_specs=[HBM] * 3, out_specs=[VMEM] * 9, ou...  1.55 us
    ppermute x2, starting transfers between devices, swap_edges(): lax.ppermute(block_b, axis, pairing(count, True))  1.51 us
    pallas_call x1, Pallas kernels, on_device(): pl.pallas_call(rhs_kernel, in_specs=[VMEM] * 6 + [ANY], out_specs=VMEM, o...  1.28 us
  transfers between devices with their start and end apart: 7, of which 3 were waited for; matrix products, arithmetic and copies ran while one was open for 0% of the time, Pallas kernels for 10%

profile of v2, /device:TPU:0, one launch (start us, length us, event | category | flops | bytes accessed | tf_op | source)
XLA Modules:
  0.0 19.8 jit_solution(5041825721022295940)
XLA Ops:
  0.0 0.0 copy-start
  0.0 0.0 copy-start.1
  0.0 1.6 %fluxes.1 = (f32[2312,128]{1,0:T(8,128)S(1)}, f32[4,32,2,8,128]{4,3,2,1,0:T(8,128)S(1)}, f32[24,8,128]{2,1,0:T(8,128)S(1)}, f32[6,8,128]{2,1,0:T(8,128)S(1)}, f3...) custom-call(f32[32]{0:T(128)} %faces.1, ...), custom_call_target="tpu_custom_call" | custom-call | tf_op jit(solution)/shard_map/fluxes/pallas_call | solution.py:381
  1.6 0.5 %collective-permute-start = (f32[4,32,2,8,128]{4,3,2,1,0:T(8,128)S(1)}, f32[4,32,2,8,128]{4,3,2,1,0:T(8,128)S(1)}, u32[]{:S(2)}, u32[]{:S(2)}) collective-permute-start(f32[4,32,2,8,128]{4,3,2,1,0:T(8,128)S(1)} %get-tuple-element.19.flux_z), channel_id=1, source_target_pairs={{0,1},{1,0},{2,3},{3,2},{4,5},{5,4},{6,7},{7,6},{8,9},{9,8},{10,11... | collective-permute-start | bytes 3145736 | tf_op jit(solution)/shard_map/ppermute | solution.py:407
  2.1 2.6 %collective-permute-start.1 = (f32[6,8,128]{2,1,0:T(8,128)S(1)}, f32[6,8,128]{2,1,0:T(8,128)S(1)}, u32[]{:S(2)}, u32[]{:S(2)}) collective-permute-start(f32[6,8,128]{2,1,0:T(8,128)S(1)} %get-tuple-element.22), channel_id=1, source_target_pairs={{0,2},{2,0},{4,6},{6,4},{1,3},{3,1},{5,7},{7,5},{8,10},{10,8},{12,... | collective-permute-start | bytes 73736 | tf_op jit(solution)/shard_map/ppermute | solution.py:368
  4.6 1.5 %collective-permute-start.2 = (f32[6,8,128]{2,1,0:T(8,128)S(1)}, f32[6,8,128]{2,1,0:T(8,128)S(1)}, u32[]{:S(2)}, u32[]{:S(2)}) collective-permute-start(f32[6,8,128]{2,1,0:T(8,128)S(1)} %get-tuple-element.23), channel_id=1, source_target_pairs={{2,4},{4,2},{6,0},{0,6},{3,5},{5,3},{7,1},{1,7},{10,12},{12,10},{1... | collective-permute-start | bytes 73736 | tf_op jit(solution)/shard_map/ppermute | solution.py:369
  6.1 1.5 %collective-permute-start.3 = (f32[9,32,128]{2,1,0:T(8,128)S(1)}, f32[9,32,128]{2,1,0:T(8,128)S(1)}, u32[]{:S(2)}, u32[]{:S(2)}) collective-permute-start(f32[9,32,128]{2,1,0:T(8,128)S(1)} %get-tuple-element.24), channel_id=1, source_target_pairs={{0,2},{2,0},{4,6},{6,4},{1,3},{3,1},{5,7},{7,5},{8,10},{10,8},{12,... | collective-permute-start | bytes 442376 | tf_op jit(solution)/shard_map/ppermute | solution.py:368
  7.6 0.0 collective-permute-start.4
  7.7 0.0 collective-permute-done.flux_z_low.flux_z_high
  7.7 0.0 collective-permute-done.1.small_a
  7.7 1.9 %collective-permute-done.2.small_b = f32[6,8,128]{2,1,0:T(8,128)S(1)} collective-permute-done((f32[6,8,128]{2,1,0:T(8,128)S(1)}, f32[6,8,128]{2,1,0:T(8,128)S(1)}, u32[]{:S(2)}, u32[]{:S(2)}) %collective-permute-start.2) | collective-permute-done | bytes 24608 | tf_op jit(solution)/shard_map/ppermute | solution.py:369
  9.6 0.1 interface.1.after.refs_0_
  9.8 1.6 %collective-permute-start.5 = (f32[13,8,128]{2,1,0:T(8,128)S(1)}, f32[13,8,128]{2,1,0:T(8,128)S(1)}, u32[]{:S(2)}, u32[]{:S(2)}) collective-permute-start(f32[13,8,128]{2,1,0:T(8,128)S(1)} %interface.1.after.refs_0_), channel_id=1, source_target_pairs={{0,8},{8,0},{16,24},{24,16},{1,9},{9,1},{17,25},{25,17},{2,10},{10... | collective-permute-start | bytes 159752 | tf_op jit(solution)/shard_map/ppermute | solution.py:434
  11.4 2.6 %collective-permute-done.5.refs_1_ = f32[13,8,128]{2,1,0:T(8,128)S(1)} collective-permute-done((f32[13,8,128]{2,1,0:T(8,128)S(1)}, f32[13,8,128]{2,1,0:T(8,128)S(1)}, u32[]{:S(2)}, u32[]{:S(2)}) %collective-permute-start.5) | collective-permute-done | bytes 53280 | tf_op jit(solution)/shard_map/ppermute | solution.py:434
  14.0 2.7 %collective-permute-start.6 = (f32[7,8,128]{2,1,0:T(8,128)S(1)}, f32[7,8,128]{2,1,0:T(8,128)S(1)}, u32[]{:S(2)}, u32[]{:S(2)}) collective-permute-start(f32[7,8,128]{2,1,0:T(8,128)S(1)} %get-tuple-element.29.mine), channel_id=1, source_target_pairs={{0,16},{8,24},{16,0},{24,8},{1,17},{9,25},{17,1},{25,9},{2,18},{10... | collective-permute-start | bytes 86024 | tf_op jit(solution)/shard_map/ppermute | solution.py:444
  16.7 0.0 copy-done
  16.7 0.0 copy-done.1
  16.7 1.3 %rhs.1 = f32[3,32,2,8,128]{4,3,2,1,0:T(8,128)S(1)} custom-call(f32[32,2,8,128]{3,2,1,0:T(8,128)S(1)} %bitcast.10, f32[2,32,2,8,128]{4,3,2,1,0:T(8,128)S(1)} %bitcast.8, f32[2312,128]{1,0:T(8,128)S(1)} %get-tuple-element.18.flux_y, f32[4,32,2,8,128]{4,3,2,1,0:T(8,128)S(1)} %get-tuple-element.19.flux_z, ...), custom_call_target="tpu_custom_call" | custom-call | flops 3932160 | bytes 3145728 | tf_op jit(solution)/shard_map/rhs/pallas_call | solution.py:425
  18.0 0.0 collective-permute-done.3.edge_a
  18.0 0.0 collective-permute-done.4.edge_b
  18.0 0.5 %sums.1 = (f32[3,32,2,8,128]{4,3,2,1,0:T(8,128)S(1)}, f32[3,32,2,8,128]{4,3,2,1,0:T(8,128)S(1)}) custom-call(f32[3,32,2,8,128]{4,3,2,1,0:T(8,128)S(1)} %rhs.1, f32[9,32,128]{2,1,0:T(8,128)S(1)} %collective-permute-done.3.edge_a, f32[9,32,128]{2,1,0:T(8,128)S(1)} %collective-permute-done.4.edge_b, f32[64,8,128]{2,1,0:T(8,128)S(1)} %get-tuple-element.26.coefs), custom_call_target="tpu_custom_call" | custom-call | flops 1179648 | bytes 2359296 | tf_op jit(solution)/shard_map/sums/pallas_call | solution.py:445
  18.4 0.4 %collective-permute-done.6.other = f32[7,8,128]{2,1,0:T(8,128)S(1)} collective-permute-done((f32[7,8,128]{2,1,0:T(8,128)S(1)}, f32[7,8,128]{2,1,0:T(8,128)S(1)}, u32[]{:S(2)}, u32[]{:S(2)}) %collective-permute-start.6) | collective-permute-done | bytes 28704 | tf_op jit(solution)/shard_map/ppermute | solution.py:444
  18.8 1.0 %solve.1 = f32[3,32,2,8,128]{4,3,2,1,0:T(8,128)} custom-call(f32[3,32,2,8,128]{4,3,2,1,0:T(8,128)S(1)} %get-tuple-element.27.ahead, f32[3,32,2,8,128]{4,3,2,1,0:T(8,128)S(1)} %get-tuple-element.28.behind, f32[64,8,128]{2,1,0:T(8,128)S(1)} %get-tuple-element.26.coefs, f32[8,128]{1,0:T(8,128)S(1)} %get-tuple-element.21.scalars, ...), custom_call_target="tpu_custom_call" | custom-call | tf_op jit(solution)/shard_map/solve/pallas_call | solution.py:455
  (3 shorter events, 0.0 us)
Async XLA Ops:
  0.0 16.7 %copy-start = (f32[2,32,16,128]{3,2,1,0:T(8,128)S(1)}, f32[2,32,16,128]{3,2,1,0:T(8,128)}, u32[]{:S(2)}) copy-start(f32[2,32,16,128]{3,2,1,0:T(8,128)} %param.4) | copy-start | bytes 1572868
  0.0 16.7 %copy-start.1 = (f32[32,16,128]{2,1,0:T(8,128)S(1)}, f32[32,16,128]{2,1,0:T(8,128)}, u32[]{:S(2)}) copy-start(f32[32,16,128]{2,1,0:T(8,128)} %param.3) | copy-start | bytes 786436
  1.6 6.1 %collective-permute-start = (f32[4,32,2,8,128]{4,3,2,1,0:T(8,128)S(1)}, f32[4,32,2,8,128]{4,3,2,1,0:T(8,128)S(1)}, u32[]{:S(2)}, u32[]{:S(2)}) collective-permute-start(f32[4,32,2,8,128]{4,3,2,1,0:T(8,128)S(1)} %get-tuple-element.19.flux_z), channel_id=1, source_target_pairs={{0,1},{1,0},{2,3},{3,2},{4,5},{5,4},{6,7},{7,6},{8,9},{9,8},{10,11... | collective-permute-start | bytes 3145736 | tf_op jit(solution)/shard_map/ppermute | solution.py:407
  2.1 5.6 %collective-permute-start.1 = (f32[6,8,128]{2,1,0:T(8,128)S(1)}, f32[6,8,128]{2,1,0:T(8,128)S(1)}, u32[]{:S(2)}, u32[]{:S(2)}) collective-permute-start(f32[6,8,128]{2,1,0:T(8,128)S(1)} %get-tuple-element.22), channel_id=1, source_target_pairs={{0,2},{2,0},{4,6},{6,4},{1,3},{3,1},{5,7},{7,5},{8,10},{10,8},{12,... | collective-permute-start | bytes 73736 | tf_op jit(solution)/shard_map/ppermute | solution.py:368
  4.6 5.0 %collective-permute-start.2 = (f32[6,8,128]{2,1,0:T(8,128)S(1)}, f32[6,8,128]{2,1,0:T(8,128)S(1)}, u32[]{:S(2)}, u32[]{:S(2)}) collective-permute-start(f32[6,8,128]{2,1,0:T(8,128)S(1)} %get-tuple-element.23), channel_id=1, source_target_pairs={{2,4},{4,2},{6,0},{0,6},{3,5},{5,3},{7,1},{1,7},{10,12},{12,10},{1... | collective-permute-start | bytes 73736 | tf_op jit(solution)/shard_map/ppermute | solution.py:369
  6.1 11.8 %collective-permute-start.3 = (f32[9,32,128]{2,1,0:T(8,128)S(1)}, f32[9,32,128]{2,1,0:T(8,128)S(1)}, u32[]{:S(2)}, u32[]{:S(2)}) collective-permute-start(f32[9,32,128]{2,1,0:T(8,128)S(1)} %get-tuple-element.24), channel_id=1, source_target_pairs={{0,2},{2,0},{4,6},{6,4},{1,3},{3,1},{5,7},{7,5},{8,10},{10,8},{12,... | collective-permute-start | bytes 442376 | tf_op jit(solution)/shard_map/ppermute | solution.py:368
  7.6 10.3 %collective-permute-start.4 = (f32[9,32,128]{2,1,0:T(8,128)S(1)}, f32[9,32,128]{2,1,0:T(8,128)S(1)}, u32[]{:S(2)}, u32[]{:S(2)}) collective-permute-start(f32[9,32,128]{2,1,0:T(8,128)S(1)} %get-tuple-element.25), channel_id=1, source_target_pairs={{2,4},{4,2},{6,0},{0,6},{3,5},{5,3},{7,1},{1,7},{10,12},{12,10},{1... | collective-permute-start | bytes 442376 | tf_op jit(solution)/shard_map/ppermute | solution.py:369
  9.8 4.2 %collective-permute-start.5 = (f32[13,8,128]{2,1,0:T(8,128)S(1)}, f32[13,8,128]{2,1,0:T(8,128)S(1)}, u32[]{:S(2)}, u32[]{:S(2)}) collective-permute-start(f32[13,8,128]{2,1,0:T(8,128)S(1)} %interface.1.after.refs_0_), channel_id=1, source_target_pairs={{0,8},{8,0},{16,24},{24,16},{1,9},{9,1},{17,25},{25,17},{2,10},{10... | collective-permute-start | bytes 159752 | tf_op jit(solution)/shard_map/ppermute | solution.py:434
  14.0 4.8 %collective-permute-start.6 = (f32[7,8,128]{2,1,0:T(8,128)S(1)}, f32[7,8,128]{2,1,0:T(8,128)S(1)}, u32[]{:S(2)}, u32[]{:S(2)}) collective-permute-start(f32[7,8,128]{2,1,0:T(8,128)S(1)} %get-tuple-element.29.mine), channel_id=1, source_target_pairs={{0,16},{8,24},{16,0},{24,8},{1,17},{9,25},{17,1},{25,9},{2,18},{10... | collective-permute-start | bytes 86024 | tf_op jit(solution)/shard_map/ppermute | solution.py:444

commit v3 on v2

v3 whole, which is shorter than its diff:
```python
import functools

import jax
import jax.numpy as jnp
from jax import lax
from jax.experimental import pallas as pl
from jax.experimental.pallas import tpu as pltpu
from jax.sharding import PartitionSpec as P

time_step = 0.2
scale = time_step / 60.0
ROWS = 8
RHS_COST, SUMS_COST, JOIN_COST, EDGE_COST, FACE_COST = 60, 200, 20, 20000, 20000
F32 = jnp.float32
VMEM = pl.BlockSpec(memory_space=pltpu.VMEM)
ANY = pl.BlockSpec(memory_space=pl.ANY)
HBM = pl.BlockSpec(memory_space=pltpu.HBM)


def pairing(count, odd):
    pairs = []
    for low in range(1 if odd else 0, count, 2):
        high = (low + 1) % count
        pairs += [(low, high), (high, low)]
    return pairs


def partner_by(count, step):
    return [(i, i ^ step) for i in range(count)]


def rows_of(block):
    return block.reshape(block.shape[0] * block.shape[1], block.shape[2])


def shifted_z(own, low, high, k):
    nz = own.shape[-1]
    if nz % 128 == 0:
        lane = lax.broadcasted_iota(jnp.int32, own.shape, own.ndim - 1)
        if k > 0:
            return pltpu.roll(jnp.where(lane < k, high, own), nz - k, own.ndim - 1)
        return pltpu.roll(jnp.where(lane >= nz + k, low, own), -k, own.ndim - 1)
    if k > 0:
        return jnp.concatenate([own[..., k:], high[..., :k]], -1)
    return jnp.concatenate([low[..., nz + k :], own[..., : nz + k]], -1)


def sixth(take):
    return 45.0 * (take(1) - take(-1)) - 9.0 * (take(2) - take(-2)) + (take(3) - take(-3))


def sixth_z(own, low, high):
    return sixth(lambda k: shifted_z(own, low, high, k))


def join(left, right):
    inv_delta = 1.0 / (right[5] + right[2] + left[3])
    jump = (right[0] - left[1]) * inv_delta
    from_in = left[4] * inv_delta
    from_out = right[4] * inv_delta
    group = (
        left[0] + left[4] * jump,
        right[1] - right[4] * jump,
        left[2] - left[4] * from_in,
        right[3] - right[4] * from_out,
        left[4] * from_out,
        left[5],
        right[6],
    )
    return group, (jump, from_in, from_out)


def pick(cond, yes, no):
    return tuple(jnp.where(cond, a, b) for a, b in zip(yes, no))


def join_own(is_left, own, other, forms):
    left = pick(is_left, own, other)
    right = pick(is_left, other, own)
    group, (jump, from_in, from_out) = join(left, right)
    new = []
    for c0, c1, c2 in forms:
        through = jnp.where(is_left, c2, c1)
        new.append(
            (
                c0 + through * jump,
                jnp.where(is_left, c1, 0.0) + through * from_in,
                jnp.where(is_left, 0.0, c2) + through * from_out,
            )
        )
    return group, new


def closing(is_left, group, forms):
    first, last, alpha, beta, m, inv_first, inv_last = group
    kappa = 1.0 / jnp.where(is_left, inv_first + alpha, inv_last + beta)
    outer = jnp.where(is_left, first, -last) * kappa
    gain = kappa * m
    facing = jnp.where(is_left, last - m * outer, first + m * outer)
    resist = jnp.where(is_left, beta, alpha + inv_first) - m * gain
    out = []
    for c0, c1, c2 in forms:
        far = jnp.where(is_left, c1, c2)
        near = jnp.where(is_left, c2, c1)
        out.append((c0 + far * outer, far * gain + near))
    return facing, resist, out


def put_scalars(ref, block, values):
    for row, value in enumerate(values):
        ref[block, row : row + 1] = value


def get_scalars(ref, block, count):
    return [ref[block, row : row + 1] for row in range(count)]


def store_group(ref, group, tiles):
    for f in range(3):
        ref[f * tiles : (f + 1) * tiles] = group[0][f]
        ref[(3 + f) * tiles : (4 + f) * tiles] = group[1][f]
    put_scalars(ref, 6 * tiles, group[2:])


def load_group(ref, tiles):
    shape = (3, tiles) + ref.shape[1:]
    first = ref[: 3 * tiles].reshape(shape)
    last = ref[3 * tiles : 6 * tiles].reshape(shape)
    return (first, last, *get_scalars(ref, 6 * tiles, 5))


def store_closing(msg_ref, own_ref, facing, resist, out, tiles):
    own_ref[6 * tiles + 1 : 9 * tiles + 1] = facing.reshape((3 * tiles,) + facing.shape[2:])
    put_scalars(own_ref, 9 * tiles + 1, [resist])
    for f in range(3):
        msg_ref[f * tiles : (f + 1) * tiles] = facing[f]
        own_ref[f * tiles : (f + 1) * tiles] = out[0][0][f]
        own_ref[(3 + f) * tiles : (4 + f) * tiles] = out[1][0][f]
    put_scalars(msg_ref, 3 * tiles, [resist])
    put_scalars(own_ref, 6 * tiles, [out[0][1], out[1][1]])


def store_forms(ref, forms, tiles):
    for f in range(3):
        ref[f * tiles : (f + 1) * tiles] = forms[0][0][f]
        ref[(3 + f) * tiles : (4 + f) * tiles] = forms[1][0][f]
    put_scalars(ref, 6 * tiles, [*forms[0][1:], *forms[1][1:]])


def load_forms(ref, tiles):
    shape = (3, tiles) + ref.shape[1:]
    scalars = get_scalars(ref, 6 * tiles, 4)
    return [
        (ref[: 3 * tiles].reshape(shape), scalars[0], scalars[1]),
        (ref[3 * tiles : 6 * tiles].reshape(shape), scalars[2], scalars[3]),
    ]


def sums_at(nx, ny, side, k):
    start = 3 * nx * ny + (6 * side + k) * ny
    return slice(start, start + ny)


def pick_edges(ref_a, ref_b, take):
    odd = lax.rem(lax.axis_index("gy"), 2)
    for ref, high in ((ref_a, 1 - odd), (ref_b, odd)):
        take(ref, high)


def first_kernel(
    chunks, faces, density, momentum,
    rho_v, mom_v, flux_y, flux_z, small_b, small_a, edge_a, edge_b, coefs, scalars,
    face_s, sems,
):
    nx = faces.shape[0]
    nz = density.shape[1]
    ny = density.shape[0] // nx
    tiles = ny // ROWS
    face_copy = pltpu.make_async_copy(faces, face_s, sems.at[0])
    face_copy.start()
    step = nx * ny // chunks
    copies = []
    for c in range(chunks):
        at = pl.ds(c * step, step)
        copies.append(
            (
                pltpu.make_async_copy(density.at[at], rho_v.at[at], sems.at[1 + 2 * c]),
                pltpu.make_async_copy(momentum.at[:, at], mom_v.at[:, at], sems.at[2 + 2 * c]),
            )
        )
        for copy in copies[-1]:
            copy.start()
    tile = (ROWS, nz)
    pitch = ny + ROWS
    for line in range(3 * nx + 1):
        flux_y[line * pitch : line * pitch + ROWS] = jnp.zeros(tile, F32)
    face_copy.wait()
    inv = [1.0 / jnp.full(tile, face_s[i], F32) for i in range(nx)]
    phi = [jnp.ones(tile, F32)]
    flux = phi[0]
    for i in range(1, nx):
        phi.append(phi[-1] + flux * inv[i])
        flux = flux + phi[-1]
    m = 1.0 / flux
    psi = [jnp.ones(tile, F32)]
    flux = psi[0]
    for i in range(nx - 1, 0, -1):
        psi.append(psi[-1] + flux * inv[i])
        flux = flux + psi[-1]
    psi = psi[::-1]
    for i in range(nx):
        coefs[i] = phi[i]
        coefs[nx + i] = psi[i] * m
    scalars[0:1] = (psi[0] * m)[0:1]
    scalars[1:2] = (phi[nx - 1] * m)[0:1]
    scalars[2:3] = m[0:1]
    scalars[3:4] = inv[0][0:1]
    scalars[4:5] = inv[nx - 1][0:1]
    scalars[5:8] = jnp.zeros((3, nz), F32)
    total = [[None] * 6, [None] * 6]
    for x in range(nx):
        if x % (nx // chunks) == 0:
            for copy in copies[x // (nx // chunks)]:
                copy.wait()
        at = slice(x * ny, (x + 1) * ny)
        rho, m0, m1 = [b.reshape(tiles, ROWS, nz) for b in (rho_v[at], mom_v[0, at], mom_v[1, at])]
        inv_rho = 1.0 / rho
        v0, v1 = m0 * inv_rho, m1 * inv_rho
        values = (rho, m0, m1, m0 * v0, m0 * v1, m1 * v1)
        for side, weight in enumerate((coefs[nx + x], coefs[x])):
            for k, value in enumerate(values):
                term = weight * value
                total[side][k] = term if x == 0 else total[side][k] + term
        for f in range(3):
            start = (f * nx + x) * pitch + ROWS
            flux_y[start : start + ny] = values[(1, 3, 4)[f]].reshape(ny, nz)
            flux_z[f * nx * ny + x * ny : f * nx * ny + (x + 1) * ny] = values[(2, 4, 5)[f]].reshape(ny, nz)
    for side in range(2):
        for k in range(6):
            flux_z[sums_at(nx, ny, side, k)] = total[side][k].reshape(ny, nz)

    def take_small(ref, high):
        for side in range(2):
            for f, k in enumerate((1, 3, 4)):
                start = sums_at(nx, ny, side, k).start + high * (ny - ROWS)
                ref[3 * side + f] = flux_z[pl.ds(pl.multiple_of(start, ROWS), ROWS)]

    def take_edge(ref, high):
        sign = jnp.where(high == 1, scale, -scale)
        rows = [pl.ds(high * (ny - 1) + (1 - 2 * high) * k, nx, stride=ny) for k in range(3)]
        m0, m1, v0 = [], [], []
        for at in rows:
            m0.append(mom_v[0, at])
            m1.append(mom_v[1, at])
            v0.append(m0[-1] / rho_v[at] * sign)
        for f in range(3):
            n1, n2, n3 = [(m0[k] * sign, m0[k] * v0[k], m1[k] * v0[k])[f] for k in range(3)]
            ref[3 * f] = 45.0 * n1 - 9.0 * n2 + n3
            ref[3 * f + 1] = n2 - 9.0 * n1
            ref[3 * f + 2] = n1

    pick_edges(small_a, small_b, take_small)
    pick_edges(edge_a, edge_b, take_edge)


def halos_y(is_odd, from_a, from_b):
    low = jnp.where(is_odd, from_a, from_b)
    high = jnp.where(is_odd, from_b, from_a)
    return low, high


def second_kernel(stages, nx, ny, small_a, small_b, sums, sums_low, sums_high, scalars, *refs):
    nz = sums.shape[1]
    tiles = ny // ROWS
    pad = refs[-1]
    is_odd = lax.rem(lax.axis_index("gy"), 2) == 1
    low, high = halos_y(is_odd, small_a[...], small_b[...])
    alpha, beta, m, inv_first, inv_last = [scalars[i : i + 1] for i in range(5)]
    values = []
    for side in range(2):
        for f, (state, along_y, along_z) in enumerate(((0, 1, 2), (1, 3, 4), (2, 4, 5))):
            k = 3 * side + f
            pad[k, 0:ROWS] = low[k]
            pad[k, ROWS : ROWS + ny] = sums[sums_at(nx, ny, side, along_y)]
            pad[k, ROWS + ny : 2 * ROWS + ny] = high[k]
            dy = sixth(lambda s: pad[k, ROWS + s : ROWS + s + ny])
            dz = sixth_z(*[r[sums_at(nx, ny, side, along_z)] for r in (sums, sums_low, sums_high)])
            value = sums[sums_at(nx, ny, side, state)] - scale * (dy + dz)
            values.append(value.reshape(tiles, ROWS, nz))
    first = jnp.stack(values[:3])
    last = jnp.stack(values[3:]) * m
    group = (first, last, alpha, beta, m, inv_first, inv_last)
    if stages == 1:
        is_left = lax.rem(lax.axis_index("gx"), 2) == 0
        zero = jnp.zeros_like(first)
        one = jnp.ones_like(alpha)
        forms = [(zero, one, 0.0 * one), (zero, 0.0 * one, one)]
        facing, resist, out = closing(is_left, group, forms)
        store_closing(refs[0], refs[1], facing, resist, out, tiles)
    else:
        store_group(refs[0], group, tiles)


def join_kernel(stage, stages, tiles, *refs):
    refs = refs[:2] + refs[3:]
    if stage == 0:
        mine, other, msg, own = refs
        shape = (3, tiles) + mine.shape[1:]
        zero, one = jnp.zeros(shape, F32), jnp.ones((1, shape[-1]), F32)
        forms = [(zero, one, 0.0 * one), (zero, 0.0 * one, one)]
    else:
        mine, other, forms_ref, msg, own = refs
        forms = load_forms(forms_ref, tiles)
    at = lax.axis_index("gx")
    is_left = lax.rem(lax.div(at, 1 << stage), 2) == 0
    group, forms = join_own(is_left, load_group(mine, tiles), load_group(other, tiles), forms)
    if stage + 2 == stages:
        is_left = lax.rem(lax.div(at, 2 << stage), 2) == 0
        facing, resist, out = closing(is_left, group, forms)
        store_closing(msg, own, facing, resist, out, tiles)
    else:
        store_group(msg, group, tiles)
        store_forms(own, forms, tiles)


def rhs_kernel(nx, density, momentum, flux_y, flux_z, flux_z_low, flux_z_high, rhs):
    ny = density.shape[0] // nx
    pitch = ny + ROWS
    for f in range(3):
        for x in range(nx):
            at = (f * nx + x) * pitch + ROWS
            dy = sixth(lambda s: flux_y[at + s : at + s + ny])
            cells = slice(x * ny, (x + 1) * ny)
            lines = slice((f * nx + x) * ny, (f * nx + x + 1) * ny)
            dz = sixth_z(*[r[lines] for r in (flux_z, flux_z_low, flux_z_high)])
            state = density[cells] if f == 0 else momentum[f - 1, cells]
            rhs[f, cells] = state - scale * (dy + dz)


def add_edge(nx, rhs, edge, high):
    ny = rhs.shape[1] // nx
    for f in range(3):
        for k in range(3):
            at = pl.ds(high * (ny - 1) + (1 - 2 * high) * k, nx, stride=ny)
            rhs[f, at] = rhs[f, at] + edge[3 * f + k]


def edge_kernel(nx, rhs_in, edge_b, rhs):
    add_edge(nx, rhs, edge_b, lax.rem(lax.axis_index("gy"), 2))


def sums_kernel(nx, rhs_in, edge_a, coefs, rhs, ahead, behind):
    ny, nz = rhs.shape[1] // nx, rhs.shape[2]
    shape = (ny // ROWS, ROWS, nz)
    add_edge(nx, rhs, edge_a, 1 - lax.rem(lax.axis_index("gy"), 2))
    for f in range(3):
        total = None
        for x in range(nx):
            r = rhs[f, x * ny : (x + 1) * ny].reshape(shape)
            total = coefs[x] * r if x == 0 else total + coefs[x] * r
            ahead[f, x] = total
        total = jnp.zeros(shape, F32)
        for x in range(nx - 1, -1, -1):
            behind[f, x] = total
            if x > 0:
                r = rhs[f, x * ny : (x + 1) * ny].reshape(shape)
                total = total + coefs[nx + x] * r


def last_kernel(stages, parts, ahead, behind, coefs, scalars, other, own, updated, out_v, sems):
    _, nx, tiles, _, nz = ahead.shape
    is_left = lax.rem(lax.div(lax.axis_index("gx"), 1 << (stages - 1)), 2) == 0
    sign = jnp.where(is_left, 1.0, -1.0)
    inv = sign / (own[9 * tiles + 1, 0:1] + other[3 * tiles, 0:1])
    m = scalars[2:3]
    copies = []
    for f in range(3):
        at = slice(f * tiles, (f + 1) * tiles)
        mid = (other[at] - own[(6 + f) * tiles + 1 : (7 + f) * tiles + 1]) * inv
        jin = own[at] + own[6 * tiles, 0:1] * mid
        jout = m * (own[(3 + f) * tiles : (4 + f) * tiles] + own[6 * tiles, 1:2] * mid)
        for x in range(nx):
            out_v[f, x] = coefs[nx + x] * (ahead[f, x] - jin) + coefs[x] * (behind[f, x] + jout)
            if (x + 1) % (nx // parts) == 0:
                part = pl.ds(x + 1 - nx // parts, nx // parts)
                copy = pltpu.make_async_copy(out_v.at[f, part], updated.at[f, part], sems.at[len(copies)])
                copy.start()
                copies.append(copy)
    for copy in copies:
        copy.wait()


def params(limit=48):
    return pltpu.CompilerParams(vmem_limit_bytes=limit * 1024 * 1024)


def swap(block, axis, pairs, crossed):
    if not crossed:
        return lax.ppermute(block, axis, pairs)
    both = [(2 * a + c, 2 * b + 1 - c) for a, b in pairs for c in range(2)]
    return lax.ppermute(block, (axis, "gz"), both)


def swap_edges(block_a, block_b, crossed=False):
    count = lax.axis_size("gy")
    return (
        swap(block_a, "gy", pairing(count, False), crossed),
        swap(block_b, "gy", pairing(count, True), crossed),
    )


def swap_whole(block, axis):
    count = lax.axis_size(axis)
    if count == 2:
        got = lax.ppermute(block, axis, pairing(2, False))
        return got, got
    ring = [(i, (i + 1) % count) for i in range(count)]
    return lax.ppermute(block, axis, ring), lax.ppermute(block, axis, [(b, a) for a, b in ring])


def on_device(density, momentum, lower_face):
    nx, ny, nz = density.shape
    tiles = ny // ROWS
    cells = nx * ny
    chunks, parts = (4 if nx % 4 == 0 else 1), (2 if nx % 2 == 0 else 1)
    devices = lax.axis_size("gx")
    stages = (devices - 1).bit_length()
    crossed = lax.axis_size("gz") == 2
    full = lambda *lead: jax.ShapeDtypeStruct(lead + (ROWS, nz), F32)
    vec = lambda *lead: jax.ShapeDtypeStruct(lead + (nz,), F32)
    cost = lambda n: pl.CostEstimate(flops=n * cells * nz, bytes_accessed=n * cells * nz, transcendentals=0)
    inputs = (lower_face, density.reshape(cells, nz), momentum.reshape(2, cells, nz))
    inputs = [pltpu.with_memory_space_constraint(x, pltpu.HBM) for x in inputs]
    density, momentum, flux_y, flux_z, small_b, small_a, edge_a, edge_b, coefs, scalars = pl.pallas_call(
        functools.partial(first_kernel, chunks),
        in_specs=[HBM] * 3,
        out_specs=[VMEM] * 10,
        out_shape=[
            vec(cells),
            vec(2, cells),
            vec(3 * nx * (ny + ROWS) + ROWS),
            vec(3 * cells + 12 * ny),
            full(6),
            full(6),
            vec(9, nx),
            vec(9, nx),
            full(2 * nx),
            full(),
        ],
        scratch_shapes=[pltpu.SMEM((nx,), F32), pltpu.SemaphoreType.DMA((1 + 2 * chunks,))],
        compiler_params=params(),
        name="load",
    )(*inputs)
    got_a, got_b = swap_edges(small_a, small_b, crossed)
    far_a, far_b = swap_edges(edge_a, edge_b)
    z_low, z_high = swap_whole(flux_z, "gz")
    rhs = pl.pallas_call(
        functools.partial(rhs_kernel, nx),
        in_specs=[VMEM] * 6,
        out_specs=VMEM,
        out_shape=vec(3, cells),
        compiler_params=params(),
        cost_estimate=cost(RHS_COST),
        name="rhs",
    )(density, momentum, flux_y, flux_z, z_low, z_high)
    handled = (z_low, flux_z, flux_z) if crossed else (flux_z, z_low, z_high)
    msg_shapes = [full(6 * tiles + 1), full(3 * tiles + 1)]
    own_shapes = [full(6 * tiles + 1), full(9 * tiles + 2)]
    msg, *own = pl.pallas_call(
        functools.partial(second_kernel, stages, nx, ny),
        in_specs=[VMEM] * 6,
        out_specs=[VMEM] * (1 + (stages == 1)),
        out_shape=[msg_shapes[1], own_shapes[1]] if stages == 1 else msg_shapes[:1],
        scratch_shapes=[pltpu.VMEM((6, ny + 2 * ROWS, nz), F32)],
        compiler_params=params(),
        cost_estimate=cost(FACE_COST),
        name="interface",
    )(got_a, got_b, *handled, scalars)
    other = swap(msg, "gx", partner_by(devices, 1), crossed)
    if crossed:
        if stages == 1:
            own = [swap_whole(own[0], "gz")[0]]
        else:
            msg, _ = swap_whole(msg, "gz")
    for stage in range(stages - 1):
        closing_next = stage + 2 == stages
        msg, *own = pl.pallas_call(
            functools.partial(join_kernel, stage, stages, tiles),
            in_specs=[VMEM, VMEM, ANY] + [VMEM] * len(own),
            out_specs=[VMEM] * 2,
            out_shape=[msg_shapes[closing_next], own_shapes[closing_next]],
            compiler_params=params(),
            cost_estimate=cost(JOIN_COST),
            name="join",
        )(msg, other, rhs, *own)
        other = lax.ppermute(msg, "gx", partner_by(devices, 2 << stage))
    own = own[0]
    rhs = pl.pallas_call(
        functools.partial(edge_kernel, nx),
        in_specs=[VMEM] * 2,
        out_specs=VMEM,
        out_shape=vec(3, cells),
        input_output_aliases={0: 0},
        compiler_params=params(),
        cost_estimate=cost(EDGE_COST),
        name="edge",
    )(rhs, far_b)
    _, ahead, behind = pl.pallas_call(
        functools.partial(sums_kernel, nx),
        in_specs=[VMEM] * 3,
        out_specs=[VMEM] * 3,
        out_shape=[vec(3, cells)] + [full(3, nx, tiles)] * 2,
        input_output_aliases={0: 0},
        compiler_params=params(),
        cost_estimate=cost(SUMS_COST),
        name="sums",
    )(rhs, far_a, coefs)
    updated = pl.pallas_call(
        functools.partial(last_kernel, stages, parts),
        in_specs=[VMEM] * 6,
        out_specs=HBM,
        out_shape=full(3, nx, tiles),
        scratch_shapes=[
            pltpu.VMEM((3, nx, tiles, ROWS, nz), F32),
            pltpu.SemaphoreType.DMA((3 * parts,)),
        ],
        compiler_params=params(),
        name="solve",
    )(ahead, behind, coefs, scalars, other, own)
    return updated.reshape(3, nx, ny, nz)


def solution(mesh):
    placed = (P("gx", "gy", "gz"), P(None, "gx", "gy", "gz"), P("gx"))
    return jax.shard_map(
        on_device, mesh=mesh, in_specs=placed, out_specs=P(None, "gx", "gy", "gz"), check_vma=False
    )
```

time: 20 us -> 18.9 us (0.945)
  waiting for transfers between devices: 4.9 us -> 3.5 us
  starting transfers between devices: 10.4 us -> 10.8 us
    ppermute x6 -> x7, waiting for transfers between devices: 4.5 us -> 2.62 us  [the longest x3 1.73 us: swap(): return lax.ppermute(block, (axis, 'gz'), both)]
    ppermute x1, waiting for transfers between devices: 0.41 us -> 0.89 us  [on_device(): other = lax.ppermute(msg, 'gx', partner_by(devices, 2 << stage))]
    ppermute x6 -> x7, starting transfers between devices: 7.73 us -> 8.17 us  [the longest x3 5.14 us: swap(): return lax.ppermute(block, (axis, 'gz'), both)]
    pallas_call x5 -> x6, Pallas kernels: 4.41 us -> 4.35 us  [the longest x1 1.54 us: on_device(): pl.pallas_call(functools.partial(first_kernel, chunks), in_specs=[HBM] *...]
  transfers between devices with their start and end apart: 7 -> 8, of which waited for: 3 -> 4; matrix products, arithmetic and copies ran while one was open for 0% -> 0% of each run, Pallas kernels for 10% -> 10%
where the time goes in v3:
time: 18.9 us; the launch traced here: 18.8 us
  starting transfers between devices  10.8 us (57%)
  Pallas kernels  4.39 us (23%)
  waiting for transfers between devices  3.5 us (19%)
    ppermute x3, starting transfers between devices, swap(): return lax.ppermute(block, (axis, 'gz'), both)  5.14 us
    ppermute x1, starting transfers between devices, on_device(): other = lax.ppermute(msg, 'gx', partner_by(devices, 2 << stage))  2.65 us
    ppermute x2, starting transfers between devices, swap(): return lax.ppermute(block, axis, pairs)  2.12 us
    ppermute x3, waiting for transfers between devices, swap(): return lax.ppermute(block, (axis, 'gz'), both)  1.73 us
    pallas_call x1, Pallas kernels, on_device(): pl.pallas_call(functools.partial(first_kernel, chunks), in_specs=[HBM] *...  1.54 us
    pallas_call x1, Pallas kernels, on_device(): pl.pallas_call(functools.partial(rhs_kernel, nx), in_specs=[VMEM] * 6, ou...  1.3 us
    pallas_call x1, Pallas kernels, on_device(): pl.pallas_call(functools.partial(last_kernel, stages, parts), in_specs=[V...  0.96 us
    ppermute x2, starting transfers between devices, swap_whole(): got = lax.ppermute(block, axis, pairing(2, False))  0.91 us
  transfers between devices with their start and end apart: 8, of which 4 were waited for; matrix products, arithmetic and copies ran while one was open for 0% of the time, Pallas kernels for 10%

profile of v3, /device:TPU:0, one launch (start us, length us, event | category | flops | bytes accessed | tf_op | source)
XLA Modules:
  0.0 18.8 jit_solution(2848389799876438469)
XLA Ops:
  0.0 1.5 %load.1 = (f32[512,128]{1,0:T(8,128)S(1)}, f32[2,512,128]{2,1,0:T(8,128)S(1)}, f32[2312,128]{1,0:T(8,128)S(1)}, f32[1728,128]{1,0:T(8,128)S(1)}, f32[6,8,128]{2,...) custom-call(f32[32]{0:T(128)} %faces.1, ...), custom_call_target="tpu_custom_call" | custom-call | tf_op jit(solution)/shard_map/load/pallas_call | solution.py:434
  1.6 0.5 %collective-permute-start = (f32[1728,128]{1,0:T(8,128)S(1)}, f32[1728,128]{1,0:T(8,128)S(1)}, u32[]{:S(2)}, u32[]{:S(2)}) collective-permute-start(f32[1728,128]{1,0:T(8,128)S(1)} %get-tuple-element.22.flux_z.sums_low.sums_high), channel_id=1, source_target_pairs={{0,1},{1,0},{2,3},{3,2},{4,5},{5,4},{6,7},{7,6},{8,9},{9,8},{10,11... | collective-permute-start | bytes 2654216 | tf_op jit(solution)/shard_map/ppermute | solution.py:415
  2.1 2.6 %collective-permute-start.3 = (f32[6,8,128]{2,1,0:T(8,128)S(1)}, f32[6,8,128]{2,1,0:T(8,128)S(1)}, u32[]{:S(2)}, u32[]{:S(2)}) collective-permute-start(f32[6,8,128]{2,1,0:T(8,128)S(1)} %get-tuple-element.29), channel_id=1, source_target_pairs={{0,3},{1,2},{2,1},{3,0},{4,7},{5,6},{6,5},{7,4},{8,11},{9,10},{10,... | collective-permute-start | bytes 73736 | tf_op jit(solution)/shard_map/ppermute | solution.py:401
  4.7 1.2 %collective-permute-start.4 = (f32[6,8,128]{2,1,0:T(8,128)S(1)}, f32[6,8,128]{2,1,0:T(8,128)S(1)}, u32[]{:S(2)}, u32[]{:S(2)}) collective-permute-start(f32[6,8,128]{2,1,0:T(8,128)S(1)} %get-tuple-element.30), channel_id=1, source_target_pairs={{2,5},{3,4},{4,3},{5,2},{6,1},{7,0},{0,7},{1,6},{10,13},{11,12},{1... | collective-permute-start | bytes 73736 | tf_op jit(solution)/shard_map/ppermute | solution.py:401
  5.8 1.4 %collective-permute-start.1 = (f32[9,32,128]{2,1,0:T(8,128)S(1)}, f32[9,32,128]{2,1,0:T(8,128)S(1)}, u32[]{:S(2)}, u32[]{:S(2)}) collective-permute-start(f32[9,32,128]{2,1,0:T(8,128)S(1)} %get-tuple-element.23), channel_id=1, source_target_pairs={{2,4},{4,2},{6,0},{0,6},{3,5},{5,3},{7,1},{1,7},{10,12},{12,10},{1... | collective-permute-start | bytes 442376 | tf_op jit(solution)/shard_map/ppermute | solution.py:399
  7.3 0.0 collective-permute-done.3.small_a
  7.3 1.6 %collective-permute-done.4.small_b = f32[6,8,128]{2,1,0:T(8,128)S(1)} collective-permute-done((f32[6,8,128]{2,1,0:T(8,128)S(1)}, f32[6,8,128]{2,1,0:T(8,128)S(1)}, u32[]{:S(2)}, u32[]{:S(2)}) %collective-permute-start.4) | collective-permute-done | bytes 24608 | tf_op jit(solution)/shard_map/ppermute | solution.py:401
  8.9 0.0 collective-permute-done.flux_z_low.flux_z_high.sums
  8.9 0.1 interface.1
  9.0 1.4 %collective-permute-start.6 = (f32[13,8,128]{2,1,0:T(8,128)S(1)}, f32[13,8,128]{2,1,0:T(8,128)S(1)}, u32[]{:S(2)}, u32[]{:S(2)}) collective-permute-start(f32[13,8,128]{2,1,0:T(8,128)S(1)} %interface.1), channel_id=1, source_target_pairs={{0,9},{1,8},{8,1},{9,0},{16,25},{17,24},{24,17},{25,16},{2,11},{3,... | collective-permute-start | bytes 159752 | tf_op jit(solution)/shard_map/ppermute | solution.py:401
  10.4 0.4 %collective-permute-start.5 = (f32[13,8,128]{2,1,0:T(8,128)S(1)}, f32[13,8,128]{2,1,0:T(8,128)S(1)}, u32[]{:S(2)}, u32[]{:S(2)}) collective-permute-start(f32[13,8,128]{2,1,0:T(8,128)S(1)} %interface.1), channel_id=1, source_target_pairs={{0,1},{1,0},{2,3},{3,2},{4,5},{5,4},{6,7},{7,6},{8,9},{9,8},{10,11... | collective-permute-start | bytes 159752 | tf_op jit(solution)/shard_map/ppermute | solution.py:415
  10.8 0.7 %collective-permute-start.2 = (f32[9,32,128]{2,1,0:T(8,128)S(1)}, f32[9,32,128]{2,1,0:T(8,128)S(1)}, u32[]{:S(2)}, u32[]{:S(2)}) collective-permute-start(f32[9,32,128]{2,1,0:T(8,128)S(1)} %get-tuple-element.24), channel_id=1, source_target_pairs={{0,2},{2,0},{4,6},{6,4},{1,3},{3,1},{5,7},{7,5},{8,10},{10,8},{12,... | collective-permute-start | bytes 442376 | tf_op jit(solution)/shard_map/ppermute | solution.py:399
  11.5 1.3 %rhs.1.rhs_in.refs_2_ = f32[3,512,128]{2,1,0:T(8,128)S(1)} custom-call(f32[512,128]{1,0:T(8,128)S(1)} %get-tuple-element.19.density, f32[2,512,128]{2,1,0:T(8,128)S(1)} %get-tuple-element.20.momentum, f32[2312,128]{1,0:T(8,128)S(1)} %get-tuple-element.21.flux_y, f32[1728,128]{1,0:T(8,128)S(1)} %get-tuple-element.22.flux_z.sums_low.sums_high, ...), custom_call_target="tpu_custom_call" | custom-call | flops 3932160 | bytes 3932160 | tf_op jit(solution)/shard_map/rhs/pallas_call | solution.py:457
  12.8 0.2 collective-permute-done.6.refs_1_
  12.9 0.0 collective-permute-done.5.refs_0_
  13.0 2.7 %collective-permute-start.7 = (f32[7,8,128]{2,1,0:T(8,128)S(1)}, f32[7,8,128]{2,1,0:T(8,128)S(1)}, u32[]{:S(2)}, u32[]{:S(2)}) collective-permute-start(f32[7,8,128]{2,1,0:T(8,128)S(1)} %get-tuple-element.31), channel_id=1, source_target_pairs={{0,16},{8,24},{16,0},{24,8},{1,17},{9,25},{17,1},{25,9},{2,18},{10... | collective-permute-start | bytes 86024 | tf_op jit(solution)/shard_map/ppermute | solution.py:496
  15.6 0.0 collective-permute-done.1.edge_b
  15.6 0.1 edge.1.rhs_in
  15.8 0.9 %collective-permute-done.2.edge_a = f32[9,32,128]{2,1,0:T(8,128)S(1)} collective-permute-done((f32[9,32,128]{2,1,0:T(8,128)S(1)}, f32[9,32,128]{2,1,0:T(8,128)S(1)}, u32[]{:S(2)}, u32[]{:S(2)}) %collective-permute-start.2) | collective-permute-done | bytes 147488 | tf_op jit(solution)/shard_map/ppermute | solution.py:399
  16.6 0.3 %sums.1 = (f32[3,512,128]{2,1,0:T(8,128)S(1)}, f32[3,32,2,8,128]{4,3,2,1,0:T(8,128)S(1)}, f32[3,32,2,8,128]{4,3,2,1,0:T(8,128)S(1)}) custom-call(f32[3,512,128]{2,1,0:T(8,128)S(1)} %edge.1.rhs_in, f32[9,32,128]{2,1,0:T(8,128)S(1)} %collective-permute-done.2.edge_a, f32[64,8,128]{2,1,0:T(8,128)S(1)} %get-tuple-element.25.coefs), custom_call_target="tpu_custom_call", output_to_operand_aliasing={{0}: (0, {})} | custom-call | flops 13107200 | bytes 13107200 | tf_op jit(solution)/shard_map/sums/pallas_call | solution.py:508
  16.9 0.9 %collective-permute-done.7.other = f32[7,8,128]{2,1,0:T(8,128)S(1)} collective-permute-done((f32[7,8,128]{2,1,0:T(8,128)S(1)}, f32[7,8,128]{2,1,0:T(8,128)S(1)}, u32[]{:S(2)}, u32[]{:S(2)}) %collective-permute-start.7) | collective-permute-done | bytes 28704 | tf_op jit(solution)/shard_map/ppermute | solution.py:496
  17.8 1.0 %solve.1 = f32[3,32,2,8,128]{4,3,2,1,0:T(8,128)} custom-call(f32[3,32,2,8,128]{4,3,2,1,0:T(8,128)S(1)} %get-tuple-element.26.ahead, f32[3,32,2,8,128]{4,3,2,1,0:T(8,128)S(1)} %get-tuple-element.27.behind, f32[64,8,128]{2,1,0:T(8,128)S(1)} %get-tuple-element.25.coefs, f32[8,128]{1,0:T(8,128)S(1)} %get-tuple-element.28.scalars, ...), custom_call_target="tpu_custom_call" | custom-call | tf_op jit(solution)/shard_map/solve/pallas_call | solution.py:518
  (1 shorter events, 0.0 us)
Async XLA Ops:
  1.6 7.3 %collective-permute-start = (f32[1728,128]{1,0:T(8,128)S(1)}, f32[1728,128]{1,0:T(8,128)S(1)}, u32[]{:S(2)}, u32[]{:S(2)}) collective-permute-start(f32[1728,128]{1,0:T(8,128)S(1)} %get-tuple-element.22.flux_z.sums_low.sums_high), channel_id=1, source_target_pairs={{0,1},{1,0},{2,3},{3,2},{4,5},{5,4},{6,7},{7,6},{8,9},{9,8},{10,11... | collective-permute-start | bytes 2654216 | tf_op jit(solution)/shard_map/ppermute | solution.py:415
  2.1 5.2 %collective-permute-start.3 = (f32[6,8,128]{2,1,0:T(8,128)S(1)}, f32[6,8,128]{2,1,0:T(8,128)S(1)}, u32[]{:S(2)}, u32[]{:S(2)}) collective-permute-start(f32[6,8,128]{2,1,0:T(8,128)S(1)} %get-tuple-element.29), channel_id=1, source_target_pairs={{0,3},{1,2},{2,1},{3,0},{4,7},{5,6},{6,5},{7,4},{8,11},{9,10},{10,... | collective-permute-start | bytes 73736 | tf_op jit(solution)/shard_map/ppermute | solution.py:401
  4.7 4.2 %collective-permute-start.4 = (f32[6,8,128]{2,1,0:T(8,128)S(1)}, f32[6,8,128]{2,1,0:T(8,128)S(1)}, u32[]{:S(2)}, u32[]{:S(2)}) collective-permute-start(f32[6,8,128]{2,1,0:T(8,128)S(1)} %get-tuple-element.30), channel_id=1, source_target_pairs={{2,5},{3,4},{4,3},{5,2},{6,1},{7,0},{0,7},{1,6},{10,13},{11,12},{1... | collective-permute-start | bytes 73736 | tf_op jit(solution)/shard_map/ppermute | solution.py:401
  5.8 9.8 %collective-permute-start.1 = (f32[9,32,128]{2,1,0:T(8,128)S(1)}, f32[9,32,128]{2,1,0:T(8,128)S(1)}, u32[]{:S(2)}, u32[]{:S(2)}) collective-permute-start(f32[9,32,128]{2,1,0:T(8,128)S(1)} %get-tuple-element.23), channel_id=1, source_target_pairs={{2,4},{4,2},{6,0},{0,6},{3,5},{5,3},{7,1},{1,7},{10,12},{12,10},{1... | collective-permute-start | bytes 442376 | tf_op jit(solution)/shard_map/ppermute | solution.py:399
  9.0 3.9 %collective-permute-start.6 = (f32[13,8,128]{2,1,0:T(8,128)S(1)}, f32[13,8,128]{2,1,0:T(8,128)S(1)}, u32[]{:S(2)}, u32[]{:S(2)}) collective-permute-start(f32[13,8,128]{2,1,0:T(8,128)S(1)} %interface.1), channel_id=1, source_target_pairs={{0,9},{1,8},{8,1},{9,0},{16,25},{17,24},{24,17},{25,16},{2,11},{3,... | collective-permute-start | bytes 159752 | tf_op jit(solution)/shard_map/ppermute | solution.py:401
  10.4 2.5 %collective-permute-start.5 = (f32[13,8,128]{2,1,0:T(8,128)S(1)}, f32[13,8,128]{2,1,0:T(8,128)S(1)}, u32[]{:S(2)}, u32[]{:S(2)}) collective-permute-start(f32[13,8,128]{2,1,0:T(8,128)S(1)} %interface.1), channel_id=1, source_target_pairs={{0,1},{1,0},{2,3},{3,2},{4,5},{5,4},{6,7},{7,6},{8,9},{9,8},{10,11... | collective-permute-start | bytes 159752 | tf_op jit(solution)/shard_map/ppermute | solution.py:415
  10.8 5.9 %collective-permute-start.2 = (f32[9,32,128]{2,1,0:T(8,128)S(1)}, f32[9,32,128]{2,1,0:T(8,128)S(1)}, u32[]{:S(2)}, u32[]{:S(2)}) collective-permute-start(f32[9,32,128]{2,1,0:T(8,128)S(1)} %get-tuple-element.24), channel_id=1, source_target_pairs={{0,2},{2,0},{4,6},{6,4},{1,3},{3,1},{5,7},{7,5},{8,10},{10,8},{12,... | collective-permute-start | bytes 442376 | tf_op jit(solution)/shard_map/ppermute | solution.py:399
  13.0 4.8 %collective-permute-start.7 = (f32[7,8,128]{2,1,0:T(8,128)S(1)}, f32[7,8,128]{2,1,0:T(8,128)S(1)}, u32[]{:S(2)}, u32[]{:S(2)}) collective-permute-start(f32[7,8,128]{2,1,0:T(8,128)S(1)} %get-tuple-element.31), channel_id=1, source_target_pairs={{0,16},{8,24},{16,0},{24,8},{1,17},{9,25},{17,1},{25,9},{2,18},{10... | collective-permute-start | bytes 86024 | tf_op jit(solution)/shard_map/ppermute | solution.py:496

commit v4 on v3

--- a/solution.py
+++ b/solution.py
@@ -10,7 +10,7 @@
 time_step = 0.2
 scale = time_step / 60.0
 ROWS = 8
-RHS_COST, SUMS_COST, JOIN_COST, EDGE_COST, FACE_COST = 60, 200, 20, 20000, 20000
+RHS_COST, SUMS_COST, JOIN_COST, EDGE_COST, FACE_COST, PACK_COST, HALO_COST = 60, 200, 20, 20000, 200000, 20, 20000
 F32 = jnp.float32
 VMEM = pl.BlockSpec(memory_space=pltpu.VMEM)
 ANY = pl.BlockSpec(memory_space=pl.ANY)
@@ -156,8 +156,8 @@
     ]
 
 
-def sums_at(nx, ny, side, k):
-    start = 3 * nx * ny + (6 * side + k) * ny
+def sums_at(ny, side, k):
+    start = (6 * side + k) * ny
     return slice(start, start + ny)
 
 
@@ -169,7 +169,7 @@
 
 def first_kernel(
     chunks, faces, density, momentum,
-    rho_v, mom_v, flux_y, flux_z, small_b, small_a, edge_a, edge_b, coefs, scalars,
+    rho_v, mom_v, flux_y, flux_z, sums, small_b, small_a, coefs, scalars,
     face_s, sems,
 ):
     nx = faces.shape[0]
@@ -237,30 +237,34 @@
             flux_z[f * nx * ny + x * ny : f * nx * ny + (x + 1) * ny] = values[(2, 4, 5)[f]].reshape(ny, nz)
     for side in range(2):
         for k in range(6):
-            flux_z[sums_at(nx, ny, side, k)] = total[side][k].reshape(ny, nz)
+            sums[sums_at(ny, side, k)] = total[side][k].reshape(ny, nz)
 
     def take_small(ref, high):
         for side in range(2):
             for f, k in enumerate((1, 3, 4)):
-                start = sums_at(nx, ny, side, k).start + high * (ny - ROWS)
-                ref[3 * side + f] = flux_z[pl.ds(pl.multiple_of(start, ROWS), ROWS)]
-
-    def take_edge(ref, high):
-        sign = jnp.where(high == 1, scale, -scale)
-        rows = [pl.ds(high * (ny - 1) + (1 - 2 * high) * k, nx, stride=ny) for k in range(3)]
-        m0, m1, v0 = [], [], []
-        for at in rows:
-            m0.append(mom_v[0, at])
-            m1.append(mom_v[1, at])
-            v0.append(m0[-1] / rho_v[at] * sign)
-        for f in range(3):
-            n1, n2, n3 = [(m0[k] * sign, m0[k] * v0[k], m1[k] * v0[k])[f] for k in range(3)]
-            ref[3 * f] = 45.0 * n1 - 9.0 * n2 + n3
-            ref[3 * f + 1] = n2 - 9.0 * n1
-            ref[3 * f + 2] = n1
+                start = sums_at(ny, side, k).start + high * (ny - 3)
+                ref[9 * side + 3 * f : 9 * side + 3 * f + 3] = sums[pl.ds(start, 3)]
+        ref[18:24] = jnp.zeros((6, nz), F32)
 
     pick_edges(small_a, small_b, take_small)
-    pick_edges(edge_a, edge_b, take_edge)
+
+
+def pack_kernel(nx, second, rho_v, mom_v, ref):
+    ny = rho_v.shape[0] // nx
+    odd = lax.rem(lax.axis_index("gy"), 2)
+    high = odd if second else 1 - odd
+    sign = jnp.where(high == 1, scale, -scale)
+    rows = [pl.ds(high * (ny - 1) + (1 - 2 * high) * k, nx, stride=ny) for k in range(3)]
+    m0, m1, v0 = [], [], []
+    for at in rows:
+        m0.append(mom_v[0, at])
+        m1.append(mom_v[1, at])
+        v0.append(m0[-1] / rho_v[at] * sign)
+    for f in range(3):
+        n1, n2, n3 = [(m0[k] * sign, m0[k] * v0[k], m1[k] * v0[k])[f] for k in range(3)]
+        ref[3 * f] = 45.0 * n1 - 9.0 * n2 + n3
+        ref[3 * f + 1] = n2 - 9.0 * n1
+        ref[3 * f + 2] = n1
 
 
 def halos_y(is_odd, from_a, from_b):
@@ -269,23 +273,30 @@
     return low, high
 
 
-def second_kernel(stages, nx, ny, small_a, small_b, sums, sums_low, sums_high, scalars, *refs):
+def halo_kernel(small_a, small_b, halos):
+    is_odd = lax.rem(lax.axis_index("gy"), 2) == 1
+    low, high = halos_y(is_odd, small_a[...], small_b[...])
+    for k in range(6):
+        halos[k, 0, ROWS - 3 : ROWS] = low[3 * k : 3 * k + 3]
+        halos[k, 1, 0:3] = high[3 * k : 3 * k + 3]
+
+
+def second_kernel(stages, halos, sums, sums_low, sums_high, scalars, *refs):
     nz = sums.shape[1]
+    ny = sums.shape[0] // 12
     tiles = ny // ROWS
     pad = refs[-1]
-    is_odd = lax.rem(lax.axis_index("gy"), 2) == 1
-    low, high = halos_y(is_odd, small_a[...], small_b[...])
     alpha, beta, m, inv_first, inv_last = [scalars[i : i + 1] for i in range(5)]
     values = []
     for side in range(2):
         for f, (state, along_y, along_z) in enumerate(((0, 1, 2), (1, 3, 4), (2, 4, 5))):
             k = 3 * side + f
-            pad[k, 0:ROWS] = low[k]
-            pad[k, ROWS : ROWS + ny] = sums[sums_at(nx, ny, side, along_y)]
-            pad[k, ROWS + ny : 2 * ROWS + ny] = high[k]
+            pad[k, 0:ROWS] = halos[k, 0]
+            pad[k, ROWS : ROWS + ny] = sums[sums_at(ny, side, along_y)]
+            pad[k, ROWS + ny : 2 * ROWS + ny] = halos[k, 1]
             dy = sixth(lambda s: pad[k, ROWS + s : ROWS + s + ny])
-            dz = sixth_z(*[r[sums_at(nx, ny, side, along_z)] for r in (sums, sums_low, sums_high)])
-            value = sums[sums_at(nx, ny, side, state)] - scale * (dy + dz)
+            dz = sixth_z(*[r[sums_at(ny, side, along_z)] for r in (sums, sums_low, sums_high)])
+            value = sums[sums_at(ny, side, state)] - scale * (dy + dz)
             values.append(value.reshape(tiles, ROWS, nz))
     first = jnp.stack(values[:3])
     last = jnp.stack(values[3:]) * m
@@ -431,19 +442,18 @@
     cost = lambda n: pl.CostEstimate(flops=n * cells * nz, bytes_accessed=n * cells * nz, transcendentals=0)
     inputs = (lower_face, density.reshape(cells, nz), momentum.reshape(2, cells, nz))
     inputs = [pltpu.with_memory_space_constraint(x, pltpu.HBM) for x in inputs]
-    density, momentum, flux_y, flux_z, small_b, small_a, edge_a, edge_b, coefs, scalars = pl.pallas_call(
+    density, momentum, flux_y, flux_z, sums, small_b, small_a, coefs, scalars = pl.pallas_call(
         functools.partial(first_kernel, chunks),
         in_specs=[HBM] * 3,
-        out_specs=[VMEM] * 10,
+        out_specs=[VMEM] * 9,
         out_shape=[
             vec(cells),
             vec(2, cells),
             vec(3 * nx * (ny + ROWS) + ROWS),
-            vec(3 * cells + 12 * ny),
-            full(6),
-            full(6),
-            vec(9, nx),
-            vec(9, nx),
+            vec(3 * cells),
+            vec(12 * ny),
+            vec(3 * ROWS),
+            vec(3 * ROWS),
             full(2 * nx),
             full(),
         ],
@@ -452,7 +462,20 @@
         name="load",
     )(*inputs)
     got_a, got_b = swap_edges(small_a, small_b, crossed)
+    edge_a, edge_b = [
+        pl.pallas_call(
+            functools.partial(pack_kernel, nx, second),
+            in_specs=[VMEM] * 2,
+            out_specs=VMEM,
+            out_shape=vec(9, nx),
+            compiler_params=params(),
+            cost_estimate=cost(PACK_COST),
+            name="pack",
+        )(density, momentum)
+        for second in (False, True)
+    ]
     far_a, far_b = swap_edges(edge_a, edge_b)
+    sums_low, sums_high = swap_whole(sums, "gz")
     z_low, z_high = swap_whole(flux_z, "gz")
     rhs = pl.pallas_call(
         functools.partial(rhs_kernel, nx),
@@ -463,25 +486,29 @@
         cost_estimate=cost(RHS_COST),
         name="rhs",
     )(density, momentum, flux_y, flux_z, z_low, z_high)
-    handled = (z_low, flux_z, flux_z) if crossed else (flux_z, z_low, z_high)
+    halos = pl.pallas_call(
+        halo_kernel,
+        in_specs=[VMEM] * 2,
+        out_specs=VMEM,
+        out_shape=full(6, 2),
+        compiler_params=params(),
+        cost_estimate=cost(HALO_COST),
+        name="halo",
+    )(got_a, got_b)
+    handled = (sums_low, sums, sums) if crossed else (sums, sums_low, sums_high)
     msg_shapes = [full(6 * tiles + 1), full(3 * tiles + 1)]
     own_shapes = [full(6 * tiles + 1), full(9 * tiles + 2)]
     msg, *own = pl.pallas_call(
-        functools.partial(second_kernel, stages, nx, ny),
-        in_specs=[VMEM] * 6,
+        functools.partial(second_kernel, stages),
+        in_specs=[VMEM] * 5,
         out_specs=[VMEM] * (1 + (stages == 1)),
         out_shape=[msg_shapes[1], own_shapes[1]] if stages == 1 else msg_shapes[:1],
         scratch_shapes=[pltpu.VMEM((6, ny + 2 * ROWS, nz), F32)],
         compiler_params=params(),
         cost_estimate=cost(FACE_COST),
         name="interface",
-    )(got_a, got_b, *handled, scalars)
-    other = swap(msg, "gx", partner_by(devices, 1), crossed)
-    if crossed:
-        if stages == 1:
-            own = [swap_whole(own[0], "gz")[0]]
-        else:
-            msg, _ = swap_whole(msg, "gz")
+    )(halos, *handled, scalars)
+    other = swap(msg, "gx", partner_by(devices, 1), crossed and stages == 1)
     for stage in range(stages - 1):
         closing_next = stage + 2 == stages
         msg, *own = pl.pallas_call(
@@ -493,8 +520,10 @@
             cost_estimate=cost(JOIN_COST),
             name="join",
         )(msg, other, rhs, *own)
-        other = lax.ppermute(msg, "gx", partner_by(devices, 2 << stage))
+        other = swap(msg, "gx", partner_by(devices, 2 << stage), crossed and closing_next)
     own = own[0]
+    if crossed:
+        own, _ = swap_whole(own, "gz")
     rhs = pl.pallas_call(
         functools.partial(edge_kernel, nx),
         in_specs=[VMEM] * 2,

time: 18.9 us -> 18 us (0.952)
  waiting for transfers between devices: 3.5 us -> 1.77 us
  starting transfers between devices: 10.8 us -> 11.6 us
    ppermute x1 -> x0, starting transfers between devices: 2.65 us -> none  [on_device(): other = lax.ppermute(msg, 'gx', partner_by(devices, 2 << stage))]
    ppermute x2 -> x3, starting transfers between devices: 2.12 us -> 4.09 us  [swap(): return lax.ppermute(block, axis, pairs)]
    ppermute x3, starting transfers between devices: 5.14 us -> 6.29 us  [swap(): return lax.ppermute(block, (axis, 'gz'), both)]
    ppermute x3, waiting for transfers between devices: 1.73 us -> 0.75 us  [swap(): return lax.ppermute(block, (axis, 'gz'), both)]
    ppermute x1 -> x0, waiting for transfers between devices: 0.89 us -> none  [on_device(): other = lax.ppermute(msg, 'gx', partner_by(devices, 2 << stage))]
    ppermute x2 -> x3, starting transfers between devices: 0.91 us -> 1.2 us  [swap_whole(): got = lax.ppermute(block, axis, pairing(2, False))]
    ppermute x2 -> x3, waiting for transfers between devices: 0.89 us -> 1.02 us  [swap(): return lax.ppermute(block, axis, pairs)]
  transfers between devices with their start and end apart: 8 -> 9, of which waited for: 4 -> 4; matrix products, arithmetic and copies ran while one was open for 0% -> 0% of each run, Pallas kernels for 10% -> 12%
where the time goes in v4:
time: 18 us; the launch traced here: 17.8 us
  starting transfers between devices  11.6 us (64%)
  Pallas kernels  4.43 us (25%)
  waiting for transfers between devices  1.77 us (10%)
    ppermute x3, starting transfers between devices, swap(): return lax.ppermute(block, (axis, 'gz'), both)  6.29 us
    ppermute x3, starting transfers between devices, swap(): return lax.ppermute(block, axis, pairs)  4.09 us
    pallas_call x1, Pallas kernels, on_device(): pl.pallas_call(functools.partial(first_kernel, chunks), in_specs=[HBM] *...  1.38 us
    pallas_call x1, Pallas kernels, on_device(): pl.pallas_call(functools.partial(rhs_kernel, nx), in_specs=[VMEM] * 6, ou...  1.33 us
    ppermute x3, starting transfers between devices, swap_whole(): got = lax.ppermute(block, axis, pairing(2, False))  1.2 us
    ppermute x3, waiting for transfers between devices, swap(): return lax.ppermute(block, axis, pairs)  1.02 us
    pallas_call x1, Pallas kernels, on_device(): pl.pallas_call(functools.partial(last_kernel, stages, parts), in_specs=[V...  0.97 us
    ppermute x3, waiting for transfers between devices, swap(): return lax.ppermute(block, (axis, 'gz'), both)  0.75 us
  transfers between devices with their start and end apart: 9, of which 4 were waited for; matrix products, arithmetic and copies ran while one was open for 0% of the time, Pallas kernels for 12%

profile of v4, /device:TPU:0, one launch (start us, length us, event | category | flops | bytes accessed | tf_op | source)
XLA Modules:
  0.0 17.8 jit_solution(16866826154207271493)
XLA Ops:
  0.0 1.4 %load.1 = (f32[512,128]{1,0:T(8,128)S(1)}, f32[2,512,128]{2,1,0:T(8,128)S(1)}, f32[2312,128]{1,0:T(8,128)S(1)}, f32[1536,128]{1,0:T(8,128)S(1)}, f32[192,128]{1,...) custom-call(f32[32]{0:T(128)} %faces.1, ...), custom_call_target="tpu_custom_call" | custom-call | tf_op jit(solution)/shard_map/load/pallas_call | solution.py:445
  1.4 2.4 %collective-permute-start.3 = (f32[24,128]{1,0:T(8,128)S(1)}, f32[24,128]{1,0:T(8,128)S(1)}, u32[]{:S(2)}, u32[]{:S(2)}) collective-permute-start(f32[24,128]{1,0:T(8,128)S(1)} %get-tuple-element.26), channel_id=1, source_target_pairs={{0,3},{1,2},{2,1},{3,0},{4,7},{5,6},{6,5},{7,4},{8,11},{9,10},{10,... | collective-permute-start | bytes 36872 | tf_op jit(solution)/shard_map/ppermute | solution.py:412
  3.8 1.8 %collective-permute-start.4 = (f32[24,128]{1,0:T(8,128)S(1)}, f32[24,128]{1,0:T(8,128)S(1)}, u32[]{:S(2)}, u32[]{:S(2)}) collective-permute-start(f32[24,128]{1,0:T(8,128)S(1)} %get-tuple-element.27), channel_id=1, source_target_pairs={{2,5},{3,4},{4,3},{5,2},{6,1},{7,0},{0,7},{1,6},{10,13},{11,12},{1... | collective-permute-start | bytes 36872 | tf_op jit(solution)/shard_map/ppermute | solution.py:412
  5.6 0.0 collective-permute-start.5
  5.6 0.5 %collective-permute-start = (f32[1536,128]{1,0:T(8,128)S(1)}, f32[1536,128]{1,0:T(8,128)S(1)}, u32[]{:S(2)}, u32[]{:S(2)}) collective-permute-start(f32[1536,128]{1,0:T(8,128)S(1)} %get-tuple-element.21.flux_z), channel_id=1, source_target_pairs={{0,1},{1,0},{2,3},{3,2},{4,5},{5,4},{6,7},{7,6},{8,9},{9,8},{10,11... | collective-permute-start | bytes 2359304 | tf_op jit(solution)/shard_map/ppermute | solution.py:426
  6.1 0.1 pack.2
  6.2 1.5 %collective-permute-start.1 = (f32[9,32,128]{2,1,0:T(8,128)S(1)}, f32[9,32,128]{2,1,0:T(8,128)S(1)}, u32[]{:S(2)}, u32[]{:S(2)}) collective-permute-start(f32[9,32,128]{2,1,0:T(8,128)S(1)} %pack.2), channel_id=1, source_target_pairs={{2,4},{4,2},{6,0},{0,6},{3,5},{5,3},{7,1},{1,7},{10,12},{12,10},{1... | collective-permute-start | bytes 442376 | tf_op jit(solution)/shard_map/ppermute | solution.py:410
  7.7 0.0 collective-permute-done.3.small_a
  7.7 0.2 collective-permute-done.4.small_b
  7.9 0.0 collective-permute-done.5.sums
  7.9 0.1 interface.1.refs_0_
  8.0 1.6 %collective-permute-start.6 = (f32[13,8,128]{2,1,0:T(8,128)S(1)}, f32[13,8,128]{2,1,0:T(8,128)S(1)}, u32[]{:S(2)}, u32[]{:S(2)}) collective-permute-start(f32[13,8,128]{2,1,0:T(8,128)S(1)} %interface.1.refs_0_), channel_id=1, source_target_pairs={{0,8},{8,0},{16,24},{24,16},{1,9},{9,1},{17,25},{25,17},{2,10},{10... | collective-permute-start | bytes 159752 | tf_op jit(solution)/shard_map/ppermute | solution.py:410
  9.7 0.1 pack.3
  9.7 0.9 %collective-permute-start.2 = (f32[9,32,128]{2,1,0:T(8,128)S(1)}, f32[9,32,128]{2,1,0:T(8,128)S(1)}, u32[]{:S(2)}, u32[]{:S(2)}) collective-permute-start(f32[9,32,128]{2,1,0:T(8,128)S(1)} %pack.3), channel_id=1, source_target_pairs={{0,2},{2,0},{4,6},{6,4},{1,3},{3,1},{5,7},{7,5},{8,10},{10,8},{12,... | collective-permute-start | bytes 442376 | tf_op jit(solution)/shard_map/ppermute | solution.py:410
  10.7 0.0 collective-permute-done.flux_z_low.flux_z_high
  10.7 1.3 %rhs.1.rhs_in.refs_2_ = f32[3,512,128]{2,1,0:T(8,128)S(1)} custom-call(f32[512,128]{1,0:T(8,128)S(1)} %get-tuple-element.18.density.rho_v, f32[2,512,128]{2,1,0:T(8,128)S(1)} %get-tuple-element.19.momentum.mom_v, f32[2312,128]{1,0:T(8,128)S(1)} %get-tuple-element.20.flux_y, f32[1536,128]{1,0:T(8,128)S(1)} %get-tuple-element.21.flux_z, ...), custom_call_target="tpu_custom_call" | custom-call | flops 3932160 | bytes 3932160 | tf_op jit(solution)/shard_map/rhs/pallas_call | solution.py:480
  12.0 0.5 %collective-permute-done.6.refs_1_ = f32[13,8,128]{2,1,0:T(8,128)S(1)} collective-permute-done((f32[13,8,128]{2,1,0:T(8,128)S(1)}, f32[13,8,128]{2,1,0:T(8,128)S(1)}, u32[]{:S(2)}, u32[]{:S(2)}) %collective-permute-start.6) | collective-permute-done | bytes 53280 | tf_op jit(solution)/shard_map/ppermute | solution.py:410
  12.5 2.1 %collective-permute-start.7 = (f32[7,8,128]{2,1,0:T(8,128)S(1)}, f32[7,8,128]{2,1,0:T(8,128)S(1)}, u32[]{:S(2)}, u32[]{:S(2)}) collective-permute-start(f32[7,8,128]{2,1,0:T(8,128)S(1)} %get-tuple-element.29), channel_id=1, source_target_pairs={{0,17},{1,16},{8,25},{9,24},{16,1},{17,0},{24,9},{25,8},{2,19},{3,... | collective-permute-start | bytes 86024 | tf_op jit(solution)/shard_map/ppermute | solution.py:412
  14.6 0.7 %collective-permute-start.8 = (f32[20,8,128]{2,1,0:T(8,128)S(1)}, f32[20,8,128]{2,1,0:T(8,128)S(1)}, u32[]{:S(2)}, u32[]{:S(2)}) collective-permute-start(f32[20,8,128]{2,1,0:T(8,128)S(1)} %get-tuple-element.30), channel_id=1, source_target_pairs={{0,1},{1,0},{2,3},{3,2},{4,5},{5,4},{6,7},{7,6},{8,9},{9,8},{10,11... | collective-permute-start | bytes 245768 | tf_op jit(solution)/shard_map/ppermute | solution.py:426
  15.3 0.0 collective-permute-done.1.edge_b
  15.3 0.1 edge.1.rhs_in
  15.4 0.5 %collective-permute-done.2.edge_a = f32[9,32,128]{2,1,0:T(8,128)S(1)} collective-permute-done((f32[9,32,128]{2,1,0:T(8,128)S(1)}, f32[9,32,128]{2,1,0:T(8,128)S(1)}, u32[]{:S(2)}, u32[]{:S(2)}) %collective-permute-start.2) | collective-permute-done | bytes 147488 | tf_op jit(solution)/shard_map/ppermute | solution.py:410
  16.0 0.3 %sums.1 = (f32[3,512,128]{2,1,0:T(8,128)S(1)}, f32[3,32,2,8,128]{4,3,2,1,0:T(8,128)S(1)}, f32[3,32,2,8,128]{4,3,2,1,0:T(8,128)S(1)}) custom-call(f32[3,512,128]{2,1,0:T(8,128)S(1)} %edge.1.rhs_in, f32[9,32,128]{2,1,0:T(8,128)S(1)} %collective-permute-done.2.edge_a, f32[64,8,128]{2,1,0:T(8,128)S(1)} %get-tuple-element.22.coefs), custom_call_target="tpu_custom_call", output_to_operand_aliasing={{0}: (0, {})} | custom-call | flops 13107200 | bytes 13107200 | tf_op jit(solution)/shard_map/sums/pallas_call | solution.py:537
  16.3 0.6 %collective-permute-done.7.other = f32[7,8,128]{2,1,0:T(8,128)S(1)} collective-permute-done((f32[7,8,128]{2,1,0:T(8,128)S(1)}, f32[7,8,128]{2,1,0:T(8,128)S(1)}, u32[]{:S(2)}, u32[]{:S(2)}) %collective-permute-start.7) | collective-permute-done | bytes 28704 | tf_op jit(solution)/shard_map/ppermute | solution.py:412
  16.9 0.0 collective-permute-done.8.own
  16.9 1.0 %solve.1 = f32[3,32,2,8,128]{4,3,2,1,0:T(8,128)} custom-call(f32[3,32,2,8,128]{4,3,2,1,0:T(8,128)S(1)} %get-tuple-element.23.ahead, f32[3,32,2,8,128]{4,3,2,1,0:T(8,128)S(1)} %get-tuple-element.24.behind, f32[64,8,128]{2,1,0:T(8,128)S(1)} %get-tuple-element.22.coefs, f32[8,128]{1,0:T(8,128)S(1)} %get-tuple-element.25.scalars, ...), custom_call_target="tpu_custom_call" | custom-call | tf_op jit(solution)/shard_map/solve/pallas_call | solution.py:547
  (2 shorter events, 0.0 us)
Async XLA Ops:
  1.4 6.3 %collective-permute-start.3 = (f32[24,128]{1,0:T(8,128)S(1)}, f32[24,128]{1,0:T(8,128)S(1)}, u32[]{:S(2)}, u32[]{:S(2)}) collective-permute-start(f32[24,128]{1,0:T(8,128)S(1)} %get-tuple-element.26), channel_id=1, source_target_pairs={{0,3},{1,2},{2,1},{3,0},{4,7},{5,6},{6,5},{7,4},{8,11},{9,10},{10,... | collective-permute-start | bytes 36872 | tf_op jit(solution)/shard_map/ppermute | solution.py:412
  3.8 4.0 %collective-permute-start.4 = (f32[24,128]{1,0:T(8,128)S(1)}, f32[24,128]{1,0:T(8,128)S(1)}, u32[]{:S(2)}, u32[]{:S(2)}) collective-permute-start(f32[24,128]{1,0:T(8,128)S(1)} %get-tuple-element.27), channel_id=1, source_target_pairs={{2,5},{3,4},{4,3},{5,2},{6,1},{7,0},{0,7},{1,6},{10,13},{11,12},{1... | collective-permute-start | bytes 36872 | tf_op jit(solution)/shard_map/ppermute | solution.py:412
  5.6 2.3 %collective-permute-start.5 = (f32[192,128]{1,0:T(8,128)S(1)}, f32[192,128]{1,0:T(8,128)S(1)}, u32[]{:S(2)}, u32[]{:S(2)}) collective-permute-start(f32[192,128]{1,0:T(8,128)S(1)} %get-tuple-element.28.sums_low.sums_high), channel_id=1, source_target_pairs={{0,1},{1,0},{2,3},{3,2},{4,5},{5,4},{6,7},{7,6},{8,9},{9,8},{10,11... | collective-permute-start | bytes 294920 | tf_op jit(solution)/shard_map/ppermute | solution.py:426
  5.6 5.1 %collective-permute-start = (f32[1536,128]{1,0:T(8,128)S(1)}, f32[1536,128]{1,0:T(8,128)S(1)}, u32[]{:S(2)}, u32[]{:S(2)}) collective-permute-start(f32[1536,128]{1,0:T(8,128)S(1)} %get-tuple-element.21.flux_z), channel_id=1, source_target_pairs={{0,1},{1,0},{2,3},{3,2},{4,5},{5,4},{6,7},{7,6},{8,9},{9,8},{10,11... | collective-permute-start | bytes 2359304 | tf_op jit(solution)/shard_map/ppermute | solution.py:426
  6.2 9.1 %collective-permute-start.1 = (f32[9,32,128]{2,1,0:T(8,128)S(1)}, f32[9,32,128]{2,1,0:T(8,128)S(1)}, u32[]{:S(2)}, u32[]{:S(2)}) collective-permute-start(f32[9,32,128]{2,1,0:T(8,128)S(1)} %pack.2), channel_id=1, source_target_pairs={{2,4},{4,2},{6,0},{0,6},{3,5},{5,3},{7,1},{1,7},{10,12},{12,10},{1... | collective-permute-start | bytes 442376 | tf_op jit(solution)/shard_map/ppermute | solution.py:410
  8.0 4.5 %collective-permute-start.6 = (f32[13,8,128]{2,1,0:T(8,128)S(1)}, f32[13,8,128]{2,1,0:T(8,128)S(1)}, u32[]{:S(2)}, u32[]{:S(2)}) collective-permute-start(f32[13,8,128]{2,1,0:T(8,128)S(1)} %interface.1.refs_0_), channel_id=1, source_target_pairs={{0,8},{8,0},{16,24},{24,16},{1,9},{9,1},{17,25},{25,17},{2,10},{10... | collective-permute-start | bytes 159752 | tf_op jit(solution)/shard_map/ppermute | solution.py:410
  9.7 6.2 %collective-permute-start.2 = (f32[9,32,128]{2,1,0:T(8,128)S(1)}, f32[9,32,128]{2,1,0:T(8,128)S(1)}, u32[]{:S(2)}, u32[]{:S(2)}) collective-permute-start(f32[9,32,128]{2,1,0:T(8,128)S(1)} %pack.3), channel_id=1, source_target_pairs={{0,2},{2,0},{4,6},{6,4},{1,3},{3,1},{5,7},{7,5},{8,10},{10,8},{12,... | collective-permute-start | bytes 442376 | tf_op jit(solution)/shard_map/ppermute | solution.py:410
  12.5 4.3 %collective-permute-start.7 = (f32[7,8,128]{2,1,0:T(8,128)S(1)}, f32[7,8,128]{2,1,0:T(8,128)S(1)}, u32[]{:S(2)}, u32[]{:S(2)}) collective-permute-start(f32[7,8,128]{2,1,0:T(8,128)S(1)} %get-tuple-element.29), channel_id=1, source_target_pairs={{0,17},{1,16},{8,25},{9,24},{16,1},{17,0},{24,9},{25,8},{2,19},{3,... | collective-permute-start | bytes 86024 | tf_op jit(solution)/shard_map/ppermute | solution.py:412
  14.6 2.2 %collective-permute-start.8 = (f32[20,8,128]{2,1,0:T(8,128)S(1)}, f32[20,8,128]{2,1,0:T(8,128)S(1)}, u32[]{:S(2)}, u32[]{:S(2)}) collective-permute-start(f32[20,8,128]{2,1,0:T(8,128)S(1)} %get-tuple-element.30), channel_id=1, source_target_pairs={{0,1},{1,0},{2,3},{3,2},{4,5},{5,4},{6,7},{7,6},{8,9},{9,8},{10,11... | collective-permute-start | bytes 245768 | tf_op jit(solution)/shard_map/ppermute | solution.py:426

commit v5 on v4

--- a/solution.py
+++ b/solution.py
@@ -10,7 +10,7 @@
 time_step = 0.2
 scale = time_step / 60.0
 ROWS = 8
-RHS_COST, SUMS_COST, JOIN_COST, EDGE_COST, FACE_COST, PACK_COST, HALO_COST = 60, 200, 20, 20000, 200000, 20, 20000
+RHS_COST, SUMS_COST, JOIN_COST, EDGE_COST, FACE_COST, PACK_COST, HALO_COST = 60, 200, 20, 20000, 200000, 20000, 20
 F32 = jnp.float32
 VMEM = pl.BlockSpec(memory_space=pltpu.VMEM)
 ANY = pl.BlockSpec(memory_space=pl.ANY)
@@ -157,7 +157,7 @@
 
 
 def sums_at(ny, side, k):
-    start = (6 * side + k) * ny
+    start = (2 * k + side) * ny
     return slice(start, start + ny)
 
 
@@ -226,31 +226,34 @@
         rho, m0, m1 = [b.reshape(tiles, ROWS, nz) for b in (rho_v[at], mom_v[0, at], mom_v[1, at])]
         inv_rho = 1.0 / rho
         v0, v1 = m0 * inv_rho, m1 * inv_rho
-        values = (rho, m0, m1, m0 * v0, m0 * v1, m1 * v1)
+        values = (m0, m0 * v0, m0 * v1, rho, m1, m1 * v1)
         for side, weight in enumerate((coefs[nx + x], coefs[x])):
             for k, value in enumerate(values):
                 term = weight * value
                 total[side][k] = term if x == 0 else total[side][k] + term
         for f in range(3):
             start = (f * nx + x) * pitch + ROWS
-            flux_y[start : start + ny] = values[(1, 3, 4)[f]].reshape(ny, nz)
-            flux_z[f * nx * ny + x * ny : f * nx * ny + (x + 1) * ny] = values[(2, 4, 5)[f]].reshape(ny, nz)
+            flux_y[start : start + ny] = values[f].reshape(ny, nz)
+            flux_z[f * nx * ny + x * ny : f * nx * ny + (x + 1) * ny] = values[(4, 2, 5)[f]].reshape(ny, nz)
     for side in range(2):
         for k in range(6):
             sums[sums_at(ny, side, k)] = total[side][k].reshape(ny, nz)
 
     def take_small(ref, high):
-        for side in range(2):
-            for f, k in enumerate((1, 3, 4)):
-                start = sums_at(ny, side, k).start + high * (ny - 3)
-                ref[9 * side + 3 * f : 9 * side + 3 * f + 3] = sums[pl.ds(start, 3)]
-        ref[18:24] = jnp.zeros((6, nz), F32)
+        sign = jnp.where(high == 1, scale, -scale)
+        n1, n2, n3 = [
+            sums[pl.ds(high * (ny - 1) + (1 - 2 * high) * k, 6, stride=ny)] * sign for k in range(3)
+        ]
+        ref[...] = jnp.zeros((3 * ROWS, nz), F32)
+        ref[0:6] = 45.0 * n1 - 9.0 * n2 + n3
+        ref[ROWS : ROWS + 6] = n2 - 9.0 * n1
+        ref[2 * ROWS : 2 * ROWS + 6] = n1
 
     pick_edges(small_a, small_b, take_small)
 
 
 def pack_kernel(nx, second, rho_v, mom_v, ref):
-    ny = rho_v.shape[0] // nx
+    ny = rho_v.shape[0] // (nx + 1)
     odd = lax.rem(lax.axis_index("gy"), 2)
     high = odd if second else 1 - odd
     sign = jnp.where(high == 1, scale, -scale)
@@ -273,31 +276,32 @@
     return low, high
 
 
-def halo_kernel(small_a, small_b, halos):
+def inner_kernel(sums, sums_low, sums_high, inner, pad):
+    nz = sums.shape[1]
+    ny = sums.shape[0] // 12
+    pad[0:ROWS] = jnp.zeros((ROWS, nz), F32)
+    pad[ROWS + ny : 2 * ROWS + ny] = jnp.zeros((ROWS, nz), F32)
+    for side in range(2):
+        for f, (state, along_y, along_z) in enumerate(((3, 0, 4), (0, 1, 2), (4, 2, 5))):
+            pad[ROWS : ROWS + ny] = sums[sums_at(ny, side, along_y)]
+            dy = sixth(lambda s: pad[ROWS + s : ROWS + s + ny])
+            dz = sixth_z(*[r[sums_at(ny, side, along_z)] for r in (sums, sums_low, sums_high)])
+            inner[sums_at(ny, side, f)] = sums[sums_at(ny, side, state)] - scale * (dy + dz)
+
+
+def second_kernel(stages, small_a, small_b, inner, scalars, *refs):
+    ny, nz = inner.shape[0] // 6, inner.shape[1]
+    tiles = ny // ROWS
+    block = refs[-1]
     is_odd = lax.rem(lax.axis_index("gy"), 2) == 1
     low, high = halos_y(is_odd, small_a[...], small_b[...])
-    for k in range(6):
-        halos[k, 0, ROWS - 3 : ROWS] = low[3 * k : 3 * k + 3]
-        halos[k, 1, 0:3] = high[3 * k : 3 * k + 3]
-
-
-def second_kernel(stages, halos, sums, sums_low, sums_high, scalars, *refs):
-    nz = sums.shape[1]
-    ny = sums.shape[0] // 12
-    tiles = ny // ROWS
-    pad = refs[-1]
     alpha, beta, m, inv_first, inv_last = [scalars[i : i + 1] for i in range(5)]
-    values = []
-    for side in range(2):
-        for f, (state, along_y, along_z) in enumerate(((0, 1, 2), (1, 3, 4), (2, 4, 5))):
-            k = 3 * side + f
-            pad[k, 0:ROWS] = halos[k, 0]
-            pad[k, ROWS : ROWS + ny] = sums[sums_at(ny, side, along_y)]
-            pad[k, ROWS + ny : 2 * ROWS + ny] = halos[k, 1]
-            dy = sixth(lambda s: pad[k, ROWS + s : ROWS + s + ny])
-            dz = sixth_z(*[r[sums_at(ny, side, along_z)] for r in (sums, sums_low, sums_high)])
-            value = sums[sums_at(ny, side, state)] - scale * (dy + dz)
-            values.append(value.reshape(tiles, ROWS, nz))
+    block[0 : 6 * ny] = inner[...]
+    for k in range(3):
+        for row, edge in ((k, low), (ny - 1 - k, high)):
+            at = pl.ds(row, 6, stride=ny)
+            block[at] = block[at] + edge[k * ROWS : k * ROWS + 6]
+    values = [block[sums_at(ny, side, f)].reshape(tiles, ROWS, nz) for side in range(2) for f in range(3)]
     first = jnp.stack(values[:3])
     last = jnp.stack(values[3:]) * m
     group = (first, last, alpha, beta, m, inv_first, inv_last)
@@ -335,7 +339,7 @@
 
 
 def rhs_kernel(nx, density, momentum, flux_y, flux_z, flux_z_low, flux_z_high, rhs):
-    ny = density.shape[0] // nx
+    ny = density.shape[0] // (nx + 1)
     pitch = ny + ROWS
     for f in range(3):
         for x in range(nx):
@@ -349,7 +353,7 @@
 
 
 def add_edge(nx, rhs, edge, high):
-    ny = rhs.shape[1] // nx
+    ny = rhs.shape[1] // (nx + 1)
     for f in range(3):
         for k in range(3):
             at = pl.ds(high * (ny - 1) + (1 - 2 * high) * k, nx, stride=ny)
@@ -361,7 +365,7 @@
 
 
 def sums_kernel(nx, rhs_in, edge_a, coefs, rhs, ahead, behind):
-    ny, nz = rhs.shape[1] // nx, rhs.shape[2]
+    ny, nz = rhs.shape[1] // (nx + 1), rhs.shape[2]
     shape = (ny // ROWS, ROWS, nz)
     add_edge(nx, rhs, edge_a, 1 - lax.rem(lax.axis_index("gy"), 2))
     for f in range(3):
@@ -447,8 +451,8 @@
         in_specs=[HBM] * 3,
         out_specs=[VMEM] * 9,
         out_shape=[
-            vec(cells),
-            vec(2, cells),
+            vec(cells + ny),
+            vec(2, cells + ny),
             vec(3 * nx * (ny + ROWS) + ROWS),
             vec(3 * cells),
             vec(12 * ny),
@@ -481,33 +485,34 @@
         functools.partial(rhs_kernel, nx),
         in_specs=[VMEM] * 6,
         out_specs=VMEM,
-        out_shape=vec(3, cells),
+        out_shape=vec(3, cells + ny),
         compiler_params=params(),
         cost_estimate=cost(RHS_COST),
         name="rhs",
     )(density, momentum, flux_y, flux_z, z_low, z_high)
-    halos = pl.pallas_call(
-        halo_kernel,
-        in_specs=[VMEM] * 2,
+    handled = (sums_low, sums, sums) if crossed else (sums, sums_low, sums_high)
+    inner = pl.pallas_call(
+        inner_kernel,
+        in_specs=[VMEM] * 3,
         out_specs=VMEM,
-        out_shape=full(6, 2),
+        out_shape=vec(6 * ny),
+        scratch_shapes=[pltpu.VMEM((ny + 2 * ROWS, nz), F32)],
         compiler_params=params(),
         cost_estimate=cost(HALO_COST),
-        name="halo",
-    )(got_a, got_b)
-    handled = (sums_low, sums, sums) if crossed else (sums, sums_low, sums_high)
+        name="inner",
+    )(*handled)
     msg_shapes = [full(6 * tiles + 1), full(3 * tiles + 1)]
     own_shapes = [full(6 * tiles + 1), full(9 * tiles + 2)]
     msg, *own = pl.pallas_call(
         functools.partial(second_kernel, stages),
-        in_specs=[VMEM] * 5,
+        in_specs=[VMEM] * 4,
         out_specs=[VMEM] * (1 + (stages == 1)),
         out_shape=[msg_shapes[1], own_shapes[1]] if stages == 1 else msg_shapes[:1],
-        scratch_shapes=[pltpu.VMEM((6, ny + 2 * ROWS, nz), F32)],
+        scratch_shapes=[pltpu.VMEM((7 * ny, nz), F32)],
         compiler_params=params(),
         cost_estimate=cost(FACE_COST),
         name="interface",
-    )(halos, *handled, scalars)
+    )(got_a, got_b, inner, scalars)
     other = swap(msg, "gx", partner_by(devices, 1), crossed and stages == 1)
     for stage in range(stages - 1):
         closing_next = stage + 2 == stages
@@ -528,7 +533,7 @@
         functools.partial(edge_kernel, nx),
         in_specs=[VMEM] * 2,
         out_specs=VMEM,
-        out_shape=vec(3, cells),
+        out_shape=vec(3, cells + ny),
         input_output_aliases={0: 0},
         compiler_params=params(),
         cost_estimate=cost(EDGE_COST),
@@ -538,7 +543,7 @@
         functools.partial(sums_kernel, nx),
         in_specs=[VMEM] * 3,
         out_specs=[VMEM] * 3,
-        out_shape=[vec(3, cells)] + [full(3, nx, tiles)] * 2,
+        out_shape=[vec(3, cells + ny)] + [full(3, nx, tiles)] * 2,
         input_output_aliases={0: 0},
         compiler_params=params(),
         cost_estimate=cost(SUMS_COST),

time: 18 us -> 17.9 us (level)
  transfers between devices with their start and end apart: 9 -> 9, of which waited for: 4 -> 3; matrix products, arithmetic and copies ran while one was open for 0% -> 0% of each run, Pallas kernels for 12% -> 12%
where the time goes in v5:
time: 17.9 us; the launch traced here: 17.7 us
  starting transfers between devices  11.5 us (64%)
  Pallas kernels  4.49 us (25%)
  waiting for transfers between devices  1.61 us (9%)
    ppermute x3, starting transfers between devices, swap(): return lax.ppermute(block, (axis, 'gz'), both)  6.25 us
    ppermute x3, starting transfers between devices, swap(): return lax.ppermute(block, axis, pairs)  4.05 us
    pallas_call x1, Pallas kernels, on_device(): pl.pallas_call(functools.partial(first_kernel, chunks), in_specs=[HBM] *...  1.39 us
    pallas_call x1, Pallas kernels, on_device(): pl.pallas_call(functools.partial(rhs_kernel, nx), in_specs=[VMEM] * 6, ou...  1.33 us
    ppermute x3, starting transfers between devices, swap_whole(): got = lax.ppermute(block, axis, pairing(2, False))  1.24 us
    ppermute x3, waiting for transfers between devices, swap(): return lax.ppermute(block, axis, pairs)  0.98 us
    pallas_call x1, Pallas kernels, on_device(): pl.pallas_call(functools.partial(last_kernel, stages, parts), in_specs=[V...  0.97 us
    ppermute x3, waiting for transfers between devices, swap(): return lax.ppermute(block, (axis, 'gz'), both)  0.62 us
  transfers between devices with their start and end apart: 9, of which 3 were waited for; matrix products, arithmetic and copies ran while one was open for 0% of the time, Pallas kernels for 12%

profile of v5, /device:TPU:0, one launch (start us, length us, event | category | flops | bytes accessed | tf_op | source)
XLA Modules:
  0.0 17.7 jit_solution(4095775130451356537)
XLA Ops:
  0.0 1.4 %load.1 = (f32[528,128]{1,0:T(8,128)S(1)}, f32[2,528,128]{2,1,0:T(8,128)S(1)}, f32[2312,128]{1,0:T(8,128)S(1)}, f32[1536,128]{1,0:T(8,128)S(1)}, f32[192,128]{1,...) custom-call(f32[32]{0:T(128)} %faces.1, ...), custom_call_target="tpu_custom_call" | custom-call | tf_op jit(solution)/shard_map/load/pallas_call | solution.py:449
  1.4 2.4 %collective-permute-start.3 = (f32[24,128]{1,0:T(8,128)S(1)}, f32[24,128]{1,0:T(8,128)S(1)}, u32[]{:S(2)}, u32[]{:S(2)}) collective-permute-start(f32[24,128]{1,0:T(8,128)S(1)} %get-tuple-element.26), channel_id=1, source_target_pairs={{0,3},{1,2},{2,1},{3,0},{4,7},{5,6},{6,5},{7,4},{8,11},{9,10},{10,... | collective-permute-start | bytes 36872 | tf_op jit(solution)/shard_map/ppermute | solution.py:416
  3.8 1.8 %collective-permute-start.4 = (f32[24,128]{1,0:T(8,128)S(1)}, f32[24,128]{1,0:T(8,128)S(1)}, u32[]{:S(2)}, u32[]{:S(2)}) collective-permute-start(f32[24,128]{1,0:T(8,128)S(1)} %get-tuple-element.27), channel_id=1, source_target_pairs={{2,5},{3,4},{4,3},{5,2},{6,1},{7,0},{0,7},{1,6},{10,13},{11,12},{1... | collective-permute-start | bytes 36872 | tf_op jit(solution)/shard_map/ppermute | solution.py:416
  5.6 0.0 collective-permute-start.5
  5.6 0.5 %collective-permute-start = (f32[1536,128]{1,0:T(8,128)S(1)}, f32[1536,128]{1,0:T(8,128)S(1)}, u32[]{:S(2)}, u32[]{:S(2)}) collective-permute-start(f32[1536,128]{1,0:T(8,128)S(1)} %get-tuple-element.21.flux_z), channel_id=1, source_target_pairs={{0,1},{1,0},{2,3},{3,2},{4,5},{5,4},{6,7},{7,6},{8,9},{9,8},{10,11... | collective-permute-start | bytes 2359304 | tf_op jit(solution)/shard_map/ppermute | solution.py:430
  6.1 0.1 pack.2
  6.2 1.5 %collective-permute-start.1 = (f32[9,32,128]{2,1,0:T(8,128)S(1)}, f32[9,32,128]{2,1,0:T(8,128)S(1)}, u32[]{:S(2)}, u32[]{:S(2)}) collective-permute-start(f32[9,32,128]{2,1,0:T(8,128)S(1)} %pack.2), channel_id=1, source_target_pairs={{2,4},{4,2},{6,0},{0,6},{3,5},{5,3},{7,1},{1,7},{10,12},{12,10},{1... | collective-permute-start | bytes 442376 | tf_op jit(solution)/shard_map/ppermute | solution.py:414
  7.7 0.0 collective-permute-done.5.sums
  7.7 0.2 inner.1
  7.9 0.0 collective-permute-done.3.small_a
  7.9 0.0 collective-permute-done.4.small_b
  7.9 1.6 %collective-permute-start.6 = (f32[13,8,128]{2,1,0:T(8,128)S(1)}, f32[13,8,128]{2,1,0:T(8,128)S(1)}, u32[]{:S(2)}, u32[]{:S(2)}) collective-permute-start(f32[13,8,128]{2,1,0:T(8,128)S(1)} %interface.1.refs_0_), channel_id=1, source_target_pairs={{0,8},{8,0},{16,24},{24,16},{1,9},{9,1},{17,25},{25,17},{2,10},{10... | collective-permute-start | bytes 159752 | tf_op jit(solution)/shard_map/ppermute | solution.py:414
  9.6 0.1 pack.3
  9.7 0.9 %collective-permute-start.2 = (f32[9,32,128]{2,1,0:T(8,128)S(1)}, f32[9,32,128]{2,1,0:T(8,128)S(1)}, u32[]{:S(2)}, u32[]{:S(2)}) collective-permute-start(f32[9,32,128]{2,1,0:T(8,128)S(1)} %pack.3), channel_id=1, source_target_pairs={{0,2},{2,0},{4,6},{6,4},{1,3},{3,1},{5,7},{7,5},{8,10},{10,8},{12,... | collective-permute-start | bytes 442376 | tf_op jit(solution)/shard_map/ppermute | solution.py:414
  10.6 0.0 collective-permute-done.flux_z_low.flux_z_high
  10.6 1.3 %rhs.1.rhs_in.refs_2_ = f32[3,528,128]{2,1,0:T(8,128)S(1)} custom-call(f32[528,128]{1,0:T(8,128)S(1)} %get-tuple-element.18.density.rho_v, f32[2,528,128]{2,1,0:T(8,128)S(1)} %get-tuple-element.19.momentum.mom_v, f32[2312,128]{1,0:T(8,128)S(1)} %get-tuple-element.20.flux_y, f32[1536,128]{1,0:T(8,128)S(1)} %get-tuple-element.21.flux_z, ...), custom_call_target="tpu_custom_call" | custom-call | flops 3932160 | bytes 3932160 | tf_op jit(solution)/shard_map/rhs/pallas_call | solution.py:484
  11.9 0.5 %collective-permute-done.6.refs_1_ = f32[13,8,128]{2,1,0:T(8,128)S(1)} collective-permute-done((f32[13,8,128]{2,1,0:T(8,128)S(1)}, f32[13,8,128]{2,1,0:T(8,128)S(1)}, u32[]{:S(2)}, u32[]{:S(2)}) %collective-permute-start.6) | collective-permute-done | bytes 53280 | tf_op jit(solution)/shard_map/ppermute | solution.py:414
  12.4 2.0 %collective-permute-start.7 = (f32[7,8,128]{2,1,0:T(8,128)S(1)}, f32[7,8,128]{2,1,0:T(8,128)S(1)}, u32[]{:S(2)}, u32[]{:S(2)}) collective-permute-start(f32[7,8,128]{2,1,0:T(8,128)S(1)} %get-tuple-element.29), channel_id=1, source_target_pairs={{0,17},{1,16},{8,25},{9,24},{16,1},{17,0},{24,9},{25,8},{2,19},{3,... | collective-permute-start | bytes 86024 | tf_op jit(solution)/shard_map/ppermute | solution.py:416
  14.5 0.7 %collective-permute-start.8 = (f32[20,8,128]{2,1,0:T(8,128)S(1)}, f32[20,8,128]{2,1,0:T(8,128)S(1)}, u32[]{:S(2)}, u32[]{:S(2)}) collective-permute-start(f32[20,8,128]{2,1,0:T(8,128)S(1)} %get-tuple-element.30), channel_id=1, source_target_pairs={{0,1},{1,0},{2,3},{3,2},{4,5},{5,4},{6,7},{7,6},{8,9},{9,8},{10,11... | collective-permute-start | bytes 245768 | tf_op jit(solution)/shard_map/ppermute | solution.py:430
  15.2 0.0 collective-permute-done.1.edge_b
  15.2 0.1 edge.1.rhs_in
  15.3 0.5 %collective-permute-done.2.edge_a = f32[9,32,128]{2,1,0:T(8,128)S(1)} collective-permute-done((f32[9,32,128]{2,1,0:T(8,128)S(1)}, f32[9,32,128]{2,1,0:T(8,128)S(1)}, u32[]{:S(2)}, u32[]{:S(2)}) %collective-permute-start.2) | collective-permute-done | bytes 147488 | tf_op jit(solution)/shard_map/ppermute | solution.py:414
  15.8 0.3 %sums.1 = (f32[3,528,128]{2,1,0:T(8,128)S(1)}, f32[3,32,2,8,128]{4,3,2,1,0:T(8,128)S(1)}, f32[3,32,2,8,128]{4,3,2,1,0:T(8,128)S(1)}) custom-call(f32[3,528,128]{2,1,0:T(8,128)S(1)} %edge.1.rhs_in, f32[9,32,128]{2,1,0:T(8,128)S(1)} %collective-permute-done.2.edge_a, f32[64,8,128]{2,1,0:T(8,128)S(1)} %get-tuple-element.22.coefs), custom_call_target="tpu_custom_call", output_to_operand_aliasing={{0}: (0, {})} | custom-call | flops 13107200 | bytes 13107200 | tf_op jit(solution)/shard_map/sums/pallas_call | solution.py:542
  16.1 0.6 %collective-permute-done.7.other = f32[7,8,128]{2,1,0:T(8,128)S(1)} collective-permute-done((f32[7,8,128]{2,1,0:T(8,128)S(1)}, f32[7,8,128]{2,1,0:T(8,128)S(1)}, u32[]{:S(2)}, u32[]{:S(2)}) %collective-permute-start.7) | collective-permute-done | bytes 28704 | tf_op jit(solution)/shard_map/ppermute | solution.py:416
  16.7 0.0 collective-permute-done.8.own
  16.7 1.0 %solve.1 = f32[3,32,2,8,128]{4,3,2,1,0:T(8,128)} custom-call(f32[3,32,2,8,128]{4,3,2,1,0:T(8,128)S(1)} %get-tuple-element.23.ahead, f32[3,32,2,8,128]{4,3,2,1,0:T(8,128)S(1)} %get-tuple-element.24.behind, f32[64,8,128]{2,1,0:T(8,128)S(1)} %get-tuple-element.22.coefs, f32[8,128]{1,0:T(8,128)S(1)} %get-tuple-element.25.scalars, ...), custom_call_target="tpu_custom_call" | custom-call | tf_op jit(solution)/shard_map/solve/pallas_call | solution.py:552
  (2 shorter events, 0.1 us)
Async XLA Ops:
  1.4 6.5 %collective-permute-start.3 = (f32[24,128]{1,0:T(8,128)S(1)}, f32[24,128]{1,0:T(8,128)S(1)}, u32[]{:S(2)}, u32[]{:S(2)}) collective-permute-start(f32[24,128]{1,0:T(8,128)S(1)} %get-tuple-element.26), channel_id=1, source_target_pairs={{0,3},{1,2},{2,1},{3,0},{4,7},{5,6},{6,5},{7,4},{8,11},{9,10},{10,... | collective-permute-start | bytes 36872 | tf_op jit(solution)/shard_map/ppermute | solution.py:416
  3.8 4.0 %collective-permute-start.4 = (f32[24,128]{1,0:T(8,128)S(1)}, f32[24,128]{1,0:T(8,128)S(1)}, u32[]{:S(2)}, u32[]{:S(2)}) collective-permute-start(f32[24,128]{1,0:T(8,128)S(1)} %get-tuple-element.27), channel_id=1, source_target_pairs={{2,5},{3,4},{4,3},{5,2},{6,1},{7,0},{0,7},{1,6},{10,13},{11,12},{1... | collective-permute-start | bytes 36872 | tf_op jit(solution)/shard_map/ppermute | solution.py:416
  5.6 2.1 %collective-permute-start.5 = (f32[192,128]{1,0:T(8,128)S(1)}, f32[192,128]{1,0:T(8,128)S(1)}, u32[]{:S(2)}, u32[]{:S(2)}) collective-permute-start(f32[192,128]{1,0:T(8,128)S(1)} %get-tuple-element.28.sums_low.sums_high), channel_id=1, source_target_pairs={{0,1},{1,0},{2,3},{3,2},{4,5},{5,4},{6,7},{7,6},{8,9},{9,8},{10,11... | collective-permute-start | bytes 294920 | tf_op jit(solution)/shard_map/ppermute | solution.py:430
  5.6 4.9 %collective-permute-start = (f32[1536,128]{1,0:T(8,128)S(1)}, f32[1536,128]{1,0:T(8,128)S(1)}, u32[]{:S(2)}, u32[]{:S(2)}) collective-permute-start(f32[1536,128]{1,0:T(8,128)S(1)} %get-tuple-element.21.flux_z), channel_id=1, source_target_pairs={{0,1},{1,0},{2,3},{3,2},{4,5},{5,4},{6,7},{7,6},{8,9},{9,8},{10,11... | collective-permute-start | bytes 2359304 | tf_op jit(solution)/shard_map/ppermute | solution.py:430
  6.2 9.0 %collective-permute-start.1 = (f32[9,32,128]{2,1,0:T(8,128)S(1)}, f32[9,32,128]{2,1,0:T(8,128)S(1)}, u32[]{:S(2)}, u32[]{:S(2)}) collective-permute-start(f32[9,32,128]{2,1,0:T(8,128)S(1)} %pack.2), channel_id=1, source_target_pairs={{2,4},{4,2},{6,0},{0,6},{3,5},{5,3},{7,1},{1,7},{10,12},{12,10},{1... | collective-permute-start | bytes 442376 | tf_op jit(solution)/shard_map/ppermute | solution.py:414
  7.9 4.4 %collective-permute-start.6 = (f32[13,8,128]{2,1,0:T(8,128)S(1)}, f32[13,8,128]{2,1,0:T(8,128)S(1)}, u32[]{:S(2)}, u32[]{:S(2)}) collective-permute-start(f32[13,8,128]{2,1,0:T(8,128)S(1)} %interface.1.refs_0_), channel_id=1, source_target_pairs={{0,8},{8,0},{16,24},{24,16},{1,9},{9,1},{17,25},{25,17},{2,10},{10... | collective-permute-start | bytes 159752 | tf_op jit(solution)/shard_map/ppermute | solution.py:414
  9.7 6.2 %collective-permute-start.2 = (f32[9,32,128]{2,1,0:T(8,128)S(1)}, f32[9,32,128]{2,1,0:T(8,128)S(1)}, u32[]{:S(2)}, u32[]{:S(2)}) collective-permute-start(f32[9,32,128]{2,1,0:T(8,128)S(1)} %pack.3), channel_id=1, source_target_pairs={{0,2},{2,0},{4,6},{6,4},{1,3},{3,1},{5,7},{7,5},{8,10},{10,8},{12,... | collective-permute-start | bytes 442376 | tf_op jit(solution)/shard_map/ppermute | solution.py:414
  12.4 4.3 %collective-permute-start.7 = (f32[7,8,128]{2,1,0:T(8,128)S(1)}, f32[7,8,128]{2,1,0:T(8,128)S(1)}, u32[]{:S(2)}, u32[]{:S(2)}) collective-permute-start(f32[7,8,128]{2,1,0:T(8,128)S(1)} %get-tuple-element.29), channel_id=1, source_target_pairs={{0,17},{1,16},{8,25},{9,24},{16,1},{17,0},{24,9},{25,8},{2,19},{3,... | collective-permute-start | bytes 86024 | tf_op jit(solution)/shard_map/ppermute | solution.py:416
  14.5 2.3 %collective-permute-start.8 = (f32[20,8,128]{2,1,0:T(8,128)S(1)}, f32[20,8,128]{2,1,0:T(8,128)S(1)}, u32[]{:S(2)}, u32[]{:S(2)}) collective-permute-start(f32[20,8,128]{2,1,0:T(8,128)S(1)} %get-tuple-element.30), channel_id=1, source_target_pairs={{0,1},{1,0},{2,3},{3,2},{4,5},{5,4},{6,7},{7,6},{8,9},{9,8},{10,11... | collective-permute-start | bytes 245768 | tf_op jit(solution)/shard_map/ppermute | solution.py:430

commit v6 on v5

--- a/solution.py
+++ b/solution.py
@@ -27,10 +27,6 @@
 
 def partner_by(count, step):
     return [(i, i ^ step) for i in range(count)]
-
-
-def rows_of(block):
-    return block.reshape(block.shape[0] * block.shape[1], block.shape[2])
 
 
 def shifted_z(own, low, high, k):
@@ -361,12 +357,14 @@
 
 
 def edge_kernel(nx, rhs_in, edge_b, rhs):
+    rhs[...] = rhs_in[...]
     add_edge(nx, rhs, edge_b, lax.rem(lax.axis_index("gy"), 2))
 
 
 def sums_kernel(nx, rhs_in, edge_a, coefs, rhs, ahead, behind):
     ny, nz = rhs.shape[1] // (nx + 1), rhs.shape[2]
     shape = (ny // ROWS, ROWS, nz)
+    rhs[...] = rhs_in[...]
     add_edge(nx, rhs, edge_a, 1 - lax.rem(lax.axis_index("gy"), 2))
     for f in range(3):
         total = None

time: 17.9 us -> 17.9 us (level)
  Pallas kernels: 4.49 us -> 4.69 us
  waiting for transfers between devices: 1.61 us -> 1.41 us
  transfers between devices with their start and end apart: 9 -> 9, of which waited for: 3 -> 3; matrix products, arithmetic and copies ran while one was open for 0% -> 0% of each run, Pallas kernels for 12% -> 13%
where the time goes in v6:
time: 17.9 us; the launch traced here: 17.7 us
  starting transfers between devices  11.5 us (64%)
  Pallas kernels  4.69 us (26%)
  waiting for transfers between devices  1.41 us (8%)
    ppermute x3, starting transfers between devices, swap(): return lax.ppermute(block, (axis, 'gz'), both)  6.25 us
    ppermute x3, starting transfers between devices, swap(): return lax.ppermute(block, axis, pairs)  4.05 us
    pallas_call x1, Pallas kernels, on_device(): pl.pallas_call(functools.partial(first_kernel, chunks), in_specs=[HBM] *...  1.39 us
    pallas_call x1, Pallas kernels, on_device(): pl.pallas_call(functools.partial(rhs_kernel, nx), in_specs=[VMEM] * 6, ou...  1.33 us
    ppermute x3, starting transfers between devices, swap_whole(): got = lax.ppermute(block, axis, pairing(2, False))  1.24 us
    pallas_call x1, Pallas kernels, on_device(): pl.pallas_call(functools.partial(last_kernel, stages, parts), in_specs=[V...  0.97 us
    ppermute x3, waiting for transfers between devices, swap(): return lax.ppermute(block, axis, pairs)  0.88 us
    ppermute x3, waiting for transfers between devices, swap(): return lax.ppermute(block, (axis, 'gz'), both)  0.52 us
  transfers between devices with their start and end apart: 9, of which 3 were waited for; matrix products, arithmetic and copies ran while one was open for 0% of the time, Pallas kernels for 13%

profile of v6, /device:TPU:0, one launch (start us, length us, event | category | flops | bytes accessed | tf_op | source)
XLA Modules:
  0.0 17.7 jit_solution(5852593592337555934)
XLA Ops:
  0.0 1.4 %load.1 = (f32[528,128]{1,0:T(8,128)S(1)}, f32[2,528,128]{2,1,0:T(8,128)S(1)}, f32[2312,128]{1,0:T(8,128)S(1)}, f32[1536,128]{1,0:T(8,128)S(1)}, f32[192,128]{1,...) custom-call(f32[32]{0:T(128)} %faces.1, ...), custom_call_target="tpu_custom_call" | custom-call | tf_op jit(solution)/shard_map/load/pallas_call | solution.py:447
  1.4 2.4 %collective-permute-start.3 = (f32[24,128]{1,0:T(8,128)S(1)}, f32[24,128]{1,0:T(8,128)S(1)}, u32[]{:S(2)}, u32[]{:S(2)}) collective-permute-start(f32[24,128]{1,0:T(8,128)S(1)} %get-tuple-element.26), channel_id=1, source_target_pairs={{0,3},{1,2},{2,1},{3,0},{4,7},{5,6},{6,5},{7,4},{8,11},{9,10},{10,... | collective-permute-start | bytes 36872 | tf_op jit(solution)/shard_map/ppermute | solution.py:414
  3.8 1.8 %collective-permute-start.4 = (f32[24,128]{1,0:T(8,128)S(1)}, f32[24,128]{1,0:T(8,128)S(1)}, u32[]{:S(2)}, u32[]{:S(2)}) collective-permute-start(f32[24,128]{1,0:T(8,128)S(1)} %get-tuple-element.27), channel_id=1, source_target_pairs={{2,5},{3,4},{4,3},{5,2},{6,1},{7,0},{0,7},{1,6},{10,13},{11,12},{1... | collective-permute-start | bytes 36872 | tf_op jit(solution)/shard_map/ppermute | solution.py:414
  5.6 0.0 collective-permute-start.5
  5.6 0.5 %collective-permute-start = (f32[1536,128]{1,0:T(8,128)S(1)}, f32[1536,128]{1,0:T(8,128)S(1)}, u32[]{:S(2)}, u32[]{:S(2)}) collective-permute-start(f32[1536,128]{1,0:T(8,128)S(1)} %get-tuple-element.21.flux_z), channel_id=1, source_target_pairs={{0,1},{1,0},{2,3},{3,2},{4,5},{5,4},{6,7},{7,6},{8,9},{9,8},{10,11... | collective-permute-start | bytes 2359304 | tf_op jit(solution)/shard_map/ppermute | solution.py:428
  6.1 0.1 pack.2
  6.2 1.5 %collective-permute-start.1 = (f32[9,32,128]{2,1,0:T(8,128)S(1)}, f32[9,32,128]{2,1,0:T(8,128)S(1)}, u32[]{:S(2)}, u32[]{:S(2)}) collective-permute-start(f32[9,32,128]{2,1,0:T(8,128)S(1)} %pack.2), channel_id=1, source_target_pairs={{2,4},{4,2},{6,0},{0,6},{3,5},{5,3},{7,1},{1,7},{10,12},{12,10},{1... | collective-permute-start | bytes 442376 | tf_op jit(solution)/shard_map/ppermute | solution.py:412
  7.7 0.0 collective-permute-done.5.sums
  7.7 0.2 inner.1
  7.9 0.0 collective-permute-done.3.small_a
  7.9 0.0 collective-permute-done.4.small_b
  7.9 1.6 %collective-permute-start.6 = (f32[13,8,128]{2,1,0:T(8,128)S(1)}, f32[13,8,128]{2,1,0:T(8,128)S(1)}, u32[]{:S(2)}, u32[]{:S(2)}) collective-permute-start(f32[13,8,128]{2,1,0:T(8,128)S(1)} %interface.1.refs_0_), channel_id=1, source_target_pairs={{0,8},{8,0},{16,24},{24,16},{1,9},{9,1},{17,25},{25,17},{2,10},{10... | collective-permute-start | bytes 159752 | tf_op jit(solution)/shard_map/ppermute | solution.py:412
  9.6 0.1 pack.3
  9.7 0.9 %collective-permute-start.2 = (f32[9,32,128]{2,1,0:T(8,128)S(1)}, f32[9,32,128]{2,1,0:T(8,128)S(1)}, u32[]{:S(2)}, u32[]{:S(2)}) collective-permute-start(f32[9,32,128]{2,1,0:T(8,128)S(1)} %pack.3), channel_id=1, source_target_pairs={{0,2},{2,0},{4,6},{6,4},{1,3},{3,1},{5,7},{7,5},{8,10},{10,8},{12,... | collective-permute-start | bytes 442376 | tf_op jit(solution)/shard_map/ppermute | solution.py:412
  10.6 0.0 collective-permute-done.flux_z_low.flux_z_high
  10.6 1.3 %rhs.1.rhs_in.refs_2_ = f32[3,528,128]{2,1,0:T(8,128)S(1)} custom-call(f32[528,128]{1,0:T(8,128)S(1)} %get-tuple-element.18.density.rho_v, f32[2,528,128]{2,1,0:T(8,128)S(1)} %get-tuple-element.19.momentum.mom_v, f32[2312,128]{1,0:T(8,128)S(1)} %get-tuple-element.20.flux_y, f32[1536,128]{1,0:T(8,128)S(1)} %get-tuple-element.21.flux_z, ...), custom_call_target="tpu_custom_call" | custom-call | flops 3932160 | bytes 3932160 | tf_op jit(solution)/shard_map/rhs/pallas_call | solution.py:482
  11.9 0.5 %collective-permute-done.6.refs_1_ = f32[13,8,128]{2,1,0:T(8,128)S(1)} collective-permute-done((f32[13,8,128]{2,1,0:T(8,128)S(1)}, f32[13,8,128]{2,1,0:T(8,128)S(1)}, u32[]{:S(2)}, u32[]{:S(2)}) %collective-permute-start.6) | collective-permute-done | bytes 53280 | tf_op jit(solution)/shard_map/ppermute | solution.py:412
  12.4 2.0 %collective-permute-start.7 = (f32[7,8,128]{2,1,0:T(8,128)S(1)}, f32[7,8,128]{2,1,0:T(8,128)S(1)}, u32[]{:S(2)}, u32[]{:S(2)}) collective-permute-start(f32[7,8,128]{2,1,0:T(8,128)S(1)} %get-tuple-element.29), channel_id=1, source_target_pairs={{0,17},{1,16},{8,25},{9,24},{16,1},{17,0},{24,9},{25,8},{2,19},{3,... | collective-permute-start | bytes 86024 | tf_op jit(solution)/shard_map/ppermute | solution.py:414
  14.5 0.7 %collective-permute-start.8 = (f32[20,8,128]{2,1,0:T(8,128)S(1)}, f32[20,8,128]{2,1,0:T(8,128)S(1)}, u32[]{:S(2)}, u32[]{:S(2)}) collective-permute-start(f32[20,8,128]{2,1,0:T(8,128)S(1)} %get-tuple-element.30), channel_id=1, source_target_pairs={{0,1},{1,0},{2,3},{3,2},{4,5},{5,4},{6,7},{7,6},{8,9},{9,8},{10,11... | collective-permute-start | bytes 245768 | tf_op jit(solution)/shard_map/ppermute | solution.py:428
  15.2 0.0 collective-permute-done.1.edge_b
  15.2 0.2 %edge.1.rhs_in = f32[3,528,128]{2,1,0:T(8,128)S(1)} custom-call(f32[3,528,128]{2,1,0:T(8,128)S(1)} %rhs.1.rhs_in.refs_2_, f32[9,32,128]{2,1,0:T(8,128)S(1)} %collective-permute-done.1.edge_b), custom_call_target="tpu_custom_call", output_to_operand_aliasing={{}: (0, {})} | custom-call | flops 1310720000 | bytes 1310720000 | tf_op jit(solution)/shard_map/edge/pallas_call | solution.py:530
  15.4 0.4 %collective-permute-done.2.edge_a = f32[9,32,128]{2,1,0:T(8,128)S(1)} collective-permute-done((f32[9,32,128]{2,1,0:T(8,128)S(1)}, f32[9,32,128]{2,1,0:T(8,128)S(1)}, u32[]{:S(2)}, u32[]{:S(2)}) %collective-permute-start.2) | collective-permute-done | bytes 147488 | tf_op jit(solution)/shard_map/ppermute | solution.py:412
  15.8 0.4 %sums.1 = (f32[3,528,128]{2,1,0:T(8,128)S(1)}, f32[3,32,2,8,128]{4,3,2,1,0:T(8,128)S(1)}, f32[3,32,2,8,128]{4,3,2,1,0:T(8,128)S(1)}) custom-call(f32[3,528,128]{2,1,0:T(8,128)S(1)} %edge.1.rhs_in, f32[9,32,128]{2,1,0:T(8,128)S(1)} %collective-permute-done.2.edge_a, f32[64,8,128]{2,1,0:T(8,128)S(1)} %get-tuple-element.22.coefs), custom_call_target="tpu_custom_call", output_to_operand_aliasing={{0}: (0, {})} | custom-call | flops 13107200 | bytes 13107200 | tf_op jit(solution)/shard_map/sums/pallas_call | solution.py:540
  16.2 0.5 %collective-permute-done.7.other = f32[7,8,128]{2,1,0:T(8,128)S(1)} collective-permute-done((f32[7,8,128]{2,1,0:T(8,128)S(1)}, f32[7,8,128]{2,1,0:T(8,128)S(1)}, u32[]{:S(2)}, u32[]{:S(2)}) %collective-permute-start.7) | collective-permute-done | bytes 28704 | tf_op jit(solution)/shard_map/ppermute | solution.py:414
  16.7 0.0 collective-permute-done.8.own
  16.7 1.0 %solve.1 = f32[3,32,2,8,128]{4,3,2,1,0:T(8,128)} custom-call(f32[3,32,2,8,128]{4,3,2,1,0:T(8,128)S(1)} %get-tuple-element.23.ahead, f32[3,32,2,8,128]{4,3,2,1,0:T(8,128)S(1)} %get-tuple-element.24.behind, f32[64,8,128]{2,1,0:T(8,128)S(1)} %get-tuple-element.22.coefs, f32[8,128]{1,0:T(8,128)S(1)} %get-tuple-element.25.scalars, ...), custom_call_target="tpu_custom_call" | custom-call | tf_op jit(solution)/shard_map/solve/pallas_call | solution.py:550
  (2 shorter events, 0.1 us)
Async XLA Ops:
  1.4 6.5 %collective-permute-start.3 = (f32[24,128]{1,0:T(8,128)S(1)}, f32[24,128]{1,0:T(8,128)S(1)}, u32[]{:S(2)}, u32[]{:S(2)}) collective-permute-start(f32[24,128]{1,0:T(8,128)S(1)} %get-tuple-element.26), channel_id=1, source_target_pairs={{0,3},{1,2},{2,1},{3,0},{4,7},{5,6},{6,5},{7,4},{8,11},{9,10},{10,... | collective-permute-start | bytes 36872 | tf_op jit(solution)/shard_map/ppermute | solution.py:414
  3.8 4.0 %collective-permute-start.4 = (f32[24,128]{1,0:T(8,128)S(1)}, f32[24,128]{1,0:T(8,128)S(1)}, u32[]{:S(2)}, u32[]{:S(2)}) collective-permute-start(f32[24,128]{1,0:T(8,128)S(1)} %get-tuple-element.27), channel_id=1, source_target_pairs={{2,5},{3,4},{4,3},{5,2},{6,1},{7,0},{0,7},{1,6},{10,13},{11,12},{1... | collective-permute-start | bytes 36872 | tf_op jit(solution)/shard_map/ppermute | solution.py:414
  5.6 2.1 %collective-permute-start.5 = (f32[192,128]{1,0:T(8,128)S(1)}, f32[192,128]{1,0:T(8,128)S(1)}, u32[]{:S(2)}, u32[]{:S(2)}) collective-permute-start(f32[192,128]{1,0:T(8,128)S(1)} %get-tuple-element.28.sums_low.sums_high), channel_id=1, source_target_pairs={{0,1},{1,0},{2,3},{3,2},{4,5},{5,4},{6,7},{7,6},{8,9},{9,8},{10,11... | collective-permute-start | bytes 294920 | tf_op jit(solution)/shard_map/ppermute | solution.py:428
  5.6 4.9 %collective-permute-start = (f32[1536,128]{1,0:T(8,128)S(1)}, f32[1536,128]{1,0:T(8,128)S(1)}, u32[]{:S(2)}, u32[]{:S(2)}) collective-permute-start(f32[1536,128]{1,0:T(8,128)S(1)} %get-tuple-element.21.flux_z), channel_id=1, source_target_pairs={{0,1},{1,0},{2,3},{3,2},{4,5},{5,4},{6,7},{7,6},{8,9},{9,8},{10,11... | collective-permute-start | bytes 2359304 | tf_op jit(solution)/shard_map/ppermute | solution.py:428
  6.2 9.0 %collective-permute-start.1 = (f32[9,32,128]{2,1,0:T(8,128)S(1)}, f32[9,32,128]{2,1,0:T(8,128)S(1)}, u32[]{:S(2)}, u32[]{:S(2)}) collective-permute-start(f32[9,32,128]{2,1,0:T(8,128)S(1)} %pack.2), channel_id=1, source_target_pairs={{2,4},{4,2},{6,0},{0,6},{3,5},{5,3},{7,1},{1,7},{10,12},{12,10},{1... | collective-permute-start | bytes 442376 | tf_op jit(solution)/shard_map/ppermute | solution.py:412
  7.9 4.4 %collective-permute-start.6 = (f32[13,8,128]{2,1,0:T(8,128)S(1)}, f32[13,8,128]{2,1,0:T(8,128)S(1)}, u32[]{:S(2)}, u32[]{:S(2)}) collective-permute-start(f32[13,8,128]{2,1,0:T(8,128)S(1)} %interface.1.refs_0_), channel_id=1, source_target_pairs={{0,8},{8,0},{16,24},{24,16},{1,9},{9,1},{17,25},{25,17},{2,10},{10... | collective-permute-start | bytes 159752 | tf_op jit(solution)/shard_map/ppermute | solution.py:412
  9.7 6.2 %collective-permute-start.2 = (f32[9,32,128]{2,1,0:T(8,128)S(1)}, f32[9,32,128]{2,1,0:T(8,128)S(1)}, u32[]{:S(2)}, u32[]{:S(2)}) collective-permute-start(f32[9,32,128]{2,1,0:T(8,128)S(1)} %pack.3), channel_id=1, source_target_pairs={{0,2},{2,0},{4,6},{6,4},{1,3},{3,1},{5,7},{7,5},{8,10},{10,8},{12,... | collective-permute-start | bytes 442376 | tf_op jit(solution)/shard_map/ppermute | solution.py:412
  12.4 4.3 %collective-permute-start.7 = (f32[7,8,128]{2,1,0:T(8,128)S(1)}, f32[7,8,128]{2,1,0:T(8,128)S(1)}, u32[]{:S(2)}, u32[]{:S(2)}) collective-permute-start(f32[7,8,128]{2,1,0:T(8,128)S(1)} %get-tuple-element.29), channel_id=1, source_target_pairs={{0,17},{1,16},{8,25},{9,24},{16,1},{17,0},{24,9},{25,8},{2,19},{3,... | collective-permute-start | bytes 86024 | tf_op jit(solution)/shard_map/ppermute | solution.py:414
  14.5 2.3 %collective-permute-start.8 = (f32[20,8,128]{2,1,0:T(8,128)S(1)}, f32[20,8,128]{2,1,0:T(8,128)S(1)}, u32[]{:S(2)}, u32[]{:S(2)}) collective-permute-start(f32[20,8,128]{2,1,0:T(8,128)S(1)} %get-tuple-element.30), channel_id=1, source_target_pairs={{0,1},{1,0},{2,3},{3,2},{4,5},{5,4},{6,7},{7,6},{8,9},{9,8},{10,11... | collective-permute-start | bytes 245768 | tf_op jit(solution)/shard_map/ppermute | solution.py:428

commit v7 on v6

--- a/solution.py
+++ b/solution.py
@@ -10,7 +10,7 @@
 time_step = 0.2
 scale = time_step / 60.0
 ROWS = 8
-RHS_COST, SUMS_COST, JOIN_COST, EDGE_COST, FACE_COST, PACK_COST, HALO_COST = 60, 200, 20, 20000, 200000, 20000, 20
+RHS_COST, SUMS_COST, JOIN_COST, EDGE_COST, FACE_COST, PACK_COST, HALO_COST = 60, 200, 20, 20000, 200000, 200000, 20
 F32 = jnp.float32
 VMEM = pl.BlockSpec(memory_space=pltpu.VMEM)
 ANY = pl.BlockSpec(memory_space=pl.ANY)
@@ -266,15 +266,43 @@
         ref[3 * f + 2] = n1
 
 
+def z_slots(nz, tile):
+    per = nz // 6
+    return tile // per, 6 * (tile % per) + 3
+
+
+def packed_rows(nz, tiles):
+    return (z_slots(nz, tiles - 1)[0] + 1) * ROWS
+
+
+def pack_z(sums, flux_z, message):
+    nz = sums.shape[1]
+    first = sums.shape[0]
+    message[:first] = sums[...]
+    lane = lax.broadcasted_iota(jnp.int32, (ROWS, nz), 1)
+    packed = {}
+    for tile in range(flux_z.shape[0] // ROWS):
+        group, shift = z_slots(nz, tile)
+        moved = pltpu.roll(flux_z[tile * ROWS : (tile + 1) * ROWS], shift, 1)
+        packed[group] = jnp.where(lane < shift - 3, packed[group], moved) if group in packed else moved
+    for group, value in packed.items():
+        message[first + group * ROWS : first + (group + 1) * ROWS] = value
+
+
+def unpack_z(message, first, tile):
+    nz = message.shape[1]
+    group, shift = z_slots(nz, tile)
+    return pltpu.roll(message[first + group * ROWS : first + (group + 1) * ROWS], nz - shift, 1)
+
+
 def halos_y(is_odd, from_a, from_b):
     low = jnp.where(is_odd, from_a, from_b)
     high = jnp.where(is_odd, from_b, from_a)
     return low, high
 
 
-def inner_kernel(sums, sums_low, sums_high, inner, pad):
+def inner_kernel(ny, sums, sums_low, sums_high, inner, pad):
     nz = sums.shape[1]
-    ny = sums.shape[0] // 12
     pad[0:ROWS] = jnp.zeros((ROWS, nz), F32)
     pad[ROWS + ny : 2 * ROWS + ny] = jnp.zeros((ROWS, nz), F32)
     for side in range(2):
@@ -334,16 +362,23 @@
         store_forms(own, forms, tiles)
 
 
-def rhs_kernel(nx, density, momentum, flux_y, flux_z, flux_z_low, flux_z_high, rhs):
+def rhs_kernel(nx, density, momentum, flux_y, flux_z, *refs):
     ny = density.shape[0] // (nx + 1)
     pitch = ny + ROWS
+    if len(refs) == 3:
+        message, rhs, unpacked = refs
+        for tile in range(unpacked.shape[0] // ROWS):
+            unpacked[tile * ROWS : (tile + 1) * ROWS] = unpack_z(message, 12 * ny, tile)
+        flux_z_low = flux_z_high = unpacked
+    else:
+        flux_z_low, flux_z_high, rhs, _ = refs
     for f in range(3):
         for x in range(nx):
             at = (f * nx + x) * pitch + ROWS
             dy = sixth(lambda s: flux_y[at + s : at + s + ny])
-            cells = slice(x * ny, (x + 1) * ny)
             lines = slice((f * nx + x) * ny, (f * nx + x + 1) * ny)
             dz = sixth_z(*[r[lines] for r in (flux_z, flux_z_low, flux_z_high)])
+            cells = slice(x * ny, (x + 1) * ny)
             state = density[cells] if f == 0 else momentum[f - 1, cells]
             rhs[f, cells] = state - scale * (dy + dz)
 
@@ -464,6 +499,9 @@
         name="load",
     )(*inputs)
     got_a, got_b = swap_edges(small_a, small_b, crossed)
+    packed = crossed and nz % 128 == 0
+    z_rows = 12 * ny + packed_rows(nz, 3 * cells // ROWS)
+
     edge_a, edge_b = [
         pl.pallas_call(
             functools.partial(pack_kernel, nx, second),
@@ -476,21 +514,36 @@
         )(density, momentum)
         for second in (False, True)
     ]
+    if packed:
+        z_message = pl.pallas_call(
+            pack_z,
+            in_specs=[VMEM] * 2,
+            out_specs=VMEM,
+            out_shape=vec(z_rows),
+            compiler_params=params(),
+            cost_estimate=cost(RHS_COST),
+            name="pack_z",
+        )(sums, flux_z)
+        z_low, z_high = swap_whole(z_message, "gz")
+        handled = (z_low, sums, sums)
+        beyond = (z_low,)
+    else:
+        sums_low, sums_high = swap_whole(sums, "gz")
+        beyond = swap_whole(flux_z, "gz")
+        handled = (sums_low, sums, sums) if crossed else (sums, sums_low, sums_high)
     far_a, far_b = swap_edges(edge_a, edge_b)
-    sums_low, sums_high = swap_whole(sums, "gz")
-    z_low, z_high = swap_whole(flux_z, "gz")
     rhs = pl.pallas_call(
         functools.partial(rhs_kernel, nx),
-        in_specs=[VMEM] * 6,
+        in_specs=[VMEM] * (4 + len(beyond)),
         out_specs=VMEM,
         out_shape=vec(3, cells + ny),
+        scratch_shapes=[pltpu.VMEM((3 * cells, nz), F32)],
         compiler_params=params(),
         cost_estimate=cost(RHS_COST),
         name="rhs",
-    )(density, momentum, flux_y, flux_z, z_low, z_high)
-    handled = (sums_low, sums, sums) if crossed else (sums, sums_low, sums_high)
+    )(density, momentum, flux_y, flux_z, *beyond)
     inner = pl.pallas_call(
-        inner_kernel,
+        functools.partial(inner_kernel, ny),
         in_specs=[VMEM] * 3,
         out_specs=VMEM,
         out_shape=vec(6 * ny),

time: 17.9 us -> 17.9 us (level)
  Pallas kernels: 4.69 us -> 5.18 us
  waiting for transfers between devices: 1.41 us -> 1.08 us
    pallas_call x2 -> x3, Pallas kernels: 1.49 us -> 1.96 us  [the longest x1 1.54 us: on_device(): pl.pallas_call(functools.partial(rhs_kernel, nx), in_specs=[VMEM] * (4 +...]
    ppermute x3 -> x2, starting transfers between devices: 1.24 us -> 0.77 us  [swap_whole(): got = lax.ppermute(block, axis, pairing(2, False))]
    ppermute x3, waiting for transfers between devices: 0.88 us -> 0.46 us  [swap(): return lax.ppermute(block, axis, pairs)]
    ppermute x3, starting transfers between devices: 4.05 us -> 4.33 us  [swap(): return lax.ppermute(block, axis, pairs)]
  transfers between devices with their start and end apart: 9 -> 8, of which waited for: 3 -> 3; matrix products, arithmetic and copies ran while one was open for 0% -> 0% of each run, Pallas kernels for 13% -> 16%
where the time goes in v7:
time: 17.9 us; the launch traced here: 17.7 us
  starting transfers between devices  11.4 us (64%)
  Pallas kernels  5.18 us (29%)
  waiting for transfers between devices  1.08 us (6%)
    ppermute x3, starting transfers between devices, swap(): return lax.ppermute(block, (axis, 'gz'), both)  6.29 us
    ppermute x3, starting transfers between devices, swap(): return lax.ppermute(block, axis, pairs)  4.33 us
    pallas_call x1, Pallas kernels, on_device(): pl.pallas_call(functools.partial(rhs_kernel, nx), in_specs=[VMEM] * (4 +...  1.54 us
    pallas_call x1, Pallas kernels, on_device(): pl.pallas_call(functools.partial(first_kernel, chunks), in_specs=[HBM] *...  1.39 us
    pallas_call x1, Pallas kernels, on_device(): pl.pallas_call(functools.partial(last_kernel, stages, parts), in_specs=[V...  0.97 us
    ppermute x2, starting transfers between devices, swap_whole(): got = lax.ppermute(block, axis, pairing(2, False))  0.77 us
    ppermute x3, waiting for transfers between devices, swap(): return lax.ppermute(block, (axis, 'gz'), both)  0.61 us
    ppermute x3, waiting for transfers between devices, swap(): return lax.ppermute(block, axis, pairs)  0.46 us
  transfers between devices with their start and end apart: 8, of which 3 were waited for; matrix products, arithmetic and copies ran while one was open for 0% of the time, Pallas kernels for 16%

profile of v7, /device:TPU:0, one launch (start us, length us, event | category | flops | bytes accessed | tf_op | source)
XLA Modules:
  0.0 17.7 jit_solution(10085820041588334300)
XLA Ops:
  0.0 1.4 %load.1 = (f32[528,128]{1,0:T(8,128)S(1)}, f32[2,528,128]{2,1,0:T(8,128)S(1)}, f32[2312,128]{1,0:T(8,128)S(1)}, f32[1536,128]{1,0:T(8,128)S(1)}, f32[192,128]{1,...) custom-call(f32[32]{0:T(128)} %faces.1, ...), custom_call_target="tpu_custom_call" | custom-call | tf_op jit(solution)/shard_map/load/pallas_call | solution.py:482
  1.4 2.4 %collective-permute-start.3 = (f32[24,128]{1,0:T(8,128)S(1)}, f32[24,128]{1,0:T(8,128)S(1)}, u32[]{:S(2)}, u32[]{:S(2)}) collective-permute-start(f32[24,128]{1,0:T(8,128)S(1)} %get-tuple-element.27), channel_id=1, source_target_pairs={{0,3},{1,2},{2,1},{3,0},{4,7},{5,6},{6,5},{7,4},{8,11},{9,10},{10,... | collective-permute-start | bytes 36872 | tf_op jit(solution)/shard_map/ppermute | solution.py:449
  3.8 1.8 %collective-permute-start.4 = (f32[24,128]{1,0:T(8,128)S(1)}, f32[24,128]{1,0:T(8,128)S(1)}, u32[]{:S(2)}, u32[]{:S(2)}) collective-permute-start(f32[24,128]{1,0:T(8,128)S(1)} %get-tuple-element.28), channel_id=1, source_target_pairs={{2,5},{3,4},{4,3},{5,2},{6,1},{7,0},{0,7},{1,6},{10,13},{11,12},{1... | collective-permute-start | bytes 36872 | tf_op jit(solution)/shard_map/ppermute | solution.py:449
  5.6 0.3 %pack_z.1 = f32[272,128]{1,0:T(8,128)S(1)} custom-call(f32[192,128]{1,0:T(8,128)S(1)} %get-tuple-element.22.sums.sums_low.sums_high, f32[1536,128]{1,0:T(8,128)S(1)} %get-tuple-element.21.flux_z), custom_call_target="tpu_custom_call" | custom-call | flops 3932160 | bytes 3932160 | tf_op jit(solution)/shard_map/pack_z/pallas_call | solution.py:518
  5.9 0.1 collective-permute-start
  6.0 0.1 pack.2
  6.1 1.5 %collective-permute-start.1 = (f32[9,32,128]{2,1,0:T(8,128)S(1)}, f32[9,32,128]{2,1,0:T(8,128)S(1)}, u32[]{:S(2)}, u32[]{:S(2)}) collective-permute-start(f32[9,32,128]{2,1,0:T(8,128)S(1)} %pack.2), channel_id=1, source_target_pairs={{2,4},{4,2},{6,0},{0,6},{3,5},{5,3},{7,1},{1,7},{10,12},{12,10},{1... | collective-permute-start | bytes 442376 | tf_op jit(solution)/shard_map/ppermute | solution.py:447
  7.6 0.0 collective-permute-done.refs_0_.sums
  7.6 0.2 inner.1
  7.7 0.0 collective-permute-done.3.small_a
  7.7 0.1 collective-permute-done.4.small_b
  7.9 1.6 %collective-permute-start.5 = (f32[13,8,128]{2,1,0:T(8,128)S(1)}, f32[13,8,128]{2,1,0:T(8,128)S(1)}, u32[]{:S(2)}, u32[]{:S(2)}) collective-permute-start(f32[13,8,128]{2,1,0:T(8,128)S(1)} %interface.1.refs_0_), channel_id=1, source_target_pairs={{0,8},{8,0},{16,24},{24,16},{1,9},{9,1},{17,25},{25,17},{2,10},{10... | collective-permute-start | bytes 159752 | tf_op jit(solution)/shard_map/ppermute | solution.py:447
  9.5 0.1 pack.3
  9.6 1.2 %collective-permute-start.2 = (f32[9,32,128]{2,1,0:T(8,128)S(1)}, f32[9,32,128]{2,1,0:T(8,128)S(1)}, u32[]{:S(2)}, u32[]{:S(2)}) collective-permute-start(f32[9,32,128]{2,1,0:T(8,128)S(1)} %pack.3), channel_id=1, source_target_pairs={{0,2},{2,0},{4,6},{6,4},{1,3},{3,1},{5,7},{7,5},{8,10},{10,8},{12,... | collective-permute-start | bytes 442376 | tf_op jit(solution)/shard_map/ppermute | solution.py:447
  10.8 1.5 %rhs.1.rhs_in.refs_2_ = f32[3,528,128]{2,1,0:T(8,128)S(1)} custom-call(f32[528,128]{1,0:T(8,128)S(1)} %get-tuple-element.18.density.rho_v, f32[2,528,128]{2,1,0:T(8,128)S(1)} %get-tuple-element.19.momentum.mom_v, f32[2312,128]{1,0:T(8,128)S(1)} %get-tuple-element.20.flux_y, f32[1536,128]{1,0:T(8,128)S(1)} %get-tuple-element.21.flux_z, ...), custom_call_target="tpu_custom_call" | custom-call | flops 3932160 | bytes 3932160 | tf_op jit(solution)/shard_map/rhs/pallas_call | solution.py:535
  12.4 0.0 collective-permute-done.5.refs_1_
  12.4 2.1 %collective-permute-start.6 = (f32[7,8,128]{2,1,0:T(8,128)S(1)}, f32[7,8,128]{2,1,0:T(8,128)S(1)}, u32[]{:S(2)}, u32[]{:S(2)}) collective-permute-start(f32[7,8,128]{2,1,0:T(8,128)S(1)} %get-tuple-element.29), channel_id=1, source_target_pairs={{0,17},{1,16},{8,25},{9,24},{16,1},{17,0},{24,9},{25,8},{2,19},{3,... | collective-permute-start | bytes 86024 | tf_op jit(solution)/shard_map/ppermute | solution.py:449
  14.5 0.7 %collective-permute-start.7 = (f32[20,8,128]{2,1,0:T(8,128)S(1)}, f32[20,8,128]{2,1,0:T(8,128)S(1)}, u32[]{:S(2)}, u32[]{:S(2)}) collective-permute-start(f32[20,8,128]{2,1,0:T(8,128)S(1)} %get-tuple-element.30), channel_id=1, source_target_pairs={{0,1},{1,0},{2,3},{3,2},{4,5},{5,4},{6,7},{7,6},{8,9},{9,8},{10,11... | collective-permute-start | bytes 245768 | tf_op jit(solution)/shard_map/ppermute | solution.py:463
  15.2 0.0 collective-permute-done.1.edge_b
  15.2 0.2 %edge.1.rhs_in = f32[3,528,128]{2,1,0:T(8,128)S(1)} custom-call(f32[3,528,128]{2,1,0:T(8,128)S(1)} %rhs.1.rhs_in.refs_2_, f32[9,32,128]{2,1,0:T(8,128)S(1)} %collective-permute-done.1.edge_b), custom_call_target="tpu_custom_call", output_to_operand_aliasing={{}: (0, {})} | custom-call | flops 1310720000 | bytes 1310720000 | tf_op jit(solution)/shard_map/edge/pallas_call | solution.py:583
  15.4 0.4 %collective-permute-done.2.edge_a = f32[9,32,128]{2,1,0:T(8,128)S(1)} collective-permute-done((f32[9,32,128]{2,1,0:T(8,128)S(1)}, f32[9,32,128]{2,1,0:T(8,128)S(1)}, u32[]{:S(2)}, u32[]{:S(2)}) %collective-permute-start.2) | collective-permute-done | bytes 147488 | tf_op jit(solution)/shard_map/ppermute | solution.py:447
  15.9 0.4 %sums.1 = (f32[3,528,128]{2,1,0:T(8,128)S(1)}, f32[3,32,2,8,128]{4,3,2,1,0:T(8,128)S(1)}, f32[3,32,2,8,128]{4,3,2,1,0:T(8,128)S(1)}) custom-call(f32[3,528,128]{2,1,0:T(8,128)S(1)} %edge.1.rhs_in, f32[9,32,128]{2,1,0:T(8,128)S(1)} %collective-permute-done.2.edge_a, f32[64,8,128]{2,1,0:T(8,128)S(1)} %get-tuple-element.23.coefs), custom_call_target="tpu_custom_call", output_to_operand_aliasing={{0}: (0, {})} | custom-call | flops 13107200 | bytes 13107200 | tf_op jit(solution)/shard_map/sums/pallas_call | solution.py:593
  16.3 0.5 %collective-permute-done.6.other = f32[7,8,128]{2,1,0:T(8,128)S(1)} collective-permute-done((f32[7,8,128]{2,1,0:T(8,128)S(1)}, f32[7,8,128]{2,1,0:T(8,128)S(1)}, u32[]{:S(2)}, u32[]{:S(2)}) %collective-permute-start.6) | collective-permute-done | bytes 28704 | tf_op jit(solution)/shard_map/ppermute | solution.py:449
  16.7 0.0 collective-permute-done.7.own
  16.7 1.0 %solve.1 = f32[3,32,2,8,128]{4,3,2,1,0:T(8,128)} custom-call(f32[3,32,2,8,128]{4,3,2,1,0:T(8,128)S(1)} %get-tuple-element.24.ahead, f32[3,32,2,8,128]{4,3,2,1,0:T(8,128)S(1)} %get-tuple-element.25.behind, f32[64,8,128]{2,1,0:T(8,128)S(1)} %get-tuple-element.23.coefs, f32[8,128]{1,0:T(8,128)S(1)} %get-tuple-element.26.scalars, ...), custom_call_target="tpu_custom_call" | custom-call | tf_op jit(solution)/shard_map/solve/pallas_call | solution.py:603
  (2 shorter events, 0.1 us)
Async XLA Ops:
  1.4 6.3 %collective-permute-start.3 = (f32[24,128]{1,0:T(8,128)S(1)}, f32[24,128]{1,0:T(8,128)S(1)}, u32[]{:S(2)}, u32[]{:S(2)}) collective-permute-start(f32[24,128]{1,0:T(8,128)S(1)} %get-tuple-element.27), channel_id=1, source_target_pairs={{0,3},{1,2},{2,1},{3,0},{4,7},{5,6},{6,5},{7,4},{8,11},{9,10},{10,... | collective-permute-start | bytes 36872 | tf_op jit(solution)/shard_map/ppermute | solution.py:449
  3.8 4.0 %collective-permute-start.4 = (f32[24,128]{1,0:T(8,128)S(1)}, f32[24,128]{1,0:T(8,128)S(1)}, u32[]{:S(2)}, u32[]{:S(2)}) collective-permute-start(f32[24,128]{1,0:T(8,128)S(1)} %get-tuple-element.28), channel_id=1, source_target_pairs={{2,5},{3,4},{4,3},{5,2},{6,1},{7,0},{0,7},{1,6},{10,13},{11,12},{1... | collective-permute-start | bytes 36872 | tf_op jit(solution)/shard_map/ppermute | solution.py:449
  5.9 1.7 %collective-permute-start = (f32[272,128]{1,0:T(8,128)S(1)}, f32[272,128]{1,0:T(8,128)S(1)}, u32[]{:S(2)}, u32[]{:S(2)}) collective-permute-start(f32[272,128]{1,0:T(8,128)S(1)} %pack_z.1), channel_id=1, source_target_pairs={{0,1},{1,0},{2,3},{3,2},{4,5},{5,4},{6,7},{7,6},{8,9},{9,8},{10,11... | collective-permute-start | bytes 417800 | tf_op jit(solution)/shard_map/ppermute | solution.py:463
  6.1 9.1 %collective-permute-start.1 = (f32[9,32,128]{2,1,0:T(8,128)S(1)}, f32[9,32,128]{2,1,0:T(8,128)S(1)}, u32[]{:S(2)}, u32[]{:S(2)}) collective-permute-start(f32[9,32,128]{2,1,0:T(8,128)S(1)} %pack.2), channel_id=1, source_target_pairs={{2,4},{4,2},{6,0},{0,6},{3,5},{5,3},{7,1},{1,7},{10,12},{12,10},{1... | collective-permute-start | bytes 442376 | tf_op jit(solution)/shard_map/ppermute | solution.py:447
  7.9 4.5 %collective-permute-start.5 = (f32[13,8,128]{2,1,0:T(8,128)S(1)}, f32[13,8,128]{2,1,0:T(8,128)S(1)}, u32[]{:S(2)}, u32[]{:S(2)}) collective-permute-start(f32[13,8,128]{2,1,0:T(8,128)S(1)} %interface.1.refs_0_), channel_id=1, source_target_pairs={{0,8},{8,0},{16,24},{24,16},{1,9},{9,1},{17,25},{25,17},{2,10},{10... | collective-permute-start | bytes 159752 | tf_op jit(solution)/shard_map/ppermute | solution.py:447
  9.6 6.2 %collective-permute-start.2 = (f32[9,32,128]{2,1,0:T(8,128)S(1)}, f32[9,32,128]{2,1,0:T(8,128)S(1)}, u32[]{:S(2)}, u32[]{:S(2)}) collective-permute-start(f32[9,32,128]{2,1,0:T(8,128)S(1)} %pack.3), channel_id=1, source_target_pairs={{0,2},{2,0},{4,6},{6,4},{1,3},{3,1},{5,7},{7,5},{8,10},{10,8},{12,... | collective-permute-start | bytes 442376 | tf_op jit(solution)/shard_map/ppermute | solution.py:447
  12.4 4.3 %collective-permute-start.6 = (f32[7,8,128]{2,1,0:T(8,128)S(1)}, f32[7,8,128]{2,1,0:T(8,128)S(1)}, u32[]{:S(2)}, u32[]{:S(2)}) collective-permute-start(f32[7,8,128]{2,1,0:T(8,128)S(1)} %get-tuple-element.29), channel_id=1, source_target_pairs={{0,17},{1,16},{8,25},{9,24},{16,1},{17,0},{24,9},{25,8},{2,19},{3,... | collective-permute-start | bytes 86024 | tf_op jit(solution)/shard_map/ppermute | solution.py:449
  14.5 2.3 %collective-permute-start.7 = (f32[20,8,128]{2,1,0:T(8,128)S(1)}, f32[20,8,128]{2,1,0:T(8,128)S(1)}, u32[]{:S(2)}, u32[]{:S(2)}) collective-permute-start(f32[20,8,128]{2,1,0:T(8,128)S(1)} %get-tuple-element.30), channel_id=1, source_target_pairs={{0,1},{1,0},{2,3},{3,2},{4,5},{5,4},{6,7},{7,6},{8,9},{9,8},{10,11... | collective-permute-start | bytes 245768 | tf_op jit(solution)/shard_map/ppermute | solution.py:463
